TPU v7x, 32 devices: a whole 2x2x4 slice. The times are simulated.
32 devices in a mesh: groups: 2 (over x), tensor: 16 (over z, y, core).
Axes of the slice: x: 2, y: 2, z: 4, core: 2. Of those that a mesh axis runs over, the one named last changes fastest.
Arguments:
- tokens: bfloat16 [256, 8192], P(('groups', 'tensor')), parts along dimension 0, may hold values from -6 to 6
- gate_weight: bfloat16 [8192, 28672], P(None, 'tensor'), may hold values from -0.0625 to 0.0625
- up_weight: bfloat16 [8192, 28672], P(None, 'tensor'), may hold values from -0.0625 to 0.0625
- adapter_down_weight: bfloat16 [32, 8192, 64], P(('groups', 'tensor')), parts along dimension 0, may hold values from -0.0625 to 0.0625
- adapter_up_weight: bfloat16 [32, 64, 28672], P('groups', None, 'tensor'), parts along dimension 0, may hold values from -0.75 to 0.75
- request_adapter_index: int32 [256], P('groups'), parts along dimension 0, may hold values from 0 to 15, as said below
- adapter_request_lists: int32 [32, 32], P('groups'), parts along dimension 0, may hold values from 0 to 128, as said below
- placement: int32 [32], P('groups'), parts along dimension 0, may hold values from 0 to 15, each once
Outputs:
- hidden: bfloat16 [256, 28672], P('groups', 'tensor'), parts along dimension 0
There are 2 independent parts, one for each index of `groups`. A program takes and returns all parts, laid end to end along the dimension named above; an argument that names none is the same for every part. Nothing has to cross between parts.
Inputs may be any that keep to these rules, and one draw needn't show every extreme that they name: Each request r appears exactly once in adapter_request_lists, in the row request_adapter_index[r]; the other entries equal 128. `request_adapter_index`: at most 32 requests share one adapter; some adapter has exactly 32.
All inputs are finite; a program needn't handle non-finite values.
Results may differ from a plain program's by a relative error of at most 0.0041.
Values may be sent and summed in bfloat16 or wider, within the bound.
No kernel may reach another device: no remote copies, remote signals or barrier semaphores. Data moves between devices by JAX's collectives and lax.ppermute only.
A program may use at most 192 MiB of HBM per device.

v0:
```python
import jax
import jax.numpy as jnp
from jax import lax
from jax.sharding import PartitionSpec as P


def body(
    tokens,
    gate_weight,
    up_weight,
    adapter_down_weight,
    adapter_up_weight,
    request_adapter_index,
    adapter_request_lists,
    placement,
):
    request_batch = request_adapter_index.shape[0]
    adapters = placement.shape[0]
    rank_width_size = adapter_down_weight.shape[2]
    own_slot = lax.axis_index("tensor")
    owner_id = jnp.sum(jnp.where(placement == own_slot, jnp.arange(adapters, dtype=jnp.int32), 0))
    wanted = lax.dynamic_slice_in_dim(adapter_request_lists, owner_id, 1, 0)[0]
    gathered = lax.all_gather(tokens, "tensor", axis=0, tiled=True)
    picker = (wanted[:, None] == jnp.arange(request_batch, dtype=jnp.int32)[None, :]).astype(
        jnp.bfloat16
    )
    picked_rows = jnp.dot(picker, gathered, preferred_element_type=jnp.float32)
    gate_pre = jnp.dot(gathered, gate_weight, preferred_element_type=jnp.float32)
    up_pre = jnp.dot(gathered, up_weight, preferred_element_type=jnp.float32)
    low_rank_output = jnp.dot(
        picked_rows.astype(jnp.bfloat16), adapter_down_weight[0], preferred_element_type=jnp.float32
    )
    partial_value = (
        jnp.zeros((request_batch, rank_width_size), jnp.float32)
        .at[wanted]
        .add(low_rank_output, mode="drop")
    )
    mixed = lax.psum(partial_value, "tensor").astype(jnp.bfloat16)
    flat_lists = adapter_request_lists.reshape(-1)
    listed_requests = jnp.take(mixed, jnp.minimum(flat_lists, request_batch - 1), axis=0)
    listed_requests = jnp.where(
        (flat_lists < request_batch)[:, None], listed_requests, jnp.zeros_like(listed_requests)
    )
    listed_requests = listed_requests.reshape(
        adapters, adapter_request_lists.shape[1], rank_width_size
    )
    grouped_rows = jnp.einsum(
        "tdb,tbh->tdh", listed_requests, adapter_up_weight, preferred_element_type=jnp.float32
    )
    delta = (
        jnp.zeros((request_batch, adapter_up_weight.shape[2]), jnp.float32)
        .at[flat_lists]
        .add(grouped_rows.reshape(-1, adapter_up_weight.shape[2]), mode="drop")
    )
    return (jax.nn.silu(gate_pre) * (up_pre + delta)).astype(jnp.bfloat16)


def solution(mesh):
    in_specs = (
        P(("groups", "tensor"), None),
        P(None, "tensor"),
        P(None, "tensor"),
        P(("groups", "tensor"), None, None),
        P("groups", None, "tensor"),
        P("groups"),
        P("groups", None),
        P("groups"),
    )
    out_specs = P("groups", "tensor")
    return jax.shard_map(body, mesh=mesh, in_specs=in_specs, out_specs=out_specs, check_vma=False)
```

profile of v0, /device:TPU:0, one launch (start us, length us, event | category | flops | bytes accessed | tf_op | source)
XLA Modules:
  0.0 164.4 jit_solution(2291143749328220311)
XLA Ops:
  6.5 0.0 copy-start
  6.5 0.0 all-gather.2.cloned.1.call-start
  6.5 0.7 all-gather.2.cloned.1.call-update
  7.3 1.3 fusion.13
  9.9 0.8 reshape.103
  11.3 0.7 fusion.15
  12.0 0.7 fusion.14
  12.7 0.7 broadcast_compare_fusion
  13.4 40.2 %all-gather.2.cloned.1.call-done = bf16[128,8192]{1,0:T(8,128)(2,1)} async-done(((bf16[8,8192]{1,0:T(8,128)(2,1)}), bf16[128,8192]{1,0:T(8,128)(2,1)}) %all-gather.2.cloned.1.call-update) | async-done | bytes 2097168 | tf_op jit(solution)/shard_map/all_gather | solution.py:23
  53.7 0.0 copy-done
  53.7 2.4 %fusion = f32[32,64]{1,0:T(8,128)S(1)} fusion(bf16[128,8192]{1,0:T(8,128)(2,1)} %all-gather.2.cloned.1.call-done, bf16[1,8192,64]{1,2,0:T(8,128)(2,1)S(1)} %copy-done, s32[32]{0:T(128)S(1)} %fusion.15), kind=kOutput, calls=%fused_computation.4 | convolution fusion | flops 100929536 | bytes 3154048 | tf_op jit(solution)/shard_map/dot_general | solution.py:30
  56.1 0.7 scatter_custom_fusion
  56.8 59.6 %psum.7 = bf16[128,64]{1,0:T(8,128)(2,1)S(1)} all-reduce(f32[128,64]{1,0:T(8,128)S(1)} %scatter_custom_fusion), channel_id=1, replica_groups=mesh['groups'=2,'tensor'=16] {'tensor'}, use_global_device_ids=true, to_apply=%region_2.3 | all-reduce | flops 8192 | bytes 49152 | tf_op jit(solution)/shard_map/psum | solution.py:38
  116.4 1.3 gather_fusion
  117.7 0.0 copy-start.2
  117.7 4.7 %fusion.2 = f32[16,32,1792]{2,1,0:T(8,128)} fusion(bf16[16,64,1792]{2,1,0:T(8,128)(2,1)} %param.12, bf16[16,32,64]{2,1,0:T(8,128)(2,1)S(1)} %bitcast.20, pred[16,32]{1,0:T(8,128)(4,1)S(1)} %get-tuple-element.6, pred[16,32]{1,0:T(8,128)(4,1)S(1)} %get-tuple-element.5), kind=kOutput, calls=%fused_computation.7 | convolution fusion | flops 117506048 | bytes 7406592 | tf_op jit(solution)/shard_map/tdb,tbh->tdh/dot_general | solution.py:47
  122.4 0.0 copy-done.2
  122.4 11.8 %fusion.18 = f32[128,1792]{1,0:T(8,128)S(1)} fusion(bf16[128,8192]{1,0:T(8,128)(2,1)S(1)} %copy-done.2, bf16[8192,1792]{1,0:T(8,128)(2,1)} %param.10), kind=kOutput, calls=%fused_computation.32 | convolution fusion | flops 3758096384 | bytes 32374784 | tf_op jit(solution)/shard_map/dot_general | solution.py:29
  134.2 8.3 %scatter_fusion = f32[128,1792]{1,0:T(8,128)S(1)} fusion(f32[128,1792]{1,0:T(8,128)S(1)} %fusion.18, s32[512]{0:T(512)S(1)} %bitcast.21, f32[512,1792]{1,0:T(8,128)} %bitcast.19), kind=kCustom, calls=%fused_computation.2 | custom fusion | flops 917504 | bytes 11012096 | tf_op jit(solution)/shard_map/scatter-add | solution.py:53
  142.5 0.0 copy-start.1
  142.5 15.0 %multiply_convert_fusion = bf16[128,1792]{1,0:T(8,128)(2,1)} fusion(f32[128,1792]{1,0:T(8,128)S(1)} %scatter_fusion, bf16[128,8192]{1,0:T(8,128)(2,1)} %all-gather.2.cloned.1.call-done, bf16[8192,1792]{1,0:T(8,128)(2,1)} %param.9), kind=kOutput, calls=%fused_computation.6 | convolution fusion | flops 3759472640 | bytes 32833536 | tf_op jit(solution)/shard_map/dot_general | solution.py:28
  157.5 0.0 copy-done.1
  (2 shorter events, 0.0 us)
Async XLA Ops:
  6.5 47.1 %copy-start = (bf16[1,8192,64]{1,2,0:T(8,128)(2,1)S(1)}, bf16[1,8192,64]{1,2,0:T(8,128)(2,1)}, u32[]{:S(2)}) copy-start(bf16[1,8192,64]{1,2,0:T(8,128)(2,1)} %param.11) | copy-start | bytes 3145732
  6.5 47.1 %all-gather.2.cloned.1.call-start = ((), (), s32[]{:S(2)}) async-start(), calls=%async_computation | async-start | bytes 2228224 | tf_op jit(solution)/shard_map/all_gather | solution.py:23
  117.7 4.7 %copy-start.2 = (bf16[128,8192]{1,0:T(8,128)(2,1)S(1)}, bf16[128,8192]{1,0:T(8,128)(2,1)}, u32[]{:S(2)}) copy-start(bf16[128,8192]{1,0:T(8,128)(2,1)} %all-gather.2.cloned.1.call-done) | copy-start | bytes 6291460
  142.5 15.0 %copy-start.1 = (bf16[1,8192,64]{1,2,0:T(8,128)(2,1)S(1)}, bf16[1,8192,64]{1,2,0:T(8,128)(2,1)}, u32[]{:S(2)}) copy-start(bf16[1,8192,64]{1,2,0:T(8,128)(2,1)} %param.11) | copy-start | bytes 3145732
Sparse Core Ops, SparseCore 0:
  9.5 44.0 all-gather.1
where the time goes:
time: 165 us; the launch traced here: 164 us
  blocking collectives  59.6 us (36%)
  waiting for transfers between devices  41 us (25%)
  matrix products  33.9 us (21%)
  between operations  15.4 us (9%)
  other arithmetic  11.7 us (7%)
  local copies, waits for them, and re-layouts  2.82 us (2%)
    psum x1, blocking collectives, body(): mixed = lax.psum(partial_value, 'tensor').astype(jnp.bfloat16)  59.6 us
    all_gather x1, waiting for transfers between devices, body(): gathered = lax.all_gather(tokens, 'tensor', axis=0, tiled=True)  40.2 us
    dot_general x1, matrix products, body(): jnp.dot(gathered, gate_weight, preferred_element_type=jnp.float32)  15 us
    dot_general x1, matrix products, body(): up_pre = jnp.dot(gathered, up_weight, preferred_element_type=jnp.float32)  11.8 us
    scatter-add x1, other arithmetic, body(): delta = jnp.zeros((request_batch, adapter_up_weight.shape[2]), jnp.float3...  8.3 us
    dot_general x1, matrix products, body(): jnp.einsum('tdb,tbh->tdh', listed_requests, adapter_up_weight, preferred_...  4.69 us
  transfers between devices with their start and end apart: 1, of which 1 were waited for; matrix products, arithmetic and copies ran while one was open for 3% of the time, Pallas kernels for 0%

commit v1 on v0

v1 whole, which is shorter than its diff:
```python
import jax
import jax.numpy as jnp
from jax import lax
from jax.sharding import PartitionSpec as P


def plan(count):
    lines = 1
    while lines * lines < count // 2:
        lines *= 2
    return lines, count // 2 // lines


def body(
    tokens,
    gate_weight,
    up_weight,
    adapter_down_weight,
    adapter_up_weight,
    request_adapter_index,
    adapter_request_lists,
    placement,
):
    count = lax.axis_size("tensor")
    depth, width = plan(count)
    rows = tokens.shape[0]
    requests = request_adapter_index.shape[0]
    adapters = placement.shape[0]
    rank_width = adapter_down_weight.shape[2]
    own = lax.axis_index("tensor")

    def send(value, da, db, dc):
        pairs = []
        for i in range(count):
            a, b, c = i // (2 * width), i // 2 % width, i % 2
            pairs.append((i, ((a + da) % depth * width + (b + db) % width) * 2 + (c + dc) % 2))
        return lax.ppermute(value, "tensor", pairs)

    by_line = [tokens] + [send(tokens, j, 0, 0) for j in range(1, depth)]
    plane = list(by_line)
    for k in range(1, width):
        plane += [send(block, 0, k, 0) for block in by_line]
    half = jnp.concatenate(plane, 0)
    other = send(half, 0, 0, 1)
    gathered = jnp.concatenate([half, other], 0)

    slot = jnp.arange(requests, dtype=jnp.int32)
    block, inner = slot // rows, slot % rows
    j, k, m = block % depth, block // depth % width, block // (depth * width)
    origin = ((own // (2 * width) - j) % depth * width + (own // 2 - k) % width) * 2 + (own + m) % 2
    row_id = origin * rows + inner

    owner = jnp.sum(jnp.where(placement == own, jnp.arange(adapters, dtype=jnp.int32), 0))
    wanted = lax.dynamic_slice_in_dim(adapter_request_lists, owner, 1, 0)[0]
    picker = (wanted[:, None] == row_id[None, :]).astype(jnp.bfloat16)
    picked = jnp.dot(picker, gathered, preferred_element_type=jnp.float32).astype(jnp.bfloat16)
    low_rank = jnp.dot(picked, adapter_down_weight[0], preferred_element_type=jnp.float32)
    spread = (jnp.arange(requests, dtype=jnp.int32)[:, None] == wanted[None, :]).astype(jnp.bfloat16)
    mixed = jnp.dot(spread, low_rank.astype(jnp.bfloat16), preferred_element_type=jnp.float32)
    mixed = mixed.astype(jnp.bfloat16)
    step = 1
    while step < count:
        mixed = mixed + lax.ppermute(mixed, "tensor", [(i, i ^ step) for i in range(count)])
        step *= 2

    gate_pre = jnp.dot(gathered, gate_weight, preferred_element_type=jnp.float32)
    up_pre = jnp.dot(gathered, up_weight, preferred_element_type=jnp.float32)
    here = (row_id[:, None] == jnp.arange(requests, dtype=jnp.int32)[None, :]).astype(jnp.bfloat16)
    mine = jnp.dot(here, mixed, preferred_element_type=jnp.float32).astype(jnp.bfloat16)
    index = jnp.take(request_adapter_index, row_id)
    chosen = index[:, None] == jnp.arange(adapters, dtype=jnp.int32)[None, :]
    expanded = jnp.where(chosen[:, :, None], mine[:, None, :], jnp.zeros((), jnp.bfloat16))
    delta = jnp.dot(
        expanded.reshape(requests, adapters * rank_width),
        adapter_up_weight.reshape(adapters * rank_width, -1),
        preferred_element_type=jnp.float32,
    )
    hidden = (jax.nn.silu(gate_pre) * (up_pre + delta)).astype(jnp.bfloat16)
    return jnp.dot(here.T, hidden, preferred_element_type=jnp.float32).astype(jnp.bfloat16)


def solution(mesh):
    in_specs = (
        P(("groups", "tensor"), None),
        P(None, "tensor"),
        P(None, "tensor"),
        P(("groups", "tensor"), None, None),
        P("groups", None, "tensor"),
        P("groups"),
        P("groups", None),
        P("groups"),
    )
    out_specs = P("groups", "tensor")
    return jax.shard_map(body, mesh=mesh, in_specs=in_specs, out_specs=out_specs, check_vma=False)
```

time: 165 us -> 71.8 us (0.44)
  blocking collectives: 59.6 us -> 0 us
  waiting for transfers between devices: 41 us -> 9.81 us
  starting transfers between devices: 0.01 us -> 18.7 us
  between operations: 15.4 us -> 2.07 us
  other arithmetic: 11.7 us -> 1.15 us
  local copies, waits for them, and re-layouts: 2.82 us -> 9.51 us
  matrix products: 33.9 us -> 30.4 us
    psum x1 -> x0, blocking collectives: 59.6 us -> none  [body(): mixed = lax.psum(partial_value, 'tensor').astype(jnp.bfloat16)]
    all_gather x1 -> x0, waiting for transfers between devices: 40.2 us -> none  [body(): gathered = lax.all_gather(tokens, 'tensor', axis=0, tiled=True)]
    ppermute x0 -> x12, starting transfers between devices: none -> 18.7 us  [the longest x8 11.9 us: send(): return lax.ppermute(value, 'tensor', pairs)]
    ppermute x0 -> x12, waiting for transfers between devices: none -> 9.81 us  [the longest x8 5.12 us: send(): return lax.ppermute(value, 'tensor', pairs)]
    scatter-add x2 -> x0, other arithmetic: 9.04 us -> none  [the longest x1 8.3 us: body(): delta = jnp.zeros((request_batch, adapter_up_weight.shape[2]), jnp.float3...]
    unnamed x6 -> x17, local copies, waits for them, and re-layouts: 0.01 us -> 5.63 us
    dot_general x1, matrix products: 15 us -> 12.4 us  [body(): jnp.dot(gathered, gate_weight, preferred_element_type=jnp.float32)]
    concatenate x0 -> x2, local copies, waits for them, and re-layouts: none -> 1.96 us  [the longest x1 1.29 us: body(): gathered = jnp.concatenate([half, other], 0)]
  transfers between devices with their start and end apart: 1 -> 12, of which waited for: 1 -> 6; matrix products, arithmetic and copies ran while one was open for 3% -> 29% of each run, Pallas kernels for 0% -> 0%
where the time goes in v1:
time: 71.8 us; the launch traced here: 71.6 us
  matrix products  30.4 us (42%)
  starting transfers between devices  18.7 us (26%)
  waiting for transfers between devices  9.81 us (14%)
  local copies, waits for them, and re-layouts  9.51 us (13%)
  between operations  2.07 us (3%)
  other arithmetic  1.15 us (2%)
    dot_general x1, matrix products, body(): jnp.dot(here.T, hidden, preferred_element_type=jnp.float32)  15 us
    dot_general x1, matrix products, body(): jnp.dot(gathered, gate_weight, preferred_element_type=jnp.float32)  12.4 us
    ppermute x8, starting transfers between devices, send(): return lax.ppermute(value, 'tensor', pairs)  11.9 us
    ppermute x4, starting transfers between devices, body(): lax.ppermute(mixed, 'tensor', [(i, i ^ step) for i in range(count)])  6.73 us
    unnamed x17, local copies, waits for them, and re-layouts  5.63 us
    ppermute x8, waiting for transfers between devices, send(): return lax.ppermute(value, 'tensor', pairs)  5.12 us
    ppermute x4, waiting for transfers between devices, body(): lax.ppermute(mixed, 'tensor', [(i, i ^ step) for i in range(count)])  4.69 us
    dot_general x1, matrix products, body(): jnp.dot(expanded.reshape(requests, adapters * rank_width), adapter_up_wei...  1.75 us
  transfers between devices with their start and end apart: 12, of which 6 were waited for; matrix products, arithmetic and copies ran while one was open for 29% of the time, Pallas kernels for 0%

profile of v1, /device:TPU:0, one launch (start us, length us, event | category | flops | bytes accessed | tf_op | source)
XLA Modules:
  0.0 71.6 jit_solution(16915644230550034911)
XLA Ops:
  0.0 3.1 %collective-permute-start = (bf16[8,8192]{1,0:T(8,128)(2,1)}, bf16[8,8192]{1,0:T(8,128)(2,1)S(1)}, u32[]{:S(2)}, u32[]{:S(2)}) collective-permute-start(bf16[8,8192]{1,0:T(8,128)(2,1)} %param.8), channel_id=1, source_target_pairs={{0,4},{1,5},{2,6},{3,7},{4,8},{5,9},{6,10},{7,11},{8,12},{9,13},{1... | collective-permute-start | bytes 393224 | tf_op jit(solution)/shard_map/ppermute | solution.py:37
  3.1 2.6 %collective-permute-start.1 = (bf16[8,8192]{1,0:T(8,128)(2,1)}, bf16[8,8192]{1,0:T(8,128)(2,1)S(1)}, u32[]{:S(2)}, u32[]{:S(2)}) collective-permute-start(bf16[8,8192]{1,0:T(8,128)(2,1)} %param.8), channel_id=1, source_target_pairs={{0,8},{1,9},{2,10},{3,11},{4,12},{5,13},{6,14},{7,15},{8,0},{9,1},... | collective-permute-start | bytes 393224 | tf_op jit(solution)/shard_map/ppermute | solution.py:37
  5.7 1.3 %collective-permute-start.2 = (bf16[8,8192]{1,0:T(8,128)(2,1)}, bf16[8,8192]{1,0:T(8,128)(2,1)S(1)}, u32[]{:S(2)}, u32[]{:S(2)}) collective-permute-start(bf16[8,8192]{1,0:T(8,128)(2,1)} %param.8), channel_id=1, source_target_pairs={{0,12},{1,13},{2,14},{3,15},{4,0},{5,1},{6,2},{7,3},{8,4},{9,5},{1... | collective-permute-start | bytes 393224 | tf_op jit(solution)/shard_map/ppermute | solution.py:37
  7.0 1.5 %collective-permute-start.3 = (bf16[8,8192]{1,0:T(8,128)(2,1)}, bf16[8,8192]{1,0:T(8,128)(2,1)S(1)}, u32[]{:S(2)}, u32[]{:S(2)}) collective-permute-start(bf16[8,8192]{1,0:T(8,128)(2,1)} %param.8), channel_id=1, source_target_pairs={{0,2},{1,3},{2,0},{3,1},{4,6},{5,7},{6,4},{7,5},{8,10},{9,11},{10,... | collective-permute-start | bytes 393224 | tf_op jit(solution)/shard_map/ppermute | solution.py:37
  8.5 1.6 %constant_dynamic-update-slice_fusion.7 = (bf16[64,8192]{1,0:T(8,128)(2,1)}, bf16[128,8192]{1,0:T(8,128)(2,1)S(1)}) fusion(bf16[8,8192]{1,0:T(8,128)(2,1)} %param.8), kind=kLoop, calls=%fused_computation.23 | loop fusion | bytes 393216
  10.2 1.4 %collective-permute-start.4 = (bf16[8,8192]{1,0:T(8,128)(2,1)S(1)}, bf16[8,8192]{1,0:T(8,128)(2,1)S(1)}, u32[]{:S(2)}, u32[]{:S(2)}) collective-permute-start(bf16[8,8192]{1,0:T(8,128)(2,1)S(1)} %collective-permute-done), channel_id=1, source_target_pairs={{0,2},{1,3},{2,0},{3,1},{4,6},{5,7},{6,4},{7,5},{8,10},{9,11},{10,... | collective-permute-start | bytes 393224 | tf_op jit(solution)/shard_map/ppermute | solution.py:37
  11.5 3.0 %collective-permute-done.1 = bf16[8,8192]{1,0:T(8,128)(2,1)S(1)} collective-permute-done((bf16[8,8192]{1,0:T(8,128)(2,1)}, bf16[8,8192]{1,0:T(8,128)(2,1)S(1)}, u32[]{:S(2)}, u32[]{:S(2)}) %collective-permute-start.1) | collective-permute-done | bytes 131104 | tf_op jit(solution)/shard_map/ppermute | solution.py:37
  14.5 1.5 %collective-permute-start.5 = (bf16[8,8192]{1,0:T(8,128)(2,1)S(1)}, bf16[8,8192]{1,0:T(8,128)(2,1)S(1)}, u32[]{:S(2)}, u32[]{:S(2)}) collective-permute-start(bf16[8,8192]{1,0:T(8,128)(2,1)S(1)} %collective-permute-done.1), channel_id=1, source_target_pairs={{0,2},{1,3},{2,0},{3,1},{4,6},{5,7},{6,4},{7,5},{8,10},{9,11},{10,... | collective-permute-start | bytes 393224 | tf_op jit(solution)/shard_map/ppermute | solution.py:37
  18.6 0.7 constant_dynamic-update-slice_fusion.3
  19.9 1.0 %collective-permute-done.5 = bf16[8,8192]{1,0:T(8,128)(2,1)S(1)} collective-permute-done((bf16[8,8192]{1,0:T(8,128)(2,1)S(1)}, bf16[8,8192]{1,0:T(8,128)(2,1)S(1)}, u32[]{:S(2)}, u32[]{:S(2)}) %collective-permute-start.5) | collective-permute-done | bytes 131104 | tf_op jit(solution)/shard_map/ppermute | solution.py:37
  21.6 1.1 %collective-permute-done.6 = bf16[8,8192]{1,0:T(8,128)(2,1)S(1)} collective-permute-done((bf16[8,8192]{1,0:T(8,128)(2,1)S(1)}, bf16[8,8192]{1,0:T(8,128)(2,1)S(1)}, u32[]{:S(2)}, u32[]{:S(2)}) %collective-permute-start.6) | collective-permute-done | bytes 131104 | tf_op jit(solution)/shard_map/ppermute | solution.py:37
  25.3 1.2 %gather_fusion = s32[128]{0:T(128)S(1)} fusion(s32[128]{0:T(128)S(1)} %copy-done.2, s32[1024]{0:T(1024)S(1)} %pad_clamp_fusion), kind=kCustom, calls=%fused_computation | custom fusion | bytes 1536 | tf_op jit(solution)/shard_map/jit(_take)/gather | solution.py:70
  27.2 0.7 dynamic-slice_bitcast_fusion
  28.0 1.3 %constant_dynamic-update-slice_fusion.8 = bf16[128,8192]{1,0:T(8,128)(2,1)S(1)} fusion(bf16[128,8192]{1,0:T(8,128)(2,1)S(1)} %get-tuple-element.8, bf16[64,8192]{1,0:T(8,128)(2,1)} %collective-permute-done.7), kind=kLoop, calls=%fused_computation.24 | loop fusion | bytes 2097152 | tf_op jit(solution)/shard_map/concatenate | solution.py:45
  29.3 0.8 %fusion.1 = bf16[32,64]{1,0:T(8,128)(2,1)S(1)} fusion(bf16[128,8192]{1,0:T(8,128)(2,1)S(1)} %constant_dynamic-update-slice_fusion.8, bf16[1,8192,64]{1,2,0:T(8,128)(2,1)S(1)} %copy-done, s32[128]{0:T(128)S(1)} %get-tuple-element.6, s32[32]{0:T(128)S(1)} %dynamic-slice_bitcast_fusion), kind=kOutput, calls=%fused_computation.8 | convolution fusion | flops 100931584 | bytes 3150464 | tf_op jit(solution)/shard_map/dot_general | solution.py:57
  30.8 0.8 %collective-permute-done.8 = bf16[128,64]{0,1:T(8,128)(2,1)S(1)} collective-permute-done((bf16[128,64]{0,1:T(8,128)(2,1)S(1)}, bf16[128,64]{0,1:T(8,128)(2,1)S(1)}, u32[]{:S(2)}, u32[]{:S(2)}) %collective-permute-start.8) | collective-permute-done | bytes 16416 | tf_op jit(solution)/shard_map/ppermute | solution.py:63
  31.7 1.6 %collective-permute-start.9 = (bf16[128,64]{0,1:T(8,128)(2,1)S(1)}, bf16[128,64]{0,1:T(8,128)(2,1)S(1)}, u32[]{:S(2)}, u32[]{:S(2)}) collective-permute-start(bf16[128,64]{0,1:T(8,128)(2,1)S(1)} %add.389), channel_id=1, source_target_pairs={{0,2},{1,3},{2,0},{3,1},{4,6},{5,7},{6,4},{7,5},{8,10},{9,11},{10,... | collective-permute-start | bytes 49160 | tf_op jit(solution)/shard_map/ppermute | solution.py:63
  33.3 2.2 %collective-permute-done.9 = bf16[128,64]{0,1:T(8,128)(2,1)S(1)} collective-permute-done((bf16[128,64]{0,1:T(8,128)(2,1)S(1)}, bf16[128,64]{0,1:T(8,128)(2,1)S(1)}, u32[]{:S(2)}, u32[]{:S(2)}) %collective-permute-start.9) | collective-permute-done | bytes 16416 | tf_op jit(solution)/shard_map/ppermute | solution.py:63
  35.5 2.1 %collective-permute-start.10 = (bf16[128,64]{0,1:T(8,128)(2,1)S(1)}, bf16[128,64]{0,1:T(8,128)(2,1)S(1)}, u32[]{:S(2)}, u32[]{:S(2)}) collective-permute-start(bf16[128,64]{0,1:T(8,128)(2,1)S(1)} %add.390), channel_id=1, source_target_pairs={{0,4},{1,5},{2,6},{3,7},{4,0},{5,1},{6,2},{7,3},{8,12},{9,13},{10,... | collective-permute-start | bytes 49160 | tf_op jit(solution)/shard_map/ppermute | solution.py:63
  37.7 1.6 %collective-permute-done.10 = bf16[128,64]{0,1:T(8,128)(2,1)S(1)} collective-permute-done((bf16[128,64]{0,1:T(8,128)(2,1)S(1)}, bf16[128,64]{0,1:T(8,128)(2,1)S(1)}, u32[]{:S(2)}, u32[]{:S(2)}) %collective-permute-start.10) | collective-permute-done | bytes 16416 | tf_op jit(solution)/shard_map/ppermute | solution.py:63
  39.4 2.5 %collective-permute-start.11 = (bf16[128,64]{0,1:T(8,128)(2,1)S(1)}, bf16[128,64]{0,1:T(8,128)(2,1)S(1)}, u32[]{:S(2)}, u32[]{:S(2)}) collective-permute-start(bf16[128,64]{0,1:T(8,128)(2,1)S(1)} %add.391), channel_id=1, source_target_pairs={{0,8},{1,9},{2,10},{3,11},{4,12},{5,13},{6,14},{7,15},{8,0},{9,1},... | collective-permute-start | bytes 49160 | tf_op jit(solution)/shard_map/ppermute | solution.py:63
  41.8 12.4 %fusion.38 = f32[128,1792]{1,0:T(8,128)} fusion(bf16[128,8192]{1,0:T(8,128)(2,1)S(1)} %constant_dynamic-update-slice_fusion.8, bf16[8192,1792]{1,0:T(8,128)(2,1)} %param.9), kind=kOutput, calls=%fused_computation.119 | convolution fusion | flops 3758096384 | bytes 32374784 | tf_op jit(solution)/shard_map/dot_general | solution.py:66
  54.8 1.7 %convolution_bitcast_fusion = f32[128,1792]{1,0:T(8,128)} fusion(bf16[16,64,1792]{2,1,0:T(8,128)(2,1)S(1)} %copy-done.3, bf16[128,16,64]{2,1,0:T(8,128)(2,1)S(1)} %broadcast_select_fusion), kind=kOutput, calls=%fused_computation.2 | convolution fusion | flops 469762048 | bytes 4849664 | tf_op jit(solution)/shard_map/dot_general | solution.py:73
  56.5 15.0 %convolution_convert_fusion.1 = bf16[128,1792]{1,0:T(8,128)(2,1)} fusion(f32[128,1792]{1,0:T(8,128)} %fusion.38, f32[128,1792]{1,0:T(8,128)} %convolution_bitcast_fusion, bf16[128,8192]{1,0:T(8,128)(2,1)S(1)} %constant_dynamic-update-slice_fusion.8, bf16[8192,1792]{1,0:T(8,128)(2,1)} %param.10, s32[128]{0:T(128)S(1)} %get-tuple-element.6), kind=kOutput, calls=%fused_computation.4 | convolution fusion | flops 3818668032 | bytes 33751552 | tf_op jit(solution)/shard_map/dot_general | solution.py:79
  (36 shorter events, 6.6 us)
Async XLA Ops:
  0.0 29.3 %copy-start = (bf16[1,8192,64]{1,2,0:T(8,128)(2,1)S(1)}, bf16[1,8192,64]{1,2,0:T(8,128)(2,1)}, u32[]{:S(2)}) copy-start(bf16[1,8192,64]{1,2,0:T(8,128)(2,1)} %param.11) | copy-start | bytes 3145732
  0.0 23.3 %copy-start.4 = (s32[16]{0:T(128)S(1)}, s32[16]{0:T(128)}, u32[]{:S(2)}) copy-start(s32[16]{0:T(128)} %param.15) | copy-start | bytes 196
  0.0 25.3 %copy-start.2 = (s32[128]{0:T(128)S(1)}, s32[128]{0:T(128)}, u32[]{:S(2)}) copy-start(s32[128]{0:T(128)} %param.13) | copy-start | bytes 1540
  0.0 10.1 %collective-permute-start = (bf16[8,8192]{1,0:T(8,128)(2,1)}, bf16[8,8192]{1,0:T(8,128)(2,1)S(1)}, u32[]{:S(2)}, u32[]{:S(2)}) collective-permute-start(bf16[8,8192]{1,0:T(8,128)(2,1)} %param.8), channel_id=1, source_target_pairs={{0,4},{1,5},{2,6},{3,7},{4,8},{5,9},{6,10},{7,11},{8,12},{9,13},{1... | collective-permute-start | bytes 393224 | tf_op jit(solution)/shard_map/ppermute | solution.py:37
  3.1 11.4 %collective-permute-start.1 = (bf16[8,8192]{1,0:T(8,128)(2,1)}, bf16[8,8192]{1,0:T(8,128)(2,1)S(1)}, u32[]{:S(2)}, u32[]{:S(2)}) collective-permute-start(bf16[8,8192]{1,0:T(8,128)(2,1)} %param.8), channel_id=1, source_target_pairs={{0,8},{1,9},{2,10},{3,11},{4,12},{5,13},{6,14},{7,15},{8,0},{9,1},... | collective-permute-start | bytes 393224 | tf_op jit(solution)/shard_map/ppermute | solution.py:37
  5.7 10.4 %collective-permute-start.2 = (bf16[8,8192]{1,0:T(8,128)(2,1)}, bf16[8,8192]{1,0:T(8,128)(2,1)S(1)}, u32[]{:S(2)}, u32[]{:S(2)}) collective-permute-start(bf16[8,8192]{1,0:T(8,128)(2,1)} %param.8), channel_id=1, source_target_pairs={{0,12},{1,13},{2,14},{3,15},{4,0},{5,1},{6,2},{7,3},{8,4},{9,5},{1... | collective-permute-start | bytes 393224 | tf_op jit(solution)/shard_map/ppermute | solution.py:37
  7.0 11.5 %collective-permute-start.3 = (bf16[8,8192]{1,0:T(8,128)(2,1)}, bf16[8,8192]{1,0:T(8,128)(2,1)S(1)}, u32[]{:S(2)}, u32[]{:S(2)}) collective-permute-start(bf16[8,8192]{1,0:T(8,128)(2,1)} %param.8), channel_id=1, source_target_pairs={{0,2},{1,3},{2,0},{3,1},{4,6},{5,7},{6,4},{7,5},{8,10},{9,11},{10,... | collective-permute-start | bytes 393224 | tf_op jit(solution)/shard_map/ppermute | solution.py:37
  10.2 9.1 %collective-permute-start.4 = (bf16[8,8192]{1,0:T(8,128)(2,1)S(1)}, bf16[8,8192]{1,0:T(8,128)(2,1)S(1)}, u32[]{:S(2)}, u32[]{:S(2)}) collective-permute-start(bf16[8,8192]{1,0:T(8,128)(2,1)S(1)} %collective-permute-done), channel_id=1, source_target_pairs={{0,2},{1,3},{2,0},{3,1},{4,6},{5,7},{6,4},{7,5},{8,10},{9,11},{10,... | collective-permute-start | bytes 393224 | tf_op jit(solution)/shard_map/ppermute | solution.py:37
  14.5 6.4 %collective-permute-start.5 = (bf16[8,8192]{1,0:T(8,128)(2,1)S(1)}, bf16[8,8192]{1,0:T(8,128)(2,1)S(1)}, u32[]{:S(2)}, u32[]{:S(2)}) collective-permute-start(bf16[8,8192]{1,0:T(8,128)(2,1)S(1)} %collective-permute-done.1), channel_id=1, source_target_pairs={{0,2},{1,3},{2,0},{3,1},{4,6},{5,7},{6,4},{7,5},{8,10},{9,11},{10,... | collective-permute-start | bytes 393224 | tf_op jit(solution)/shard_map/ppermute | solution.py:37
  16.1 6.6 %collective-permute-start.6 = (bf16[8,8192]{1,0:T(8,128)(2,1)S(1)}, bf16[8,8192]{1,0:T(8,128)(2,1)S(1)}, u32[]{:S(2)}, u32[]{:S(2)}) collective-permute-start(bf16[8,8192]{1,0:T(8,128)(2,1)S(1)} %collective-permute-done.2), channel_id=1, source_target_pairs={{0,2},{1,3},{2,0},{3,1},{4,6},{5,7},{6,4},{7,5},{8,10},{9,11},{10,... | collective-permute-start | bytes 393224 | tf_op jit(solution)/shard_map/ppermute | solution.py:37
  23.3 4.6 %collective-permute-start.7 = (bf16[64,8192]{1,0:T(8,128)(2,1)}, bf16[64,8192]{1,0:T(8,128)(2,1)}, u32[]{:S(2)}, u32[]{:S(2)}) collective-permute-start(bf16[64,8192]{1,0:T(8,128)(2,1)} %get-tuple-element.7), channel_id=1, source_target_pairs={{0,1},{1,0},{2,3},{3,2},{4,5},{5,4},{6,7},{7,6},{8,9},{9,8},{10,11... | collective-permute-start | bytes 3145736 | tf_op jit(solution)/shard_map/ppermute | solution.py:37
  30.3 1.4 %collective-permute-start.8 = (bf16[128,64]{0,1:T(8,128)(2,1)S(1)}, bf16[128,64]{0,1:T(8,128)(2,1)S(1)}, u32[]{:S(2)}, u32[]{:S(2)}) collective-permute-start(bf16[128,64]{0,1:T(8,128)(2,1)S(1)} %convolution_convert_fusion.3), channel_id=1, source_target_pairs={{0,1},{1,0},{2,3},{3,2},{4,5},{5,4},{6,7},{7,6},{8,9},{9,8},{10,11... | collective-permute-start | bytes 49160 | tf_op jit(solution)/shard_map/ppermute | solution.py:63
  31.7 3.8 %collective-permute-start.9 = (bf16[128,64]{0,1:T(8,128)(2,1)S(1)}, bf16[128,64]{0,1:T(8,128)(2,1)S(1)}, u32[]{:S(2)}, u32[]{:S(2)}) collective-permute-start(bf16[128,64]{0,1:T(8,128)(2,1)S(1)} %add.389), channel_id=1, source_target_pairs={{0,2},{1,3},{2,0},{3,1},{4,6},{5,7},{6,4},{7,5},{8,10},{9,11},{10,... | collective-permute-start | bytes 49160 | tf_op jit(solution)/shard_map/ppermute | solution.py:63
  35.5 3.9 %collective-permute-start.10 = (bf16[128,64]{0,1:T(8,128)(2,1)S(1)}, bf16[128,64]{0,1:T(8,128)(2,1)S(1)}, u32[]{:S(2)}, u32[]{:S(2)}) collective-permute-start(bf16[128,64]{0,1:T(8,128)(2,1)S(1)} %add.390), channel_id=1, source_target_pairs={{0,4},{1,5},{2,6},{3,7},{4,0},{5,1},{6,2},{7,3},{8,12},{9,13},{10,... | collective-permute-start | bytes 49160 | tf_op jit(solution)/shard_map/ppermute | solution.py:63
  39.4 15.4 %copy-start.3 = (bf16[16,64,1792]{2,1,0:T(8,128)(2,1)S(1)}, bf16[16,64,1792]{2,1,0:T(8,128)(2,1)}, u32[]{:S(2)}) copy-start(bf16[16,64,1792]{2,1,0:T(8,128)(2,1)} %param.12) | copy-start | bytes 11010052
  39.4 14.9 %collective-permute-start.11 = (bf16[128,64]{0,1:T(8,128)(2,1)S(1)}, bf16[128,64]{0,1:T(8,128)(2,1)S(1)}, u32[]{:S(2)}, u32[]{:S(2)}) collective-permute-start(bf16[128,64]{0,1:T(8,128)(2,1)S(1)} %add.391), channel_id=1, source_target_pairs={{0,8},{1,9},{2,10},{3,11},{4,12},{5,13},{6,14},{7,15},{8,0},{9,1},... | collective-permute-start | bytes 49160 | tf_op jit(solution)/shard_map/ppermute | solution.py:63
  56.5 15.0 %copy-start.1 = (bf16[1,8192,64]{1,2,0:T(8,128)(2,1)S(1)}, bf16[1,8192,64]{1,2,0:T(8,128)(2,1)}, u32[]{:S(2)}) copy-start(bf16[1,8192,64]{1,2,0:T(8,128)(2,1)} %param.11) | copy-start | bytes 3145732

commit v2 on v1

--- a/solution.py
+++ b/solution.py
@@ -1,7 +1,25 @@
+import functools
+
 import jax
 import jax.numpy as jnp
 from jax import lax
+from jax.experimental import pallas as pl
+from jax.experimental.pallas import tpu as pltpu
 from jax.sharding import PartitionSpec as P
+
+TILE = 256
+PIECES = 4
+NEAR = pl.BlockSpec(memory_space=pltpu.VMEM)
+FAR = pl.BlockSpec(memory_space=pl.ANY)
+STORED = pl.BlockSpec(memory_space=pltpu.HBM)
+
+
+def near(value):
+    return pltpu.with_memory_space_constraint(value, pltpu.VMEM)
+
+
+def far(value):
+    return pltpu.with_memory_space_constraint(value, pltpu.HBM)
 
 
 def plan(count):
@@ -11,7 +29,337 @@
     return lines, count // 2 // lines
 
 
-def body(
+def send(value, da, db, dc):
+    count = lax.axis_size("tensor")
+    depth, width = plan(count)
+    pairs = []
+    for i in range(count):
+        a, b, c = i // (2 * width), i // 2 % width, i % 2
+        pairs.append((i, ((a + da) % depth * width + (b + db) % width) * 2 + (c + dc) % 2))
+    return lax.ppermute(value, "tensor", pairs)
+
+
+def fetch_kernel(start, skipped, source, *refs):
+    target, sems = refs[skipped:]
+    rows = target.shape[0] // sems.shape[0]
+    copies = [
+        pltpu.make_async_copy(
+            source.at[pl.ds(start + i * rows, rows)], target.at[pl.ds(i * rows, rows)], sems.at[i]
+        )
+        for i in range(sems.shape[0])
+    ]
+    for copy in copies:
+        copy.start()
+    for copy in copies:
+        copy.wait()
+
+
+def fetch(weight, start, rows, name, after=()):
+    return pl.pallas_call(
+        functools.partial(fetch_kernel, start, len(after)),
+        out_shape=pltpu.VMEM((rows, weight.shape[1]), weight.dtype),
+        in_specs=[STORED] + [FAR] * len(after),
+        out_specs=NEAR,
+        scratch_shapes=[pltpu.SemaphoreType.DMA((4,))],
+        cost_estimate=pl.CostEstimate(
+            flops=0, bytes_accessed=rows * weight.shape[1] * 2, transcendentals=0
+        ),
+        compiler_params=pltpu.CompilerParams(vmem_limit_bytes=1 << 20),
+        name=name,
+    )(far(weight), *after)
+
+
+def across(row):
+    n = row.shape[1]
+    return jnp.broadcast_to(row, (n, n)).T
+
+
+def pack_kernel(n, *refs):
+    for i in range(n):
+        refs[-1][i] = refs[i][...]
+
+
+def pack(blocks, after):
+    rows, model = blocks[0].shape
+    n = len(blocks)
+    return pl.pallas_call(
+        functools.partial(pack_kernel, n),
+        out_shape=pltpu.VMEM((n, rows, model), jnp.bfloat16),
+        in_specs=[NEAR] * n + [FAR] * len(after),
+        out_specs=NEAR,
+        cost_estimate=pl.CostEstimate(flops=0, bytes_accessed=1 << 18, transcendentals=0),
+        compiler_params=pltpu.CompilerParams(vmem_limit_bytes=1 << 20),
+        name="pack",
+    )(*[near(v) for v in blocks], *after)
+
+
+def tie_kernel(*refs):
+    pass
+
+
+def tie(value, after):
+    return pl.pallas_call(
+        tie_kernel,
+        out_shape=jax.ShapeDtypeStruct(value.shape, value.dtype),
+        in_specs=[FAR] * (1 + len(after)),
+        out_specs=FAR,
+        input_output_aliases={0: 0},
+        cost_estimate=pl.CostEstimate(flops=0, bytes_accessed=1 << 10, transcendentals=0),
+        compiler_params=pltpu.CompilerParams(vmem_limit_bytes=1 << 20),
+        name="tie",
+    )(value, *after)
+
+
+def collect_kernel(depth, width, placement, index, down, *refs):
+    blocks = 2 * width
+    mine, theirs = refs[:blocks], refs[blocks : 2 * blocks]
+    packed, low = refs[2 * blocks :]
+    own = lax.axis_index("tensor")
+    a, b, c = own // (2 * width), own // 2 % width, own % 2
+    rows = mine[0].shape[0]
+    for k in range(width):
+        for j in range(depth):
+            chip = lax.rem(a - j + depth, depth) * width + lax.rem(b - k + width, width)
+            if j == 0:
+                p, q = mine[2 * k][...], theirs[2 * k][...]
+            else:
+                p, q = mine[2 * k + 1][j - 1], theirs[2 * k + 1][j - 1]
+            first, second = jnp.where(c == 0, p, q), jnp.where(c == 0, q, p)
+            packed[pl.ds(pl.multiple_of(chip * 2 * rows, 2 * rows), 2 * rows), :] = (
+                jnp.concatenate([first, second], 0)
+            )
+    full = lax.dot_general(
+        packed[...], down[...], (((1,), (1,)), ((), ())), preferred_element_type=jnp.float32
+    )
+    ids = lax.broadcasted_iota(jnp.int32, placement.shape, 1)
+    owner = jnp.sum(jnp.where(placement[...] == own, ids, 0), axis=1, keepdims=True)
+    chosen = across(jnp.where(index[...] == owner, 1, 0))[:, : full.shape[1]]
+    low[...] = jnp.where(chosen == 1, full, 0.0).astype(low.dtype)
+
+
+def collect(placement, index, down, mine, theirs, depth, width):
+    rows, model = mine[0].shape
+    requests = 2 * depth * width * rows
+    return pl.pallas_call(
+        functools.partial(collect_kernel, depth, width),
+        out_shape=[
+            pltpu.VMEM((requests, model), jnp.bfloat16),
+            jax.ShapeDtypeStruct((requests, down.shape[0]), jnp.bfloat16),
+        ],
+        in_specs=[NEAR] * (3 + 4 * width),
+        out_specs=[NEAR] * 2,
+        cost_estimate=pl.CostEstimate(
+            flops=2 * requests * model * 64, bytes_accessed=1 << 20, transcendentals=0
+        ),
+        compiler_params=pltpu.CompilerParams(vmem_limit_bytes=4 << 20),
+        name="collect",
+    )(placement, index, down, *[near(v) for v in mine], *[near(v) for v in theirs])
+
+
+def add_kernel(*refs):
+    total = refs[0][...]
+    for ref in refs[1:-1]:
+        total = total + ref[...]
+    refs[-1][...] = total
+
+
+def add(*values):
+    return pl.pallas_call(
+        add_kernel,
+        out_shape=jax.ShapeDtypeStruct(values[0].shape, values[0].dtype),
+        in_specs=[NEAR] * len(values),
+        out_specs=NEAR,
+        cost_estimate=pl.CostEstimate(flops=0, bytes_accessed=1 << 14, transcendentals=0),
+        compiler_params=pltpu.CompilerParams(vmem_limit_bytes=1 << 20),
+        name="add",
+    )(*values)
+
+
+def piecewise(tokens, pieces, start, here):
+    total = None
+    for piece in pieces:
+        rows = piece.shape[0]
+        term = jnp.dot(
+            tokens[:, start : start + rows], piece[:, here], preferred_element_type=jnp.float32
+        )
+        total = term if total is None else total + term
+        start += rows
+    return total
+
+
+def multiply_kernel(start, n, begun, fetched, *refs):
+    tokens, refs = refs[1], refs[2:]
+    pieces, refs = refs[:n], refs[n:]
+    before, refs = refs[:begun], refs[begun:]
+    copies = []
+    if fetched:
+        source, out, *targets, sems = refs
+        first = fetched[0]
+        for i, target in enumerate(targets):
+            rows = target.shape[0]
+            copies.append(
+                pltpu.make_async_copy(source.at[pl.ds(first, rows)], target, sems.at[i])
+            )
+            first += rows
+    else:
+        (out,) = refs
+    for copy in copies:
+        copy.start()
+
+    @pl.loop(0, out.shape[1] // TILE)
+    def _(i):
+        here = pl.ds(pl.multiple_of(i * TILE, TILE), TILE)
+        total = piecewise(tokens, pieces, start, here)
+        if begun:
+            total = total + before[0][:, here]
+        out[:, here] = total
+
+    for copy in copies:
+        copy.wait()
+
+
+def multiply(after, tokens, pieces, start, begun, source, fetched, name):
+    requests = tokens.shape[0]
+    hidden = pieces[0].shape[1]
+    out_shape = [pltpu.VMEM((requests, hidden), jnp.float32)]
+    operands = [after, near(tokens)] + [near(p) for p in pieces] + [near(b) for b in begun]
+    in_specs = [FAR] + [NEAR] * (len(operands) - 1)
+    scratch = []
+    if fetched:
+        operands.append(far(source))
+        in_specs.append(STORED)
+        out_shape += [pltpu.VMEM((r, hidden), source.dtype) for r in fetched[1:]]
+        scratch = [pltpu.SemaphoreType.DMA((len(fetched) - 1,))]
+    return pl.pallas_call(
+        functools.partial(multiply_kernel, start, len(pieces), len(begun), fetched),
+        out_shape=out_shape,
+        in_specs=in_specs,
+        out_specs=[NEAR] * len(out_shape),
+        scratch_shapes=scratch,
+        cost_estimate=pl.CostEstimate(
+            flops=2 * requests * sum(p.shape[0] for p in pieces) * hidden,
+            bytes_accessed=16 << 20,
+            transcendentals=0,
+        ),
+        compiler_params=pltpu.CompilerParams(vmem_limit_bytes=2 << 20),
+        name=name,
+    )(*operands)
+
+
+def finish_kernel(start, n, m, index, tokens, adapter_up, gate_pre, up_pre, *refs):
+    pieces, refs = refs[:n], refs[n:]
+    lows, refs = refs[:m], refs[m:]
+    out, near_up, expanded, sem = refs
+    rank = lows[0].shape[1]
+    copy = pltpu.make_async_copy(adapter_up, near_up, sem)
+    copy.start()
+    mixed = lows[0][...]
+    for low in lows[1:]:
+        mixed = mixed + low[...]
+    group = TILE // rank
+    lane = lax.broadcasted_iota(jnp.int32, (rank, TILE), 1)
+    repeat = (lane % rank == lax.broadcasted_iota(jnp.int32, (rank, TILE), 0)).astype(jnp.bfloat16)
+    wide = jnp.dot(mixed, repeat, preferred_element_type=jnp.float32)
+    of_lane = lax.broadcasted_iota(jnp.int32, (mixed.shape[0], TILE), 1) // rank
+    relative = jnp.concatenate([across(index[...])] * (TILE // mixed.shape[0]), 1) - of_lane
+    for i in range(expanded.shape[1] // TILE):
+        expanded[:, i * TILE : (i + 1) * TILE] = jnp.where(
+            relative == i * group, wide, 0.0
+        ).astype(jnp.bfloat16)
+    copy.wait()
+
+    @pl.loop(0, out.shape[1] // TILE)
+    def _(i):
+        here = pl.ds(pl.multiple_of(i * TILE, TILE), TILE)
+        up = up_pre[:, here] + piecewise(tokens, pieces, start, here)
+        up = up + jnp.dot(expanded[...], near_up[:, here], preferred_element_type=jnp.float32)
+        gate = gate_pre[:, here]
+        out[:, here] = (gate / (1.0 + jnp.exp(-gate)) * up).astype(out.dtype)
+
+
+def finish(index, tokens, adapter_up, gate_pre, up_pre, pieces, start, lows):
+    requests = tokens.shape[0]
+    hidden = adapter_up.shape[1]
+    return pl.pallas_call(
+        functools.partial(finish_kernel, start, len(pieces), len(lows)),
+        out_shape=jax.ShapeDtypeStruct((requests, hidden), jnp.bfloat16),
+        in_specs=[NEAR, NEAR, STORED] + [NEAR] * (len(pieces) + len(lows) + 2),
+        out_specs=NEAR,
+        scratch_shapes=[
+            pltpu.VMEM(adapter_up.shape, jnp.bfloat16),
+            pltpu.VMEM((requests, adapter_up.shape[0]), jnp.bfloat16),
+            pltpu.SemaphoreType.DMA,
+        ],
+        cost_estimate=pl.CostEstimate(
+            flops=2 * requests * sum(p.shape[0] for p in pieces) * hidden,
+            bytes_accessed=4 << 20,
+            transcendentals=requests * hidden,
+        ),
+        compiler_params=pltpu.CompilerParams(vmem_limit_bytes=8 << 20),
+        name="finish",
+    )(
+        index,
+        near(tokens),
+        far(adapter_up),
+        near(gate_pre),
+        near(up_pre),
+        *[near(p) for p in pieces],
+        *lows,
+    )
+
+
+def on_chip(tokens, gate_weight, up_weight, down, up, request_adapter_index, placement):
+    count = lax.axis_size("tensor")
+    depth, width = plan(count)
+    model, hidden = gate_weight.shape
+    index = request_adapter_index[None, :]
+    part = model // PIECES
+
+    by_line = [send(tokens, j, 0, 0) for j in range(1, depth)]
+    across_own = [send(tokens, 0, k, 0) for k in range(1, width)]
+    core_own = send(tokens, 0, 0, 1)
+    gate_0 = fetch(gate_weight, 0, part, "fetch_0")
+    gate_1 = fetch(gate_weight, part, part, "fetch_1")
+    line = pack(by_line, [gate_0, gate_1, core_own, *across_own])
+    across_line = [send(line, 0, k, 0) for k in range(1, width)]
+    core_line = send(line, 0, 0, 1)
+    core_across_own = [send(v, 0, 0, 1) for v in across_own]
+    gate_2 = fetch(gate_weight, 2 * part, part, "fetch_2", [line])
+    gate_3 = fetch(gate_weight, 3 * part, part, "fetch_3", [line])
+    across_line = [tie(v, [gate_2, gate_3]) for v in across_line]
+    core_across_line = [send(v, 0, 0, 1) for v in across_line]
+    mine, theirs = [tokens, line], [core_own, core_line]
+    for own_block, line_block in zip(across_own, across_line):
+        mine += [own_block, line_block]
+    for own_block, line_block in zip(core_across_own, core_across_line):
+        theirs += [own_block, line_block]
+    packed, low = collect(
+        placement[None, :], index, jnp.swapaxes(down[0], 0, 1), mine, theirs, depth, width
+    )
+
+    low_1 = add(low, send(low, 0, 0, 1))
+    gate_pre, up_0, up_1 = multiply(
+        low, packed, [gate_0, gate_1], 0, [], up_weight, (0, part, part), "gate_a"
+    )
+    low_2 = add(low_1, *[send(low_1, 0, k, 0) for k in range(1, width)])
+    gate_pre, up_2, up_3 = multiply(
+        low_1,
+        packed,
+        [gate_2, gate_3],
+        2 * part,
+        [gate_pre],
+        up_weight,
+        (2 * part, part, part),
+        "gate_b",
+    )
+    lows = [low_2] + [send(low_2, j, 0, 0) for j in range(1, depth)]
+    (up_pre,) = multiply(low_2, packed, [up_0, up_1], 0, [], None, (), "up_a")
+    return finish(
+        index, packed, up.reshape(-1, hidden), gate_pre, up_pre, [up_2, up_3], 2 * part, lows
+    )
+
+
+def streamed(
     tokens,
     gate_weight,
     up_weight,
@@ -29,13 +377,6 @@
     rank_width = adapter_down_weight.shape[2]
     own = lax.axis_index("tensor")
 
-    def send(value, da, db, dc):
-        pairs = []
-        for i in range(count):
-            a, b, c = i // (2 * width), i // 2 % width, i % 2
-            pairs.append((i, ((a + da) % depth * width + (b + db) % width) * 2 + (c + dc) % 2))
-        return lax.ppermute(value, "tensor", pairs)
-
     by_line = [tokens] + [send(tokens, j, 0, 0) for j in range(1, depth)]
     plane = list(by_line)
     for k in range(1, width):
@@ -79,6 +420,38 @@
     return jnp.dot(here.T, hidden, preferred_element_type=jnp.float32).astype(jnp.bfloat16)
 
 
+def body(
+    tokens,
+    gate_weight,
+    up_weight,
+    adapter_down_weight,
+    adapter_up_weight,
+    request_adapter_index,
+    adapter_request_lists,
+    placement,
+):
+    if request_adapter_index.shape[0] <= 128:
+        return on_chip(
+            tokens,
+            gate_weight,
+            up_weight,
+            adapter_down_weight,
+            adapter_up_weight,
+            request_adapter_index,
+            placement,
+        )
+    return streamed(
+        tokens,
+        gate_weight,
+        up_weight,
+        adapter_down_weight,
+        adapter_up_weight,
+        request_adapter_index,
+        adapter_request_lists,
+        placement,
+    )
+
+
 def solution(mesh):
     in_specs = (
         P(("groups", "tensor"), None),

time: 71.8 us -> 58.1 us (0.81)
  Pallas kernels: 0 us -> 34.3 us
  matrix products: 30.4 us -> 0 us
  local copies, waits for them, and re-layouts: 9.51 us -> 0.03 us
  waiting for transfers between devices: 9.81 us -> 7.13 us
  starting transfers between devices: 18.7 us -> 16.3 us
  between operations: 2.07 us -> 0.22 us
  other arithmetic: 1.15 us -> 0 us
    pallas_call x0 -> x13, Pallas kernels: none -> 34.3 us  [the longest x3 13.6 us: multiply(): pl.pallas_call(functools.partial(multiply_kernel, start, len(pieces), len...]
    dot_general x6 -> x0, matrix products: 30.4 us -> none  [the longest x1 15 us: body(): jnp.dot(here.T, hidden, preferred_element_type=jnp.float32)]
    ppermute x4 -> x0, starting transfers between devices: 6.73 us -> none  [body(): lax.ppermute(mixed, 'tensor', [(i, i ^ step) for i in range(count)])]
    unnamed x17 -> x8, local copies, waits for them, and re-layouts: 5.63 us -> 0.03 us
    ppermute x4 -> x0, waiting for transfers between devices: 4.69 us -> none  [body(): lax.ppermute(mixed, 'tensor', [(i, i ^ step) for i in range(count)])]
    ppermute x8 -> x14, starting transfers between devices: 11.9 us -> 16.3 us  [send(): return lax.ppermute(value, 'tensor', pairs)]
    ppermute x8 -> x14, waiting for transfers between devices: 5.12 us -> 7.13 us  [send(): return lax.ppermute(value, 'tensor', pairs)]
    concatenate x2 -> x0, local copies, waits for them, and re-layouts: 1.96 us -> none  [the longest x1 1.29 us: body(): gathered = jnp.concatenate([half, other], 0)]
  transfers between devices with their start and end apart: 12 -> 14, of which waited for: 6 -> 3; matrix products, arithmetic and copies ran while one was open for 29% -> 0% of each run, Pallas kernels for 0% -> 46%
where the time goes in v2:
time: 58.1 us; the launch traced here: 58 us
  Pallas kernels  34.3 us (59%)
  starting transfers between devices  16.3 us (28%)
  waiting for transfers between devices  7.13 us (12%)
    ppermute x14, starting transfers between devices, send(): return lax.ppermute(value, 'tensor', pairs)  16.3 us
    pallas_call x3, Pallas kernels, multiply(): pl.pallas_call(functools.partial(multiply_kernel, start, len(pieces), len...  13.6 us
    pallas_call x4, Pallas kernels, fetch(): pl.pallas_call(functools.partial(fetch_kernel, start, len(after)), out_sh...  12.7 us
    ppermute x14, waiting for transfers between devices, send(): return lax.ppermute(value, 'tensor', pairs)  7.13 us
    pallas_call x1, Pallas kernels, finish(): pl.pallas_call(functools.partial(finish_kernel, start, len(pieces), len(l...  6.66 us
    pallas_call x1, Pallas kernels, collect(): pl.pallas_call(functools.partial(collect_kernel, depth, width), out_shape...  1.19 us
  transfers between devices with their start and end apart: 14, of which 3 were waited for; matrix products, arithmetic and copies ran while one was open for 0% of the time, Pallas kernels for 46%

profile of v2, /device:TPU:0, one launch (start us, length us, event | category | flops | bytes accessed | tf_op | source)
XLA Modules:
  0.0 58.0 jit_solution(12984633255491316243)
XLA Ops:
  0.0 3.0 %collective-permute-start.4 = (bf16[8,8192]{1,0:T(8,128)(2,1)}, bf16[8,8192]{1,0:T(8,128)(2,1)S(1)}, u32[]{:S(2)}, u32[]{:S(2)}) collective-permute-start(bf16[8,8192]{1,0:T(8,128)(2,1)} %refs_0_.1), channel_id=1, source_target_pairs={{0,2},{1,3},{2,0},{3,1},{4,6},{5,7},{6,4},{7,5},{8,10},{9,11},{10,... | collective-permute-start | bytes 393224 | tf_op jit(solution)/shard_map/ppermute | solution.py:39
  3.0 1.6 %collective-permute-start = (bf16[8,8192]{1,0:T(8,128)(2,1)}, bf16[8,8192]{1,0:T(8,128)(2,1)S(1)}, u32[]{:S(2)}, u32[]{:S(2)}) collective-permute-start(bf16[8,8192]{1,0:T(8,128)(2,1)} %refs_0_.1), channel_id=1, source_target_pairs={{0,4},{1,5},{2,6},{3,7},{4,8},{5,9},{6,10},{7,11},{8,12},{9,13},{1... | collective-permute-start | bytes 393224 | tf_op jit(solution)/shard_map/ppermute | solution.py:39
  4.5 2.6 %collective-permute-start.1 = (bf16[8,8192]{1,0:T(8,128)(2,1)}, bf16[8,8192]{1,0:T(8,128)(2,1)S(1)}, u32[]{:S(2)}, u32[]{:S(2)}) collective-permute-start(bf16[8,8192]{1,0:T(8,128)(2,1)} %refs_0_.1), channel_id=1, source_target_pairs={{0,8},{1,9},{2,10},{3,11},{4,12},{5,13},{6,14},{7,15},{8,0},{9,1},... | collective-permute-start | bytes 393224 | tf_op jit(solution)/shard_map/ppermute | solution.py:39
  7.1 1.3 %collective-permute-start.2 = (bf16[8,8192]{1,0:T(8,128)(2,1)}, bf16[8,8192]{1,0:T(8,128)(2,1)S(1)}, u32[]{:S(2)}, u32[]{:S(2)}) collective-permute-start(bf16[8,8192]{1,0:T(8,128)(2,1)} %refs_0_.1), channel_id=1, source_target_pairs={{0,12},{1,13},{2,14},{3,15},{4,0},{5,1},{6,2},{7,3},{8,4},{9,5},{1... | collective-permute-start | bytes 393224 | tf_op jit(solution)/shard_map/ppermute | solution.py:39
  8.5 3.2 %fetch_0.1.refs_3_.refs_2_ = bf16[2048,1792]{1,0:T(8,128)(2,1)S(1)} custom-call(bf16[8192,1792]{1,0:T(8,128)(2,1)} %source.7), custom_call_target="tpu_custom_call" | custom-call | bytes 7340032 | tf_op jit(solution)/shard_map/fetch_0/pallas_call | solution.py:58
  11.7 3.2 %fetch_1.1.refs_4_.refs_3_ = bf16[2048,1792]{1,0:T(8,128)(2,1)S(1)} custom-call(bf16[8192,1792]{1,0:T(8,128)(2,1)} %source.7), custom_call_target="tpu_custom_call" | custom-call | bytes 7340032 | tf_op jit(solution)/shard_map/fetch_1/pallas_call | solution.py:58
  14.9 1.7 %collective-permute-done.1.refs_1_ = bf16[8,8192]{1,0:T(8,128)(2,1)S(1)} collective-permute-done((bf16[8,8192]{1,0:T(8,128)(2,1)}, bf16[8,8192]{1,0:T(8,128)(2,1)S(1)}, u32[]{:S(2)}, u32[]{:S(2)}) %collective-permute-start.1) | collective-permute-done | bytes 131104 | tf_op jit(solution)/shard_map/ppermute | solution.py:39
  16.7 0.6 collective-permute-start.5
  17.2 3.2 %fetch_2.1.refs_1_.refs_2_ = bf16[2048,1792]{1,0:T(8,128)(2,1)S(1)} custom-call(bf16[8192,1792]{1,0:T(8,128)(2,1)} %source.7, bf16[3,8,8192]{2,1,0:T(8,128)(2,1)S(1)} %pack.1.refs_0_.refs_1_), custom_call_target="tpu_custom_call" | custom-call | bytes 7340032 | tf_op jit(solution)/shard_map/fetch_2/pallas_call | solution.py:58
  20.4 3.2 %fetch_3.1.refs_2_.refs_3_ = bf16[2048,1792]{1,0:T(8,128)(2,1)S(1)} custom-call(bf16[8192,1792]{1,0:T(8,128)(2,1)} %source.7, bf16[3,8,8192]{2,1,0:T(8,128)(2,1)S(1)} %pack.1.refs_0_.refs_1_), custom_call_target="tpu_custom_call" | custom-call | bytes 7340032 | tf_op jit(solution)/shard_map/fetch_3/pallas_call | solution.py:58
  23.7 0.1 collective-permute-start.6
  23.8 4.0 %collective-permute-done.5.refs_0_ = bf16[3,8,8192]{2,1,0:T(8,128)(2,1)S(1)} collective-permute-done((bf16[3,8,8192]{2,1,0:T(8,128)(2,1)S(1)}, bf16[3,8,8192]{2,1,0:T(8,128)(2,1)S(1)}, u32[]{:S(2)}, u32[]{:S(2)}) %collective-permute-start.5) | collective-permute-done | bytes 393248 | tf_op jit(solution)/shard_map/ppermute | solution.py:39
  27.7 0.5 collective-permute-start.7
  28.2 1.4 %collective-permute-done.7.refs_6_ = bf16[8,8192]{1,0:T(8,128)(2,1)S(1)} collective-permute-done((bf16[8,8192]{1,0:T(8,128)(2,1)S(1)}, bf16[8,8192]{1,0:T(8,128)(2,1)S(1)}, u32[]{:S(2)}, u32[]{:S(2)}) %collective-permute-start.7) | collective-permute-done | bytes 131104 | tf_op jit(solution)/shard_map/ppermute | solution.py:39
  29.7 1.2 %collect.1 = (bf16[128,8192]{1,0:T(8,128)(2,1)S(1)}, bf16[128,64]{1,0:T(8,128)(2,1)S(1)}) custom-call(s32[1,16]{1,0:T(1,128)S(1)} %bitcast.9, s32[1,128]{1,0:T(1,128)S(1)} %bitcast.7, bf16[64,8192]{1,0:T(8,128)(2,1)S(1)} %bitcast.6, bf16[8,8192]{1,0:T(8,128)(2,1)S(1)} %copy-done.1, bf16[3,8,8192]{2,1,0:T(8,128)(2,1)S(1)} %pack.1.refs_0_.refs_1_, ...), custom_call_target="tpu_custom_call" | custom-call | flops 134217728 | bytes 1048576 | tf_op jit(solution)/shard_map/collect/pallas_call | solution.py:143
  30.9 0.2 collective-permute-start.9
  31.1 5.2 %gate_a.1 = (f32[128,1792]{1,0:T(8,128)S(1)}, bf16[2048,1792]{1,0:T(8,128)(2,1)S(1)}, bf16[2048,1792]{1,0:T(8,128)(2,1)S(1)}) custom-call(bf16[128,64]{1,0:T(8,128)(2,1)S(1)} %get-tuple-element.14.refs_0_, bf16[128,8192]{1,0:T(8,128)(2,1)S(1)} %get-tuple-element.13.refs_1_.tokens, bf16[2048,1792]{1,0:T(8,128)(2,1)S(1)} %fetch_0.1.refs_3_.refs_2_, ...), custom_call_target="tpu_custom_call" | custom-call | flops 1879048192 | bytes 16777216 | tf_op jit(solution)/shard_map/gate_a/pallas_call | solution.py:233
  36.3 0.6 %collective-permute-start.10 = (bf16[128,64]{1,0:T(8,128)(2,1)S(1)}, bf16[128,64]{1,0:T(8,128)(2,1)S(1)}, u32[]{:S(2)}, u32[]{:S(2)}) collective-permute-start(bf16[128,64]{1,0:T(8,128)(2,1)S(1)} %add.2.refs_0_), channel_id=1, source_target_pairs={{0,2},{1,3},{2,0},{3,1},{4,6},{5,7},{6,4},{7,5},{8,10},{9,11},{10,... | collective-permute-start | bytes 49160 | tf_op jit(solution)/shard_map/ppermute | solution.py:39
  36.9 5.2 %gate_b.1 = (f32[128,1792]{1,0:T(8,128)S(1)}, bf16[2048,1792]{1,0:T(8,128)(2,1)S(1)}, bf16[2048,1792]{1,0:T(8,128)(2,1)S(1)}) custom-call(bf16[128,64]{1,0:T(8,128)(2,1)S(1)} %add.2.refs_0_, bf16[128,8192]{1,0:T(8,128)(2,1)S(1)} %get-tuple-element.13.refs_1_.tokens, bf16[2048,1792]{1,0:T(8,128)(2,1)S(1)} %fetch_2.1.refs_1_.refs_2_, ...), custom_call_target="tpu_custom_call" | custom-call | flops 1879048192 | bytes 16777216 | tf_op jit(solution)/shard_map/gate_b/pallas_call | solution.py:233
  42.1 3.4 %collective-permute-start.11 = (bf16[128,64]{1,0:T(8,128)(2,1)S(1)}, bf16[128,64]{1,0:T(8,128)(2,1)S(1)}, u32[]{:S(2)}, u32[]{:S(2)}) collective-permute-start(bf16[128,64]{1,0:T(8,128)(2,1)S(1)} %add.3.refs_0_.refs_2_), channel_id=1, source_target_pairs={{0,4},{1,5},{2,6},{3,7},{4,8},{5,9},{6,10},{7,11},{8,12},{9,13},{1... | collective-permute-start | bytes 49160 | tf_op jit(solution)/shard_map/ppermute | solution.py:39
  45.5 1.3 %collective-permute-start.12 = (bf16[128,64]{1,0:T(8,128)(2,1)S(1)}, bf16[128,64]{1,0:T(8,128)(2,1)S(1)}, u32[]{:S(2)}, u32[]{:S(2)}) collective-permute-start(bf16[128,64]{1,0:T(8,128)(2,1)S(1)} %add.3.refs_0_.refs_2_), channel_id=1, source_target_pairs={{0,8},{1,9},{2,10},{3,11},{4,12},{5,13},{6,14},{7,15},{8,0},{9,1},... | collective-permute-start | bytes 49160 | tf_op jit(solution)/shard_map/ppermute | solution.py:39
  46.9 1.1 %collective-permute-start.13 = (bf16[128,64]{1,0:T(8,128)(2,1)S(1)}, bf16[128,64]{1,0:T(8,128)(2,1)S(1)}, u32[]{:S(2)}, u32[]{:S(2)}) collective-permute-start(bf16[128,64]{1,0:T(8,128)(2,1)S(1)} %add.3.refs_0_.refs_2_), channel_id=1, source_target_pairs={{0,12},{1,13},{2,14},{3,15},{4,0},{5,1},{6,2},{7,3},{8,4},{9,5},{1... | collective-permute-start | bytes 49160 | tf_op jit(solution)/shard_map/ppermute | solution.py:39
  48.0 3.3 %up_a.1.up_pre = f32[128,1792]{1,0:T(8,128)S(1)} custom-call(bf16[128,64]{1,0:T(8,128)(2,1)S(1)} %add.3.refs_0_.refs_2_, bf16[128,8192]{1,0:T(8,128)(2,1)S(1)} %get-tuple-element.13.refs_1_.tokens, bf16[2048,1792]{1,0:T(8,128)(2,1)S(1)} %get-tuple-element.17.refs_2_, bf16[2048,1792]{1,0:T(8,128)(2,1)S(1)} %get-tuple-element.18.refs_3_), custom_call_target="tpu_custom_call" | custom-call | flops 1879048192 | bytes 16777216 | tf_op jit(solution)/shard_map/up_a/pallas_call | solution.py:233
  51.3 6.7 %finish.1 = bf16[128,1792]{1,0:T(8,128)(2,1)} custom-call(s32[1,128]{1,0:T(1,128)S(1)} %bitcast.8, bf16[128,8192]{1,0:T(8,128)(2,1)S(1)} %get-tuple-element.13.refs_1_.tokens, bf16[1024,1792]{1,0:T(8,128)(2,1)} %bitcast.10, f32[128,1792]{1,0:T(8,128)S(1)} %get-tuple-element.16.gate_pre, f32[128,1792]{1,0:T(8,128)S(1)} %up_a.1.up_pre, ...), custom_call_target="tpu_custom_call" | custom-call | flops 1879048192 | bytes 4194304 | tf_op jit(solution)/shard_map/finish/pallas_call | solution.py:283
  (25 shorter events, 0.1 us)
Async XLA Ops:
  0.0 14.9 %collective-permute-start.4 = (bf16[8,8192]{1,0:T(8,128)(2,1)}, bf16[8,8192]{1,0:T(8,128)(2,1)S(1)}, u32[]{:S(2)}, u32[]{:S(2)}) collective-permute-start(bf16[8,8192]{1,0:T(8,128)(2,1)} %refs_0_.1), channel_id=1, source_target_pairs={{0,2},{1,3},{2,0},{3,1},{4,6},{5,7},{6,4},{7,5},{8,10},{9,11},{10,... | collective-permute-start | bytes 393224 | tf_op jit(solution)/shard_map/ppermute | solution.py:39
  3.0 11.9 %collective-permute-start.3 = (bf16[8,8192]{1,0:T(8,128)(2,1)}, bf16[8,8192]{1,0:T(8,128)(2,1)S(1)}, u32[]{:S(2)}, u32[]{:S(2)}) collective-permute-start(bf16[8,8192]{1,0:T(8,128)(2,1)} %refs_0_.1), channel_id=1, source_target_pairs={{0,1},{1,0},{2,3},{3,2},{4,5},{5,4},{6,7},{7,6},{8,9},{9,8},{10,11... | collective-permute-start | bytes 393224 | tf_op jit(solution)/shard_map/ppermute | solution.py:39
  3.0 11.9 %collective-permute-start = (bf16[8,8192]{1,0:T(8,128)(2,1)}, bf16[8,8192]{1,0:T(8,128)(2,1)S(1)}, u32[]{:S(2)}, u32[]{:S(2)}) collective-permute-start(bf16[8,8192]{1,0:T(8,128)(2,1)} %refs_0_.1), channel_id=1, source_target_pairs={{0,4},{1,5},{2,6},{3,7},{4,8},{5,9},{6,10},{7,11},{8,12},{9,13},{1... | collective-permute-start | bytes 393224 | tf_op jit(solution)/shard_map/ppermute | solution.py:39
  4.5 12.1 %collective-permute-start.1 = (bf16[8,8192]{1,0:T(8,128)(2,1)}, bf16[8,8192]{1,0:T(8,128)(2,1)S(1)}, u32[]{:S(2)}, u32[]{:S(2)}) collective-permute-start(bf16[8,8192]{1,0:T(8,128)(2,1)} %refs_0_.1), channel_id=1, source_target_pairs={{0,8},{1,9},{2,10},{3,11},{4,12},{5,13},{6,14},{7,15},{8,0},{9,1},... | collective-permute-start | bytes 393224 | tf_op jit(solution)/shard_map/ppermute | solution.py:39
  7.1 9.5 %collective-permute-start.2 = (bf16[8,8192]{1,0:T(8,128)(2,1)}, bf16[8,8192]{1,0:T(8,128)(2,1)S(1)}, u32[]{:S(2)}, u32[]{:S(2)}) collective-permute-start(bf16[8,8192]{1,0:T(8,128)(2,1)} %refs_0_.1), channel_id=1, source_target_pairs={{0,12},{1,13},{2,14},{3,15},{4,0},{5,1},{6,2},{7,3},{8,4},{9,5},{1... | collective-permute-start | bytes 393224 | tf_op jit(solution)/shard_map/ppermute | solution.py:39
  16.7 11.1 %collective-permute-start.5 = (bf16[3,8,8192]{2,1,0:T(8,128)(2,1)S(1)}, bf16[3,8,8192]{2,1,0:T(8,128)(2,1)S(1)}, u32[]{:S(2)}, u32[]{:S(2)}) collective-permute-start(bf16[3,8,8192]{2,1,0:T(8,128)(2,1)S(1)} %pack.1.refs_0_.refs_1_), channel_id=1, source_target_pairs={{0,2},{1,3},{2,0},{3,1},{4,6},{5,7},{6,4},{7,5},{8,10},{9,11},{10,... | collective-permute-start | bytes 1179656 | tf_op jit(solution)/shard_map/ppermute | solution.py:39
  23.6 6.0 %copy-start = (bf16[1,8192,64]{1,2,0:T(8,128)(2,1)S(1)}, bf16[1,8192,64]{1,2,0:T(8,128)(2,1)}, u32[]{:S(2)}) copy-start(bf16[1,8192,64]{1,2,0:T(8,128)(2,1)} %param.11) | copy-start | bytes 3145732
  23.6 6.0 %copy-start.1 = (bf16[8,8192]{1,0:T(8,128)(2,1)S(1)}, bf16[8,8192]{1,0:T(8,128)(2,1)}, u32[]{:S(2)}) copy-start(bf16[8,8192]{1,0:T(8,128)(2,1)} %refs_0_.1) | copy-start | bytes 393220
  23.7 6.0 %copy-start.2 = (s32[128]{0:T(128)S(1)}, s32[128]{0:T(128)}, u32[]{:S(2)}) copy-start(s32[128]{0:T(128)} %param.13) | copy-start | bytes 1540
  23.7 6.0 %copy-start.3 = (s32[16]{0:T(128)S(1)}, s32[16]{0:T(128)}, u32[]{:S(2)}) copy-start(s32[16]{0:T(128)} %param.14) | copy-start | bytes 196
  23.7 6.0 %collective-permute-start.6 = (bf16[3,8,8192]{2,1,0:T(8,128)(2,1)S(1)}, bf16[3,8,8192]{2,1,0:T(8,128)(2,1)S(1)}, u32[]{:S(2)}, u32[]{:S(2)}) collective-permute-start(bf16[3,8,8192]{2,1,0:T(8,128)(2,1)S(1)} %pack.1.refs_0_.refs_1_), channel_id=1, source_target_pairs={{0,1},{1,0},{2,3},{3,2},{4,5},{5,4},{6,7},{7,6},{8,9},{9,8},{10,11... | collective-permute-start | bytes 1179656 | tf_op jit(solution)/shard_map/ppermute | solution.py:39
  27.7 1.9 %collective-permute-start.8 = (bf16[3,8,8192]{2,1,0:T(8,128)(2,1)S(1)}, bf16[3,8,8192]{2,1,0:T(8,128)(2,1)S(1)}, u32[]{:S(2)}, u32[]{:S(2)}) collective-permute-start(bf16[3,8,8192]{2,1,0:T(8,128)(2,1)S(1)} %tie.1.refs_3_), channel_id=1, source_target_pairs={{0,1},{1,0},{2,3},{3,2},{4,5},{5,4},{6,7},{7,6},{8,9},{9,8},{10,11... | collective-permute-start | bytes 1179656 | tf_op jit(solution)/shard_map/ppermute | solution.py:39
  27.7 1.9 %collective-permute-start.7 = (bf16[8,8192]{1,0:T(8,128)(2,1)S(1)}, bf16[8,8192]{1,0:T(8,128)(2,1)S(1)}, u32[]{:S(2)}, u32[]{:S(2)}) collective-permute-start(bf16[8,8192]{1,0:T(8,128)(2,1)S(1)} %collective-permute-done.4.refs_6_.refs_2_), channel_id=1, source_target_pairs={{0,1},{1,0},{2,3},{3,2},{4,5},{5,4},{6,7},{7,6},{8,9},{9,8},{10,11... | collective-permute-start | bytes 393224 | tf_op jit(solution)/shard_map/ppermute | solution.py:39
  30.9 5.4 %collective-permute-start.9 = (bf16[128,64]{1,0:T(8,128)(2,1)S(1)}, bf16[128,64]{1,0:T(8,128)(2,1)S(1)}, u32[]{:S(2)}, u32[]{:S(2)}) collective-permute-start(bf16[128,64]{1,0:T(8,128)(2,1)S(1)} %get-tuple-element.14.refs_0_), channel_id=1, source_target_pairs={{0,1},{1,0},{2,3},{3,2},{4,5},{5,4},{6,7},{7,6},{8,9},{9,8},{10,11... | collective-permute-start | bytes 49160 | tf_op jit(solution)/shard_map/ppermute | solution.py:39
  36.3 5.8 %collective-permute-start.10 = (bf16[128,64]{1,0:T(8,128)(2,1)S(1)}, bf16[128,64]{1,0:T(8,128)(2,1)S(1)}, u32[]{:S(2)}, u32[]{:S(2)}) collective-permute-start(bf16[128,64]{1,0:T(8,128)(2,1)S(1)} %add.2.refs_0_), channel_id=1, source_target_pairs={{0,2},{1,3},{2,0},{3,1},{4,6},{5,7},{6,4},{7,5},{8,10},{9,11},{10,... | collective-permute-start | bytes 49160 | tf_op jit(solution)/shard_map/ppermute | solution.py:39
  42.1 9.1 %collective-permute-start.11 = (bf16[128,64]{1,0:T(8,128)(2,1)S(1)}, bf16[128,64]{1,0:T(8,128)(2,1)S(1)}, u32[]{:S(2)}, u32[]{:S(2)}) collective-permute-start(bf16[128,64]{1,0:T(8,128)(2,1)S(1)} %add.3.refs_0_.refs_2_), channel_id=1, source_target_pairs={{0,4},{1,5},{2,6},{3,7},{4,8},{5,9},{6,10},{7,11},{8,12},{9,13},{1... | collective-permute-start | bytes 49160 | tf_op jit(solution)/shard_map/ppermute | solution.py:39
  45.5 5.7 %collective-permute-start.12 = (bf16[128,64]{1,0:T(8,128)(2,1)S(1)}, bf16[128,64]{1,0:T(8,128)(2,1)S(1)}, u32[]{:S(2)}, u32[]{:S(2)}) collective-permute-start(bf16[128,64]{1,0:T(8,128)(2,1)S(1)} %add.3.refs_0_.refs_2_), channel_id=1, source_target_pairs={{0,8},{1,9},{2,10},{3,11},{4,12},{5,13},{6,14},{7,15},{8,0},{9,1},... | collective-permute-start | bytes 49160 | tf_op jit(solution)/shard_map/ppermute | solution.py:39
  46.9 4.4 %collective-permute-start.13 = (bf16[128,64]{1,0:T(8,128)(2,1)S(1)}, bf16[128,64]{1,0:T(8,128)(2,1)S(1)}, u32[]{:S(2)}, u32[]{:S(2)}) collective-permute-start(bf16[128,64]{1,0:T(8,128)(2,1)S(1)} %add.3.refs_0_.refs_2_), channel_id=1, source_target_pairs={{0,12},{1,13},{2,14},{3,15},{4,0},{5,1},{6,2},{7,3},{8,4},{9,5},{1... | collective-permute-start | bytes 49160 | tf_op jit(solution)/shard_map/ppermute | solution.py:39

commit v3 on v2

--- a/solution.py
+++ b/solution.py
@@ -36,6 +36,11 @@
     for i in range(count):
         a, b, c = i // (2 * width), i // 2 % width, i % 2
         pairs.append((i, ((a + da) % depth * width + (b + db) % width) * 2 + (c + dc) % 2))
+    return lax.ppermute(value, "tensor", pairs)
+
+
+def swap(value, mask):
+    pairs = [(i, i ^ mask) for i in range(lax.axis_size("tensor"))]
     return lax.ppermute(value, "tensor", pairs)
 
 
@@ -75,16 +80,19 @@
 
 
 def pack_kernel(n, *refs):
-    for i in range(n):
-        refs[-1][i] = refs[i][...]
+    place = 0
+    for ref in refs[:n]:
+        for i in range(ref.shape[0]):
+            refs[-1][place] = ref[i]
+            place += 1
 
 
 def pack(blocks, after):
-    rows, model = blocks[0].shape
+    rows, model = blocks[0].shape[1:]
     n = len(blocks)
     return pl.pallas_call(
         functools.partial(pack_kernel, n),
-        out_shape=pltpu.VMEM((n, rows, model), jnp.bfloat16),
+        out_shape=pltpu.VMEM((sum(b.shape[0] for b in blocks), rows, model), jnp.bfloat16),
         in_specs=[NEAR] * n + [FAR] * len(after),
         out_specs=NEAR,
         cost_estimate=pl.CostEstimate(flops=0, bytes_accessed=1 << 18, transcendentals=0),
@@ -110,24 +118,23 @@
     )(value, *after)
 
 
-def collect_kernel(depth, width, placement, index, down, *refs):
-    blocks = 2 * width
-    mine, theirs = refs[:blocks], refs[blocks : 2 * blocks]
-    packed, low = refs[2 * blocks :]
+def collect_kernel(depth, width, sizes, placement, index, down, *refs):
+    mine, theirs = refs[: len(sizes)], refs[len(sizes) : 2 * len(sizes)]
+    packed, low = refs[2 * len(sizes) :]
     own = lax.axis_index("tensor")
-    a, b, c = own // (2 * width), own // 2 % width, own % 2
-    rows = mine[0].shape[0]
-    for k in range(width):
-        for j in range(depth):
-            chip = lax.rem(a - j + depth, depth) * width + lax.rem(b - k + width, width)
-            if j == 0:
-                p, q = mine[2 * k][...], theirs[2 * k][...]
-            else:
-                p, q = mine[2 * k + 1][j - 1], theirs[2 * k + 1][j - 1]
+    c = own % 2
+    rows = packed.shape[0] // (2 * depth * width)
+    place = 0
+    for size, p_ref, q_ref in zip(sizes, mine, theirs):
+        for i in range(size):
+            j, k = place % depth, place // depth
+            chip = (own // 2) ^ (j * width + k)
+            p, q = p_ref[i], q_ref[i]
             first, second = jnp.where(c == 0, p, q), jnp.where(c == 0, q, p)
             packed[pl.ds(pl.multiple_of(chip * 2 * rows, 2 * rows), 2 * rows), :] = (
                 jnp.concatenate([first, second], 0)
             )
+            place += 1
     full = lax.dot_general(
         packed[...], down[...], (((1,), (1,)), ((), ())), preferred_element_type=jnp.float32
     )
@@ -138,15 +145,16 @@
 
 
 def collect(placement, index, down, mine, theirs, depth, width):
-    rows, model = mine[0].shape
+    sizes = [v.shape[0] for v in mine]
+    rows, model = mine[0].shape[1:]
     requests = 2 * depth * width * rows
     return pl.pallas_call(
-        functools.partial(collect_kernel, depth, width),
+        functools.partial(collect_kernel, depth, width, sizes),
         out_shape=[
             pltpu.VMEM((requests, model), jnp.bfloat16),
             jax.ShapeDtypeStruct((requests, down.shape[0]), jnp.bfloat16),
         ],
-        in_specs=[NEAR] * (3 + 4 * width),
+        in_specs=[NEAR] * (3 + 2 * len(sizes)),
         out_specs=[NEAR] * 2,
         cost_estimate=pl.CostEstimate(
             flops=2 * requests * model * 64, bytes_accessed=1 << 20, transcendentals=0
@@ -193,14 +201,11 @@
     before, refs = refs[:begun], refs[begun:]
     copies = []
     if fetched:
-        source, out, *targets, sems = refs
-        first = fetched[0]
-        for i, target in enumerate(targets):
-            rows = target.shape[0]
+        sources, (out, *targets, sems) = refs[: len(fetched)], refs[len(fetched) :]
+        for i, ((first, rows), source, target) in enumerate(zip(fetched, sources, targets)):
             copies.append(
                 pltpu.make_async_copy(source.at[pl.ds(first, rows)], target, sems.at[i])
             )
-            first += rows
     else:
         (out,) = refs
     for copy in copies:
@@ -218,24 +223,26 @@
         copy.wait()
 
 
-def multiply(after, tokens, pieces, start, begun, source, fetched, name):
+def multiply(after, tokens, pieces, start, begun, fetched, name):
     requests = tokens.shape[0]
     hidden = pieces[0].shape[1]
     out_shape = [pltpu.VMEM((requests, hidden), jnp.float32)]
+    out_shape += [pltpu.VMEM((rows, hidden), source.dtype) for source, first, rows in fetched]
     operands = [after, near(tokens)] + [near(p) for p in pieces] + [near(b) for b in begun]
-    in_specs = [FAR] + [NEAR] * (len(operands) - 1)
-    scratch = []
-    if fetched:
-        operands.append(far(source))
-        in_specs.append(STORED)
-        out_shape += [pltpu.VMEM((r, hidden), source.dtype) for r in fetched[1:]]
-        scratch = [pltpu.SemaphoreType.DMA((len(fetched) - 1,))]
-    return pl.pallas_call(
-        functools.partial(multiply_kernel, start, len(pieces), len(begun), fetched),
+    in_specs = [FAR] + [NEAR] * (len(operands) - 1) + [STORED] * len(fetched)
+    operands += [far(source) for source, first, rows in fetched]
+    return pl.pallas_call(
+        functools.partial(
+            multiply_kernel,
+            start,
+            len(pieces),
+            len(begun),
+            [(first, rows) for source, first, rows in fetched],
+        ),
         out_shape=out_shape,
         in_specs=in_specs,
         out_specs=[NEAR] * len(out_shape),
-        scratch_shapes=scratch,
+        scratch_shapes=[pltpu.SemaphoreType.DMA((len(fetched),))] if fetched else [],
         cost_estimate=pl.CostEstimate(
             flops=2 * requests * sum(p.shape[0] for p in pieces) * hidden,
             bytes_accessed=16 << 20,
@@ -249,10 +256,8 @@
 def finish_kernel(start, n, m, index, tokens, adapter_up, gate_pre, up_pre, *refs):
     pieces, refs = refs[:n], refs[n:]
     lows, refs = refs[:m], refs[m:]
-    out, near_up, expanded, sem = refs
+    out, expanded = refs
     rank = lows[0].shape[1]
-    copy = pltpu.make_async_copy(adapter_up, near_up, sem)
-    copy.start()
     mixed = lows[0][...]
     for low in lows[1:]:
         mixed = mixed + low[...]
@@ -266,13 +271,12 @@
         expanded[:, i * TILE : (i + 1) * TILE] = jnp.where(
             relative == i * group, wide, 0.0
         ).astype(jnp.bfloat16)
-    copy.wait()
 
     @pl.loop(0, out.shape[1] // TILE)
     def _(i):
         here = pl.ds(pl.multiple_of(i * TILE, TILE), TILE)
         up = up_pre[:, here] + piecewise(tokens, pieces, start, here)
-        up = up + jnp.dot(expanded[...], near_up[:, here], preferred_element_type=jnp.float32)
+        up = up + jnp.dot(expanded[...], adapter_up[:, here], preferred_element_type=jnp.float32)
         gate = gate_pre[:, here]
         out[:, here] = (gate / (1.0 + jnp.exp(-gate)) * up).astype(out.dtype)
 
@@ -283,24 +287,22 @@
     return pl.pallas_call(
         functools.partial(finish_kernel, start, len(pieces), len(lows)),
         out_shape=jax.ShapeDtypeStruct((requests, hidden), jnp.bfloat16),
-        in_specs=[NEAR, NEAR, STORED] + [NEAR] * (len(pieces) + len(lows) + 2),
+        in_specs=[NEAR] * (5 + len(pieces) + len(lows)),
         out_specs=NEAR,
         scratch_shapes=[
-            pltpu.VMEM(adapter_up.shape, jnp.bfloat16),
             pltpu.VMEM((requests, adapter_up.shape[0]), jnp.bfloat16),
-            pltpu.SemaphoreType.DMA,
         ],
         cost_estimate=pl.CostEstimate(
             flops=2 * requests * sum(p.shape[0] for p in pieces) * hidden,
             bytes_accessed=4 << 20,
             transcendentals=requests * hidden,
         ),
-        compiler_params=pltpu.CompilerParams(vmem_limit_bytes=8 << 20),
+        compiler_params=pltpu.CompilerParams(vmem_limit_bytes=4 << 20),
         name="finish",
     )(
         index,
         near(tokens),
-        far(adapter_up),
+        near(adapter_up),
         near(gate_pre),
         near(up_pre),
         *[near(p) for p in pieces],
@@ -309,54 +311,71 @@
 
 
 def on_chip(tokens, gate_weight, up_weight, down, up, request_adapter_index, placement):
-    count = lax.axis_size("tensor")
-    depth, width = plan(count)
+    depth, width = plan(lax.axis_size("tensor"))
     model, hidden = gate_weight.shape
     index = request_adapter_index[None, :]
     part = model // PIECES
-
-    by_line = [send(tokens, j, 0, 0) for j in range(1, depth)]
-    across_own = [send(tokens, 0, k, 0) for k in range(1, width)]
-    core_own = send(tokens, 0, 0, 1)
+    up = up.reshape(-1, hidden)
+    own = tokens[None]
+    core, column, line_1, line_2 = 1, 2, 2 * width, 4 * width
+
+    block_2 = swap(own, line_2)
+    block_1 = swap(own, line_1)
+    column_0 = swap(own, column)
     gate_0 = fetch(gate_weight, 0, part, "fetch_0")
-    gate_1 = fetch(gate_weight, part, part, "fetch_1")
-    line = pack(by_line, [gate_0, gate_1, core_own, *across_own])
-    across_line = [send(line, 0, k, 0) for k in range(1, width)]
-    core_line = send(line, 0, 0, 1)
-    core_across_own = [send(v, 0, 0, 1) for v in across_own]
+    block_2 = tie(block_2, [gate_0])
+    block_3 = swap(block_2, line_1)
+    blocks_12 = pack([block_1, block_2], [gate_0, column_0])
+    columns_12 = swap(blocks_12, column)
+    gate_1 = fetch(gate_weight, part, part, "fetch_1", [blocks_12])
+    block_3 = tie(block_3, [gate_1])
+    column_3 = swap(block_3, column)
+    line = pack([own, blocks_12, block_3], [])
+    core_line = swap(line, core)
     gate_2 = fetch(gate_weight, 2 * part, part, "fetch_2", [line])
-    gate_3 = fetch(gate_weight, 3 * part, part, "fetch_3", [line])
-    across_line = [tie(v, [gate_2, gate_3]) for v in across_line]
-    core_across_line = [send(v, 0, 0, 1) for v in across_line]
-    mine, theirs = [tokens, line], [core_own, core_line]
-    for own_block, line_block in zip(across_own, across_line):
-        mine += [own_block, line_block]
-    for own_block, line_block in zip(core_across_own, core_across_line):
-        theirs += [own_block, line_block]
+    columns = pack([column_0, columns_12, column_3], [gate_2])
+    core_columns = swap(columns, core)
     packed, low = collect(
-        placement[None, :], index, jnp.swapaxes(down[0], 0, 1), mine, theirs, depth, width
-    )
-
-    low_1 = add(low, send(low, 0, 0, 1))
-    gate_pre, up_0, up_1 = multiply(
-        low, packed, [gate_0, gate_1], 0, [], up_weight, (0, part, part), "gate_a"
-    )
-    low_2 = add(low_1, *[send(low_1, 0, k, 0) for k in range(1, width)])
-    gate_pre, up_2, up_3 = multiply(
+        placement[None, :],
+        index,
+        jnp.swapaxes(down[0], 0, 1),
+        [line, columns],
+        [core_line, core_columns],
+        depth,
+        width,
+    )
+
+    low_1 = add(low, swap(low, line_2))
+    gate_pre, gate_3, up_0 = multiply(
+        low,
+        packed,
+        [gate_0, gate_1],
+        0,
+        [],
+        [(gate_weight, 3 * part, part), (up_weight, 0, part)],
+        "gate_a",
+    )
+    low_2 = add(low_1, swap(low_1, line_1))
+    gate_pre, up_1, up_2 = multiply(
         low_1,
         packed,
         [gate_2, gate_3],
         2 * part,
         [gate_pre],
-        up_weight,
-        (2 * part, part, part),
+        [(up_weight, part, part), (up_weight, 2 * part, part)],
         "gate_b",
     )
-    lows = [low_2] + [send(low_2, j, 0, 0) for j in range(1, depth)]
-    (up_pre,) = multiply(low_2, packed, [up_0, up_1], 0, [], None, (), "up_a")
-    return finish(
-        index, packed, up.reshape(-1, hidden), gate_pre, up_pre, [up_2, up_3], 2 * part, lows
-    )
+    lows = [low_2] + [swap(low_2, mask) for mask in (core, column, core + column)]
+    up_pre, near_up, up_3 = multiply(
+        low_2,
+        packed,
+        [up_0, up_1],
+        0,
+        [],
+        [(up, 0, up.shape[0]), (up_weight, 3 * part, part)],
+        "up_a",
+    )
+    return finish(index, packed, near_up, gate_pre, up_pre, [up_2, up_3], 2 * part, lows)
 
 
 def streamed(
@@ -430,7 +449,8 @@
     adapter_request_lists,
     placement,
 ):
-    if request_adapter_index.shape[0] <= 128:
+    count = lax.axis_size("tensor")
+    if plan(count) == (4, 2) and tokens.shape[0] == 8:
         return on_chip(
             tokens,
             gate_weight,

time: 58.1 us -> 50.8 us (0.87)
  Pallas kernels: 34.3 us -> 30.2 us
  waiting for transfers between devices: 7.13 us -> 4.34 us
    pallas_call x4 -> x3, Pallas kernels: 12.7 us -> 9.56 us  [fetch(): pl.pallas_call(functools.partial(fetch_kernel, start, len(after)), out_sh...]
    ppermute x14 -> x13, waiting for transfers between devices: 7.13 us -> 4.34 us  [swap(): return lax.ppermute(value, 'tensor', pairs)]
    pallas_call x1, Pallas kernels: 6.66 us -> 4.76 us  [finish(): pl.pallas_call(functools.partial(finish_kernel, start, len(pieces), len(l...]
    pallas_call x3, Pallas kernels: 13.6 us -> 14.6 us  [multiply(): pl.pallas_call(functools.partial(multiply_kernel, start, len(pieces), len...]
    ppermute x14 -> x13, starting transfers between devices: 16.3 us -> 15.8 us  [swap(): return lax.ppermute(value, 'tensor', pairs)]
    pallas_call x2 -> x4, Pallas kernels: 1.22 us -> 1.28 us  [the longest x1 1.2 us: collect(): pl.pallas_call(functools.partial(collect_kernel, depth, width, sizes), ou...]
  transfers between devices with their start and end apart: 14 -> 13, of which waited for: 3 -> 5; matrix products, arithmetic and copies ran while one was open for 0% -> 0% of each run, Pallas kernels for 46% -> 48%
where the time goes in v3:
time: 50.8 us; the launch traced here: 50.6 us
  Pallas kernels  30.2 us (59%)
  starting transfers between devices  15.8 us (31%)
  waiting for transfers between devices  4.34 us (9%)
    ppermute x13, starting transfers between devices, swap(): return lax.ppermute(value, 'tensor', pairs)  15.8 us
    pallas_call x3, Pallas kernels, multiply(): pl.pallas_call(functools.partial(multiply_kernel, start, len(pieces), len...  14.6 us
    pallas_call x3, Pallas kernels, fetch(): pl.pallas_call(functools.partial(fetch_kernel, start, len(after)), out_sh...  9.56 us
    pallas_call x1, Pallas kernels, finish(): pl.pallas_call(functools.partial(finish_kernel, start, len(pieces), len(l...  4.76 us
    ppermute x13, waiting for transfers between devices, swap(): return lax.ppermute(value, 'tensor', pairs)  4.34 us
    pallas_call x1, Pallas kernels, collect(): pl.pallas_call(functools.partial(collect_kernel, depth, width, sizes), ou...  1.2 us
  transfers between devices with their start and end apart: 13, of which 5 were waited for; matrix products, arithmetic and copies ran while one was open for 0% of the time, Pallas kernels for 48%

profile of v3, /device:TPU:0, one launch (start us, length us, event | category | flops | bytes accessed | tf_op | source)
XLA Modules:
  0.0 50.6 jit_solution(17379896056589562994)
XLA Ops:
  0.0 4.0 %collective-permute-start.1 = (bf16[1,8,8192]{2,1,0:T(8,128)(2,1)}, bf16[1,8,8192]{2,1,0:T(8,128)(2,1)S(1)}, u32[]{:S(2)}, u32[]{:S(2)}) collective-permute-start(bf16[1,8,8192]{2,1,0:T(8,128)(2,1)} %bitcast.8), channel_id=1, source_target_pairs={{0,8},{1,9},{2,10},{3,11},{4,12},{5,13},{6,14},{7,15},{8,0},{9,1},... | collective-permute-start | bytes 393224 | tf_op jit(solution)/shard_map/ppermute | solution.py:44
  4.0 1.5 %collective-permute-start.2 = (bf16[1,8,8192]{2,1,0:T(8,128)(2,1)}, bf16[1,8,8192]{2,1,0:T(8,128)(2,1)S(1)}, u32[]{:S(2)}, u32[]{:S(2)}) collective-permute-start(bf16[1,8,8192]{2,1,0:T(8,128)(2,1)} %bitcast.9), channel_id=1, source_target_pairs={{0,2},{1,3},{2,0},{3,1},{4,6},{5,7},{6,4},{7,5},{8,10},{9,11},{10,... | collective-permute-start | bytes 393224 | tf_op jit(solution)/shard_map/ppermute | solution.py:44
  5.6 1.6 %collective-permute-start = (bf16[1,8,8192]{2,1,0:T(8,128)(2,1)}, bf16[1,8,8192]{2,1,0:T(8,128)(2,1)S(1)}, u32[]{:S(2)}, u32[]{:S(2)}) collective-permute-start(bf16[1,8,8192]{2,1,0:T(8,128)(2,1)} %bitcast.10), channel_id=1, source_target_pairs={{0,4},{1,5},{2,6},{3,7},{4,0},{5,1},{6,2},{7,3},{8,12},{9,13},{10,... | collective-permute-start | bytes 393224 | tf_op jit(solution)/shard_map/ppermute | solution.py:44
  7.1 3.2 %fetch_0.1.refs_1_.refs_2_ = bf16[2048,1792]{1,0:T(8,128)(2,1)S(1)} custom-call(bf16[8192,1792]{1,0:T(8,128)(2,1)} %refs_4_.1), custom_call_target="tpu_custom_call" | custom-call | bytes 7340032 | tf_op jit(solution)/shard_map/fetch_0/pallas_call | solution.py:63
  10.3 0.3 collective-permute-done.1.refs_0_
  10.7 0.8 %collective-permute-start.3 = (bf16[1,8,8192]{2,1,0:T(8,128)(2,1)S(1)}, bf16[1,8,8192]{2,1,0:T(8,128)(2,1)S(1)}, u32[]{:S(2)}, u32[]{:S(2)}) collective-permute-start(bf16[1,8,8192]{2,1,0:T(8,128)(2,1)S(1)} %tie.2.refs_1_), channel_id=1, source_target_pairs={{0,4},{1,5},{2,6},{3,7},{4,0},{5,1},{6,2},{7,3},{8,12},{9,13},{10,... | collective-permute-start | bytes 393224 | tf_op jit(solution)/shard_map/ppermute | solution.py:44
  11.4 0.7 %collective-permute-done.refs_0_ = bf16[1,8,8192]{2,1,0:T(8,128)(2,1)S(1)} collective-permute-done((bf16[1,8,8192]{2,1,0:T(8,128)(2,1)}, bf16[1,8,8192]{2,1,0:T(8,128)(2,1)S(1)}, u32[]{:S(2)}, u32[]{:S(2)}) %collective-permute-start) | collective-permute-done | bytes 131104 | tf_op jit(solution)/shard_map/ppermute | solution.py:44
  12.1 0.9 %collective-permute-start.4 = (bf16[2,8,8192]{2,1,0:T(8,128)(2,1)S(1)}, bf16[2,8,8192]{2,1,0:T(8,128)(2,1)S(1)}, u32[]{:S(2)}, u32[]{:S(2)}) collective-permute-start(bf16[2,8,8192]{2,1,0:T(8,128)(2,1)S(1)} %pack.3.refs_0_.refs_1_), channel_id=1, source_target_pairs={{0,2},{1,3},{2,0},{3,1},{4,6},{5,7},{6,4},{7,5},{8,10},{9,11},{10,... | collective-permute-start | bytes 786440 | tf_op jit(solution)/shard_map/ppermute | solution.py:44
  13.0 3.2 %fetch_1.1.refs_1_.refs_3_ = bf16[2048,1792]{1,0:T(8,128)(2,1)S(1)} custom-call(bf16[8192,1792]{1,0:T(8,128)(2,1)} %refs_4_.1, bf16[2,8,8192]{2,1,0:T(8,128)(2,1)S(1)} %pack.3.refs_0_.refs_1_), custom_call_target="tpu_custom_call" | custom-call | bytes 7340032 | tf_op jit(solution)/shard_map/fetch_1/pallas_call | solution.py:63
  16.2 1.3 %collective-permute-start.5 = (bf16[1,8,8192]{2,1,0:T(8,128)(2,1)S(1)}, bf16[1,8,8192]{2,1,0:T(8,128)(2,1)S(1)}, u32[]{:S(2)}, u32[]{:S(2)}) collective-permute-start(bf16[1,8,8192]{2,1,0:T(8,128)(2,1)S(1)} %tie.3.refs_2_), channel_id=1, source_target_pairs={{0,2},{1,3},{2,0},{3,1},{4,6},{5,7},{6,4},{7,5},{8,10},{9,11},{10,... | collective-permute-start | bytes 393224 | tf_op jit(solution)/shard_map/ppermute | solution.py:44
  17.5 3.2 %fetch_2.1.refs_3_.refs_2_ = bf16[2048,1792]{1,0:T(8,128)(2,1)S(1)} custom-call(bf16[8192,1792]{1,0:T(8,128)(2,1)} %refs_4_.1, bf16[4,8,8192]{2,1,0:T(8,128)(2,1)S(1)} %pack.4.refs_0_), custom_call_target="tpu_custom_call" | custom-call | bytes 7340032 | tf_op jit(solution)/shard_map/fetch_2/pallas_call | solution.py:63
  20.8 0.1 collective-permute-start.6
  20.8 1.4 %collective-permute-done.5.refs_2_ = bf16[1,8,8192]{2,1,0:T(8,128)(2,1)S(1)} collective-permute-done((bf16[1,8,8192]{2,1,0:T(8,128)(2,1)S(1)}, bf16[1,8,8192]{2,1,0:T(8,128)(2,1)S(1)}, u32[]{:S(2)}, u32[]{:S(2)}) %collective-permute-start.5) | collective-permute-done | bytes 131104 | tf_op jit(solution)/shard_map/ppermute | solution.py:44
  22.4 0.3 collective-permute-done.6.refs_2_
  22.7 1.6 %collective-permute-done.7.refs_3_ = bf16[4,8,8192]{2,1,0:T(8,128)(2,1)S(1)} collective-permute-done((bf16[4,8,8192]{2,1,0:T(8,128)(2,1)S(1)}, bf16[4,8,8192]{2,1,0:T(8,128)(2,1)S(1)}, u32[]{:S(2)}, u32[]{:S(2)}) %collective-permute-start.7) | collective-permute-done | bytes 524320 | tf_op jit(solution)/shard_map/ppermute | solution.py:44
  24.3 1.2 %collect.1 = (bf16[128,8192]{1,0:T(8,128)(2,1)S(1)}, bf16[128,64]{1,0:T(8,128)(2,1)S(1)}) custom-call(s32[1,16]{1,0:T(1,128)S(1)} %bitcast.14, s32[1,128]{1,0:T(1,128)S(1)} %bitcast.12, bf16[64,8192]{1,0:T(8,128)(2,1)S(1)} %bitcast.7, bf16[4,8,8192]{2,1,0:T(8,128)(2,1)S(1)} %pack.4.refs_0_, bf16[4,8,8192]{2,1,0:T(8,128)(2,1)S(1)} %pack.5.refs_1_, ...), custom_call_target="tpu_custom_call" | custom-call | flops 134217728 | bytes 1048576 | tf_op jit(solution)/shard_map/collect/pallas_call | solution.py:151
  25.5 3.3 %collective-permute-start.8 = (bf16[128,64]{1,0:T(8,128)(2,1)S(1)}, bf16[128,64]{1,0:T(8,128)(2,1)S(1)}, u32[]{:S(2)}, u32[]{:S(2)}) collective-permute-start(bf16[128,64]{1,0:T(8,128)(2,1)S(1)} %get-tuple-element.17.refs_0_), channel_id=1, source_target_pairs={{0,8},{1,9},{2,10},{3,11},{4,12},{5,13},{6,14},{7,15},{8,0},{9,1},... | collective-permute-start | bytes 49160 | tf_op jit(solution)/shard_map/ppermute | solution.py:44
  28.9 5.2 %gate_a.1 = (f32[128,1792]{1,0:T(8,128)S(1)}, bf16[2048,1792]{1,0:T(8,128)(2,1)S(1)}, bf16[2048,1792]{1,0:T(8,128)(2,1)S(1)}) custom-call(bf16[128,64]{1,0:T(8,128)(2,1)S(1)} %get-tuple-element.17.refs_0_, bf16[128,8192]{1,0:T(8,128)(2,1)S(1)} %get-tuple-element.16.refs_1_.tokens, bf16[2048,1792]{1,0:T(8,128)(2,1)S(1)} %fetch_0.1.refs_1_.refs_2_, ...), custom_call_target="tpu_custom_call" | custom-call | flops 1879048192 | bytes 16777216 | tf_op jit(solution)/shard_map/gate_a/pallas_call | solution.py:234
  34.1 0.4 collective-permute-start.9
  34.4 5.2 %gate_b.1 = (f32[128,1792]{1,0:T(8,128)S(1)}, bf16[2048,1792]{1,0:T(8,128)(2,1)S(1)}, bf16[2048,1792]{1,0:T(8,128)(2,1)S(1)}) custom-call(bf16[128,64]{1,0:T(8,128)(2,1)S(1)} %add.2.refs_0_, bf16[128,8192]{1,0:T(8,128)(2,1)S(1)} %get-tuple-element.16.refs_1_.tokens, bf16[2048,1792]{1,0:T(8,128)(2,1)S(1)} %fetch_2.1.refs_3_.refs_2_, ...), custom_call_target="tpu_custom_call" | custom-call | flops 1879048192 | bytes 16777216 | tf_op jit(solution)/shard_map/gate_b/pallas_call | solution.py:234
  39.7 1.5 %collective-permute-start.11 = (bf16[128,64]{1,0:T(8,128)(2,1)S(1)}, bf16[128,64]{1,0:T(8,128)(2,1)S(1)}, u32[]{:S(2)}, u32[]{:S(2)}) collective-permute-start(bf16[128,64]{1,0:T(8,128)(2,1)S(1)} %add.3.refs_0_.refs_2_), channel_id=1, source_target_pairs={{0,2},{1,3},{2,0},{3,1},{4,6},{5,7},{6,4},{7,5},{8,10},{9,11},{10,... | collective-permute-start | bytes 49160 | tf_op jit(solution)/shard_map/ppermute | solution.py:44
  41.3 0.3 collective-permute-start.12
  41.6 4.2 %up_a.1 = (f32[128,1792]{1,0:T(8,128)S(1)}, bf16[1024,1792]{1,0:T(8,128)(2,1)S(1)}, bf16[2048,1792]{1,0:T(8,128)(2,1)S(1)}) custom-call(bf16[128,64]{1,0:T(8,128)(2,1)S(1)} %add.3.refs_0_.refs_2_, bf16[128,8192]{1,0:T(8,128)(2,1)S(1)} %get-tuple-element.16.refs_1_.tokens, bf16[2048,1792]{1,0:T(8,128)(2,1)S(1)} %get-tuple-element.18.refs_2_, ...), custom_call_target="tpu_custom_call" | custom-call | flops 1879048192 | bytes 16777216 | tf_op jit(solution)/shard_map/up_a/pallas_call | solution.py:234
  45.9 4.8 %finish.1 = bf16[128,1792]{1,0:T(8,128)(2,1)} custom-call(s32[1,128]{1,0:T(1,128)S(1)} %bitcast.13, bf16[128,8192]{1,0:T(8,128)(2,1)S(1)} %get-tuple-element.16.refs_1_.tokens, bf16[1024,1792]{1,0:T(8,128)(2,1)S(1)} %get-tuple-element.22.adapter_up, f32[128,1792]{1,0:T(8,128)S(1)} %get-tuple-element.23.gate_pre, f32[128,1792]{1,0:T(8,128)S(1)} %get-tuple-element.24.up_pre, ...), custom_call_target="tpu_custom_call" | custom-call | flops 1879048192 | bytes 4194304 | tf_op jit(solution)/shard_map/finish/pallas_call | solution.py:287
  (25 shorter events, 0.3 us)
Async XLA Ops:
  0.0 10.7 %collective-permute-start.1 = (bf16[1,8,8192]{2,1,0:T(8,128)(2,1)}, bf16[1,8,8192]{2,1,0:T(8,128)(2,1)S(1)}, u32[]{:S(2)}, u32[]{:S(2)}) collective-permute-start(bf16[1,8,8192]{2,1,0:T(8,128)(2,1)} %bitcast.8), channel_id=1, source_target_pairs={{0,8},{1,9},{2,10},{3,11},{4,12},{5,13},{6,14},{7,15},{8,0},{9,1},... | collective-permute-start | bytes 393224 | tf_op jit(solution)/shard_map/ppermute | solution.py:44
  4.0 7.4 %collective-permute-start.2 = (bf16[1,8,8192]{2,1,0:T(8,128)(2,1)}, bf16[1,8,8192]{2,1,0:T(8,128)(2,1)S(1)}, u32[]{:S(2)}, u32[]{:S(2)}) collective-permute-start(bf16[1,8,8192]{2,1,0:T(8,128)(2,1)} %bitcast.9), channel_id=1, source_target_pairs={{0,2},{1,3},{2,0},{3,1},{4,6},{5,7},{6,4},{7,5},{8,10},{9,11},{10,... | collective-permute-start | bytes 393224 | tf_op jit(solution)/shard_map/ppermute | solution.py:44
  5.6 6.5 %collective-permute-start = (bf16[1,8,8192]{2,1,0:T(8,128)(2,1)}, bf16[1,8,8192]{2,1,0:T(8,128)(2,1)S(1)}, u32[]{:S(2)}, u32[]{:S(2)}) collective-permute-start(bf16[1,8,8192]{2,1,0:T(8,128)(2,1)} %bitcast.10), channel_id=1, source_target_pairs={{0,4},{1,5},{2,6},{3,7},{4,0},{5,1},{6,2},{7,3},{8,12},{9,13},{10,... | collective-permute-start | bytes 393224 | tf_op jit(solution)/shard_map/ppermute | solution.py:44
  10.7 5.5 %collective-permute-start.3 = (bf16[1,8,8192]{2,1,0:T(8,128)(2,1)S(1)}, bf16[1,8,8192]{2,1,0:T(8,128)(2,1)S(1)}, u32[]{:S(2)}, u32[]{:S(2)}) collective-permute-start(bf16[1,8,8192]{2,1,0:T(8,128)(2,1)S(1)} %tie.2.refs_1_), channel_id=1, source_target_pairs={{0,4},{1,5},{2,6},{3,7},{4,0},{5,1},{6,2},{7,3},{8,12},{9,13},{10,... | collective-permute-start | bytes 393224 | tf_op jit(solution)/shard_map/ppermute | solution.py:44
  12.1 10.2 %collective-permute-start.4 = (bf16[2,8,8192]{2,1,0:T(8,128)(2,1)S(1)}, bf16[2,8,8192]{2,1,0:T(8,128)(2,1)S(1)}, u32[]{:S(2)}, u32[]{:S(2)}) collective-permute-start(bf16[2,8,8192]{2,1,0:T(8,128)(2,1)S(1)} %pack.3.refs_0_.refs_1_), channel_id=1, source_target_pairs={{0,2},{1,3},{2,0},{3,1},{4,6},{5,7},{6,4},{7,5},{8,10},{9,11},{10,... | collective-permute-start | bytes 786440 | tf_op jit(solution)/shard_map/ppermute | solution.py:44
  16.2 1.3 %copy-start.1 = (bf16[8,8192]{1,0:T(8,128)(2,1)S(1)}, bf16[8,8192]{1,0:T(8,128)(2,1)}, u32[]{:S(2)}) copy-start(bf16[8,8192]{1,0:T(8,128)(2,1)} %param.8) | copy-start | bytes 393220
  16.2 6.1 %collective-permute-start.5 = (bf16[1,8,8192]{2,1,0:T(8,128)(2,1)S(1)}, bf16[1,8,8192]{2,1,0:T(8,128)(2,1)S(1)}, u32[]{:S(2)}, u32[]{:S(2)}) collective-permute-start(bf16[1,8,8192]{2,1,0:T(8,128)(2,1)S(1)} %tie.3.refs_2_), channel_id=1, source_target_pairs={{0,2},{1,3},{2,0},{3,1},{4,6},{5,7},{6,4},{7,5},{8,10},{9,11},{10,... | collective-permute-start | bytes 393224 | tf_op jit(solution)/shard_map/ppermute | solution.py:44
  20.7 3.6 %copy-start = (bf16[1,8192,64]{1,2,0:T(8,128)(2,1)S(1)}, bf16[1,8192,64]{1,2,0:T(8,128)(2,1)}, u32[]{:S(2)}) copy-start(bf16[1,8192,64]{1,2,0:T(8,128)(2,1)} %param.11) | copy-start | bytes 3145732
  20.7 3.6 %copy-start.2 = (s32[128]{0:T(128)S(1)}, s32[128]{0:T(128)}, u32[]{:S(2)}) copy-start(s32[128]{0:T(128)} %param.13) | copy-start | bytes 1540
  20.8 3.6 %copy-start.3 = (s32[16]{0:T(128)S(1)}, s32[16]{0:T(128)}, u32[]{:S(2)}) copy-start(s32[16]{0:T(128)} %param.14) | copy-start | bytes 196
  20.8 2.0 %collective-permute-start.6 = (bf16[4,8,8192]{2,1,0:T(8,128)(2,1)S(1)}, bf16[4,8,8192]{2,1,0:T(8,128)(2,1)S(1)}, u32[]{:S(2)}, u32[]{:S(2)}) collective-permute-start(bf16[4,8,8192]{2,1,0:T(8,128)(2,1)S(1)} %pack.4.refs_0_), channel_id=1, source_target_pairs={{0,1},{1,0},{2,3},{3,2},{4,5},{5,4},{6,7},{7,6},{8,9},{9,8},{10,11... | collective-permute-start | bytes 1572872 | tf_op jit(solution)/shard_map/ppermute | solution.py:44
  22.3 2.0 %collective-permute-start.7 = (bf16[4,8,8192]{2,1,0:T(8,128)(2,1)S(1)}, bf16[4,8,8192]{2,1,0:T(8,128)(2,1)S(1)}, u32[]{:S(2)}, u32[]{:S(2)}) collective-permute-start(bf16[4,8,8192]{2,1,0:T(8,128)(2,1)S(1)} %pack.5.refs_1_), channel_id=1, source_target_pairs={{0,1},{1,0},{2,3},{3,2},{4,5},{5,4},{6,7},{7,6},{8,9},{9,8},{10,11... | collective-permute-start | bytes 1572872 | tf_op jit(solution)/shard_map/ppermute | solution.py:44
  25.5 8.5 %collective-permute-start.8 = (bf16[128,64]{1,0:T(8,128)(2,1)S(1)}, bf16[128,64]{1,0:T(8,128)(2,1)S(1)}, u32[]{:S(2)}, u32[]{:S(2)}) collective-permute-start(bf16[128,64]{1,0:T(8,128)(2,1)S(1)} %get-tuple-element.17.refs_0_), channel_id=1, source_target_pairs={{0,8},{1,9},{2,10},{3,11},{4,12},{5,13},{6,14},{7,15},{8,0},{9,1},... | collective-permute-start | bytes 49160 | tf_op jit(solution)/shard_map/ppermute | solution.py:44
  34.1 5.6 %collective-permute-start.9 = (bf16[128,64]{1,0:T(8,128)(2,1)S(1)}, bf16[128,64]{1,0:T(8,128)(2,1)S(1)}, u32[]{:S(2)}, u32[]{:S(2)}) collective-permute-start(bf16[128,64]{1,0:T(8,128)(2,1)S(1)} %add.2.refs_0_), channel_id=1, source_target_pairs={{0,4},{1,5},{2,6},{3,7},{4,0},{5,1},{6,2},{7,3},{8,12},{9,13},{10,... | collective-permute-start | bytes 49160 | tf_op jit(solution)/shard_map/ppermute | solution.py:44
  39.7 6.2 %collective-permute-start.10 = (bf16[128,64]{1,0:T(8,128)(2,1)S(1)}, bf16[128,64]{1,0:T(8,128)(2,1)S(1)}, u32[]{:S(2)}, u32[]{:S(2)}) collective-permute-start(bf16[128,64]{1,0:T(8,128)(2,1)S(1)} %add.3.refs_0_.refs_2_), channel_id=1, source_target_pairs={{0,1},{1,0},{2,3},{3,2},{4,5},{5,4},{6,7},{7,6},{8,9},{9,8},{10,11... | collective-permute-start | bytes 49160 | tf_op jit(solution)/shard_map/ppermute | solution.py:44
  39.7 6.1 %collective-permute-start.11 = (bf16[128,64]{1,0:T(8,128)(2,1)S(1)}, bf16[128,64]{1,0:T(8,128)(2,1)S(1)}, u32[]{:S(2)}, u32[]{:S(2)}) collective-permute-start(bf16[128,64]{1,0:T(8,128)(2,1)S(1)} %add.3.refs_0_.refs_2_), channel_id=1, source_target_pairs={{0,2},{1,3},{2,0},{3,1},{4,6},{5,7},{6,4},{7,5},{8,10},{9,11},{10,... | collective-permute-start | bytes 49160 | tf_op jit(solution)/shard_map/ppermute | solution.py:44
  41.3 4.6 %collective-permute-start.12 = (bf16[128,64]{1,0:T(8,128)(2,1)S(1)}, bf16[128,64]{1,0:T(8,128)(2,1)S(1)}, u32[]{:S(2)}, u32[]{:S(2)}) collective-permute-start(bf16[128,64]{1,0:T(8,128)(2,1)S(1)} %add.3.refs_0_.refs_2_), channel_id=1, source_target_pairs={{0,3},{1,2},{2,1},{3,0},{4,7},{5,6},{6,5},{7,4},{8,11},{9,10},{10,... | collective-permute-start | bytes 49160 | tf_op jit(solution)/shard_map/ppermute | solution.py:44

commit v4 on v3

--- a/solution.py
+++ b/solution.py
@@ -118,9 +118,11 @@
     )(value, *after)
 
 
-def collect_kernel(depth, width, sizes, placement, index, down, *refs):
+def collect_kernel(depth, width, sizes, first, placement, index, down, core_down, *refs):
     mine, theirs = refs[: len(sizes)], refs[len(sizes) : 2 * len(sizes)]
-    packed, low = refs[2 * len(sizes) :]
+    source, packed, low, target, sem = refs[2 * len(sizes) :]
+    copy = pltpu.make_async_copy(source.at[pl.ds(first, target.shape[0])], target, sem)
+    copy.start()
     own = lax.axis_index("tensor")
     c = own % 2
     rows = packed.shape[0] // (2 * depth * width)
@@ -130,38 +132,52 @@
             j, k = place % depth, place // depth
             chip = (own // 2) ^ (j * width + k)
             p, q = p_ref[i], q_ref[i]
-            first, second = jnp.where(c == 0, p, q), jnp.where(c == 0, q, p)
+            before, after = jnp.where(c == 0, p, q), jnp.where(c == 0, q, p)
             packed[pl.ds(pl.multiple_of(chip * 2 * rows, 2 * rows), 2 * rows), :] = (
-                jnp.concatenate([first, second], 0)
+                jnp.concatenate([before, after], 0)
             )
             place += 1
-    full = lax.dot_general(
-        packed[...], down[...], (((1,), (1,)), ((), ())), preferred_element_type=jnp.float32
-    )
     ids = lax.broadcasted_iota(jnp.int32, placement.shape, 1)
-    owner = jnp.sum(jnp.where(placement[...] == own, ids, 0), axis=1, keepdims=True)
-    chosen = across(jnp.where(index[...] == owner, 1, 0))[:, : full.shape[1]]
-    low[...] = jnp.where(chosen == 1, full, 0.0).astype(low.dtype)
-
-
-def collect(placement, index, down, mine, theirs, depth, width):
+    total = None
+    for slot, weight in ((own, down), (own ^ 1, core_down)):
+        full = lax.dot_general(
+            packed[...], weight[...], (((1,), (1,)), ((), ())), preferred_element_type=jnp.float32
+        )
+        owner = jnp.sum(jnp.where(placement[...] == slot, ids, 0), axis=1, keepdims=True)
+        chosen = across(jnp.where(index[...] == owner, 1, 0))[:, : full.shape[1]]
+        total = jnp.where(chosen == 1, full, 0.0 if total is None else total)
+    low[...] = total.astype(low.dtype)
+    copy.wait()
+
+
+def collect(placement, index, downs, mine, theirs, depth, width, fetched):
     sizes = [v.shape[0] for v in mine]
     rows, model = mine[0].shape[1:]
     requests = 2 * depth * width * rows
-    return pl.pallas_call(
-        functools.partial(collect_kernel, depth, width, sizes),
+    source, first, fetched_rows = fetched
+    return pl.pallas_call(
+        functools.partial(collect_kernel, depth, width, sizes, first),
         out_shape=[
             pltpu.VMEM((requests, model), jnp.bfloat16),
-            jax.ShapeDtypeStruct((requests, down.shape[0]), jnp.bfloat16),
+            jax.ShapeDtypeStruct((requests, downs[0].shape[0]), jnp.bfloat16),
+            pltpu.VMEM((fetched_rows, source.shape[1]), source.dtype),
         ],
-        in_specs=[NEAR] * (3 + 2 * len(sizes)),
-        out_specs=[NEAR] * 2,
+        in_specs=[NEAR] * (4 + 2 * len(sizes)) + [STORED],
+        out_specs=[NEAR] * 3,
+        scratch_shapes=[pltpu.SemaphoreType.DMA],
         cost_estimate=pl.CostEstimate(
-            flops=2 * requests * model * 64, bytes_accessed=1 << 20, transcendentals=0
+            flops=4 * requests * model * 64, bytes_accessed=1 << 20, transcendentals=0
         ),
         compiler_params=pltpu.CompilerParams(vmem_limit_bytes=4 << 20),
         name="collect",
-    )(placement, index, down, *[near(v) for v in mine], *[near(v) for v in theirs])
+    )(
+        placement,
+        index,
+        *downs,
+        *[near(v) for v in mine],
+        *[near(v) for v in theirs],
+        far(source),
+    )
 
 
 def add_kernel(*refs):
@@ -315,67 +331,67 @@
     model, hidden = gate_weight.shape
     index = request_adapter_index[None, :]
     part = model // PIECES
+    unit = part // 4
     up = up.reshape(-1, hidden)
+    down = jnp.swapaxes(down[0], 0, 1)
     own = tokens[None]
     core, column, line_1, line_2 = 1, 2, 2 * width, 4 * width
 
+    block_1 = swap(own, line_1)
     block_2 = swap(own, line_2)
-    block_1 = swap(own, line_1)
     column_0 = swap(own, column)
+    core_down = swap(down, core)
     gate_0 = fetch(gate_weight, 0, part, "fetch_0")
-    block_2 = tie(block_2, [gate_0])
+    block_1 = tie(block_1, [gate_0, column_0])
+    column_1 = swap(block_1, column)
+    gate_1 = fetch(gate_weight, part, part, "fetch_1", [block_1, core_down])
+    block_2 = tie(block_2, [gate_1, column_1])
     block_3 = swap(block_2, line_1)
-    blocks_12 = pack([block_1, block_2], [gate_0, column_0])
-    columns_12 = swap(blocks_12, column)
-    gate_1 = fetch(gate_weight, part, part, "fetch_1", [blocks_12])
-    block_3 = tie(block_3, [gate_1])
+    column_2 = swap(block_2, column)
+    gate_2 = fetch(gate_weight, 2 * part, part, "fetch_2", [block_2])
+    block_3 = tie(block_3, [gate_2, column_2])
     column_3 = swap(block_3, column)
-    line = pack([own, blocks_12, block_3], [])
+    line = pack([own, block_1, block_2, block_3], [])
     core_line = swap(line, core)
-    gate_2 = fetch(gate_weight, 2 * part, part, "fetch_2", [line])
-    columns = pack([column_0, columns_12, column_3], [gate_2])
+    gate_3 = fetch(gate_weight, 3 * part, part, "fetch_3", [line])
+    columns = pack([column_0, column_1, column_2, column_3], [gate_3])
     core_columns = swap(columns, core)
-    packed, low = collect(
+    packed, low, up_0 = collect(
         placement[None, :],
         index,
-        jnp.swapaxes(down[0], 0, 1),
+        [down, core_down],
         [line, columns],
         [core_line, core_columns],
         depth,
         width,
+        (up_weight, 0, 2 * unit),
     )
 
     low_1 = add(low, swap(low, line_2))
-    gate_pre, gate_3, up_0 = multiply(
-        low,
-        packed,
-        [gate_0, gate_1],
-        0,
-        [],
-        [(gate_weight, 3 * part, part), (up_weight, 0, part)],
-        "gate_a",
+    gate_pre, up_1 = multiply(
+        low, packed, [gate_0, gate_1], 0, [], [(up_weight, 2 * unit, 5 * unit)], "gate_a"
     )
     low_2 = add(low_1, swap(low_1, line_1))
-    gate_pre, up_1, up_2 = multiply(
+    gate_pre, up_2, up_3 = multiply(
         low_1,
         packed,
         [gate_2, gate_3],
         2 * part,
         [gate_pre],
-        [(up_weight, part, part), (up_weight, 2 * part, part)],
+        [(up_weight, 7 * unit, unit), (up_weight, 8 * unit, part)],
         "gate_b",
     )
-    lows = [low_2] + [swap(low_2, mask) for mask in (core, column, core + column)]
-    up_pre, near_up, up_3 = multiply(
+    lows = [low_2, swap(low_2, column)]
+    up_pre, near_up, up_4 = multiply(
         low_2,
         packed,
-        [up_0, up_1],
+        [up_0, up_1, up_2],
         0,
         [],
         [(up, 0, up.shape[0]), (up_weight, 3 * part, part)],
         "up_a",
     )
-    return finish(index, packed, near_up, gate_pre, up_pre, [up_2, up_3], 2 * part, lows)
+    return finish(index, packed, near_up, gate_pre, up_pre, [up_3, up_4], 2 * part, lows)
 
 
 def streamed(

time: 50.8 us -> 52.5 us (1.033)
  waiting for transfers between devices: 4.34 us -> 5.72 us
  Pallas kernels: 30.2 us -> 31.4 us
  starting transfers between devices: 15.8 us -> 15 us
    pallas_call x3 -> x4, Pallas kernels: 9.56 us -> 12.7 us  [fetch(): pl.pallas_call(functools.partial(fetch_kernel, start, len(after)), out_sh...]
    pallas_call x3, Pallas kernels: 14.6 us -> 11.5 us  [multiply(): pl.pallas_call(functools.partial(multiply_kernel, start, len(pieces), len...]
    ppermute x13, waiting for transfers between devices: 4.34 us -> 5.72 us  [swap(): return lax.ppermute(value, 'tensor', pairs)]
    pallas_call x1, Pallas kernels: 1.2 us -> 2.25 us  [collect(): pl.pallas_call(functools.partial(collect_kernel, depth, width, sizes, fir...]
    ppermute x13, starting transfers between devices: 15.8 us -> 15 us  [swap(): return lax.ppermute(value, 'tensor', pairs)]
  transfers between devices with their start and end apart: 13 -> 13, of which waited for: 5 -> 5; matrix products, arithmetic and copies ran while one was open for 0% -> 0% of each run, Pallas kernels for 48% -> 46%
where the time goes in v4:
time: 52.5 us; the launch traced here: 52.3 us
  Pallas kernels  31.4 us (60%)
  starting transfers between devices  15 us (29%)
  waiting for transfers between devices  5.72 us (11%)
    ppermute x13, starting transfers between devices, swap(): return lax.ppermute(value, 'tensor', pairs)  15 us
    pallas_call x4, Pallas kernels, fetch(): pl.pallas_call(functools.partial(fetch_kernel, start, len(after)), out_sh...  12.7 us
    pallas_call x3, Pallas kernels, multiply(): pl.pallas_call(functools.partial(multiply_kernel, start, len(pieces), len...  11.5 us
    ppermute x13, waiting for transfers between devices, swap(): return lax.ppermute(value, 'tensor', pairs)  5.72 us
    pallas_call x1, Pallas kernels, finish(): pl.pallas_call(functools.partial(finish_kernel, start, len(pieces), len(l...  4.77 us
    pallas_call x1, Pallas kernels, collect(): pl.pallas_call(functools.partial(collect_kernel, depth, width, sizes, fir...  2.25 us
  transfers between devices with their start and end apart: 13, of which 5 were waited for; matrix products, arithmetic and copies ran while one was open for 0% of the time, Pallas kernels for 46%

profile of v4, /device:TPU:0, one launch (start us, length us, event | category | flops | bytes accessed | tf_op | source)
XLA Modules:
  0.0 52.3 jit_solution(7473244260540558599)
XLA Ops:
  0.0 0.5 collective-permute-start
  0.5 2.5 %collective-permute-start.2 = (bf16[1,8,8192]{2,1,0:T(8,128)(2,1)}, bf16[1,8,8192]{2,1,0:T(8,128)(2,1)S(1)}, u32[]{:S(2)}, u32[]{:S(2)}) collective-permute-start(bf16[1,8,8192]{2,1,0:T(8,128)(2,1)} %bitcast.9), channel_id=1, source_target_pairs={{0,2},{1,3},{2,0},{3,1},{4,6},{5,7},{6,4},{7,5},{8,10},{9,11},{10,... | collective-permute-start | bytes 393224 | tf_op jit(solution)/shard_map/ppermute | solution.py:44
  3.0 1.6 %collective-permute-start.1 = (bf16[1,8,8192]{2,1,0:T(8,128)(2,1)}, bf16[1,8,8192]{2,1,0:T(8,128)(2,1)S(1)}, u32[]{:S(2)}, u32[]{:S(2)}) collective-permute-start(bf16[1,8,8192]{2,1,0:T(8,128)(2,1)} %bitcast.10), channel_id=1, source_target_pairs={{0,4},{1,5},{2,6},{3,7},{4,0},{5,1},{6,2},{7,3},{8,12},{9,13},{10,... | collective-permute-start | bytes 393224 | tf_op jit(solution)/shard_map/ppermute | solution.py:44
  4.5 2.6 %collective-permute-start.3 = (bf16[1,8,8192]{2,1,0:T(8,128)(2,1)}, bf16[1,8,8192]{2,1,0:T(8,128)(2,1)S(1)}, u32[]{:S(2)}, u32[]{:S(2)}) collective-permute-start(bf16[1,8,8192]{2,1,0:T(8,128)(2,1)} %bitcast.11), channel_id=1, source_target_pairs={{0,8},{1,9},{2,10},{3,11},{4,12},{5,13},{6,14},{7,15},{8,0},{9,1},... | collective-permute-start | bytes 393224 | tf_op jit(solution)/shard_map/ppermute | solution.py:44
  7.1 3.2 %fetch_0.1.refs_1_.refs_2_ = bf16[2048,1792]{1,0:T(8,128)(2,1)S(1)} custom-call(bf16[8192,1792]{1,0:T(8,128)(2,1)} %source.7), custom_call_target="tpu_custom_call" | custom-call | bytes 7340032 | tf_op jit(solution)/shard_map/fetch_0/pallas_call | solution.py:63
  10.3 0.9 %collective-permute-done.1.refs_0_ = bf16[1,8,8192]{2,1,0:T(8,128)(2,1)S(1)} collective-permute-done((bf16[1,8,8192]{2,1,0:T(8,128)(2,1)}, bf16[1,8,8192]{2,1,0:T(8,128)(2,1)S(1)}, u32[]{:S(2)}, u32[]{:S(2)}) %collective-permute-start.1) | collective-permute-done | bytes 131104 | tf_op jit(solution)/shard_map/ppermute | solution.py:44
  11.5 3.2 %fetch_1.1.refs_1_.refs_3_ = bf16[2048,1792]{1,0:T(8,128)(2,1)S(1)} custom-call(bf16[8192,1792]{1,0:T(8,128)(2,1)} %source.7, bf16[1,8,8192]{2,1,0:T(8,128)(2,1)S(1)} %tie.3.refs_0_.refs_1_, bf16[64,8192]{1,0:T(8,128)(2,1)S(1)} %collective-permute-done.refs_1_.core_down), custom_call_target="tpu_custom_call" | custom-call | bytes 7340032 | tf_op jit(solution)/shard_map/fetch_1/pallas_call | solution.py:63
  14.7 1.5 %collective-permute-done.4.refs_2_.refs_1_ = bf16[1,8,8192]{2,1,0:T(8,128)(2,1)S(1)} collective-permute-done((bf16[1,8,8192]{2,1,0:T(8,128)(2,1)S(1)}, bf16[1,8,8192]{2,1,0:T(8,128)(2,1)S(1)}, u32[]{:S(2)}, u32[]{:S(2)}) %collective-permute-start.4) | collective-permute-done | bytes 131104 | tf_op jit(solution)/shard_map/ppermute | solution.py:44
  16.2 0.3 collective-permute-start.6
  16.6 3.2 %fetch_2.1.refs_1_.refs_2_ = bf16[2048,1792]{1,0:T(8,128)(2,1)S(1)} custom-call(bf16[8192,1792]{1,0:T(8,128)(2,1)} %source.7, bf16[1,8,8192]{2,1,0:T(8,128)(2,1)S(1)} %tie.4.refs_0_.refs_2_), custom_call_target="tpu_custom_call" | custom-call | bytes 7340032 | tf_op jit(solution)/shard_map/fetch_2/pallas_call | solution.py:63
  19.8 1.4 %collective-permute-done.6.refs_2_ = bf16[1,8,8192]{2,1,0:T(8,128)(2,1)S(1)} collective-permute-done((bf16[1,8,8192]{2,1,0:T(8,128)(2,1)S(1)}, bf16[1,8,8192]{2,1,0:T(8,128)(2,1)S(1)}, u32[]{:S(2)}, u32[]{:S(2)}) %collective-permute-start.6) | collective-permute-done | bytes 131104 | tf_op jit(solution)/shard_map/ppermute | solution.py:44
  21.2 0.3 collective-permute-done.5.refs_0_
  21.5 1.7 %collective-permute-start.7 = (bf16[1,8,8192]{2,1,0:T(8,128)(2,1)S(1)}, bf16[1,8,8192]{2,1,0:T(8,128)(2,1)S(1)}, u32[]{:S(2)}, u32[]{:S(2)}) collective-permute-start(bf16[1,8,8192]{2,1,0:T(8,128)(2,1)S(1)} %tie.5.refs_3_), channel_id=1, source_target_pairs={{0,2},{1,3},{2,0},{3,1},{4,6},{5,7},{6,4},{7,5},{8,10},{9,11},{10,... | collective-permute-start | bytes 393224 | tf_op jit(solution)/shard_map/ppermute | solution.py:44
  23.3 3.2 %fetch_3.1.refs_4_.refs_3_ = bf16[2048,1792]{1,0:T(8,128)(2,1)S(1)} custom-call(bf16[8192,1792]{1,0:T(8,128)(2,1)} %source.7, bf16[4,8,8192]{2,1,0:T(8,128)(2,1)S(1)} %pack.2.refs_0_), custom_call_target="tpu_custom_call" | custom-call | bytes 7340032 | tf_op jit(solution)/shard_map/fetch_3/pallas_call | solution.py:63
  26.6 0.6 %collective-permute-start.9 = (bf16[4,8,8192]{2,1,0:T(8,128)(2,1)S(1)}, bf16[4,8,8192]{2,1,0:T(8,128)(2,1)S(1)}, u32[]{:S(2)}, u32[]{:S(2)}) collective-permute-start(bf16[4,8,8192]{2,1,0:T(8,128)(2,1)S(1)} %pack.3.refs_1_), channel_id=1, source_target_pairs={{0,1},{1,0},{2,3},{3,2},{4,5},{5,4},{6,7},{7,6},{8,9},{9,8},{10,11... | collective-permute-start | bytes 1572872 | tf_op jit(solution)/shard_map/ppermute | solution.py:44
  27.2 1.5 %collective-permute-done.9.refs_3_ = bf16[4,8,8192]{2,1,0:T(8,128)(2,1)S(1)} collective-permute-done((bf16[4,8,8192]{2,1,0:T(8,128)(2,1)S(1)}, bf16[4,8,8192]{2,1,0:T(8,128)(2,1)S(1)}, u32[]{:S(2)}, u32[]{:S(2)}) %collective-permute-start.9) | collective-permute-done | bytes 524320 | tf_op jit(solution)/shard_map/ppermute | solution.py:44
  28.7 2.3 %collect.1 = (bf16[128,8192]{1,0:T(8,128)(2,1)S(1)}, bf16[128,64]{1,0:T(8,128)(2,1)S(1)}, bf16[1024,1792]{1,0:T(8,128)(2,1)S(1)}) custom-call(s32[1,16]{1,0:T(1,128)S(1)} %bitcast.15, s32[1,128]{1,0:T(1,128)S(1)} %bitcast.13, bf16[64,8192]{1,0:T(8,128)(2,1)S(1)} %bitcast.8, bf16[64,8192]{1,0:T(8,128)(2,1)S(1)} %collective-permute-done.refs_1_.core_down, ...), custom_call_target="tpu_custom_call" | custom-call | flops 268435456 | bytes 1048576 | tf_op jit(solution)/shard_map/collect/pallas_call | solution.py:158
  31.0 1.7 %collective-permute-start.10 = (bf16[128,64]{1,0:T(8,128)(2,1)S(1)}, bf16[128,64]{1,0:T(8,128)(2,1)S(1)}, u32[]{:S(2)}, u32[]{:S(2)}) collective-permute-start(bf16[128,64]{1,0:T(8,128)(2,1)S(1)} %get-tuple-element.17.refs_0_), channel_id=1, source_target_pairs={{0,8},{1,9},{2,10},{3,11},{4,12},{5,13},{6,14},{7,15},{8,0},{9,1},... | collective-permute-start | bytes 49160 | tf_op jit(solution)/shard_map/ppermute | solution.py:44
  32.7 3.6 %gate_a.1 = (f32[128,1792]{1,0:T(8,128)S(1)}, bf16[2560,1792]{1,0:T(8,128)(2,1)S(1)}) custom-call(bf16[128,64]{1,0:T(8,128)(2,1)S(1)} %get-tuple-element.17.refs_0_, bf16[128,8192]{1,0:T(8,128)(2,1)S(1)} %get-tuple-element.16.refs_1_.tokens, bf16[2048,1792]{1,0:T(8,128)(2,1)S(1)} %fetch_0.1.refs_1_.refs_2_, bf16[2048,1792]{1,0:T(8,128)(2,1)S(1)} %fetch_1.1.refs_1_.refs_3_, ...), custom_call_target="tpu_custom_call" | custom-call | flops 1879048192 | bytes 16777216 | tf_op jit(solution)/shard_map/gate_a/pallas_call | solution.py:250
  36.4 1.7 %collective-permute-start.11 = (bf16[128,64]{1,0:T(8,128)(2,1)S(1)}, bf16[128,64]{1,0:T(8,128)(2,1)S(1)}, u32[]{:S(2)}, u32[]{:S(2)}) collective-permute-start(bf16[128,64]{1,0:T(8,128)(2,1)S(1)} %add.2.refs_0_), channel_id=1, source_target_pairs={{0,4},{1,5},{2,6},{3,7},{4,0},{5,1},{6,2},{7,3},{8,12},{9,13},{10,... | collective-permute-start | bytes 49160 | tf_op jit(solution)/shard_map/ppermute | solution.py:44
  38.1 3.7 %gate_b.1 = (f32[128,1792]{1,0:T(8,128)S(1)}, bf16[512,1792]{1,0:T(8,128)(2,1)S(1)}, bf16[2048,1792]{1,0:T(8,128)(2,1)S(1)}) custom-call(bf16[128,64]{1,0:T(8,128)(2,1)S(1)} %add.2.refs_0_, bf16[128,8192]{1,0:T(8,128)(2,1)S(1)} %get-tuple-element.16.refs_1_.tokens, bf16[2048,1792]{1,0:T(8,128)(2,1)S(1)} %fetch_2.1.refs_1_.refs_2_, ...), custom_call_target="tpu_custom_call" | custom-call | flops 1879048192 | bytes 16777216 | tf_op jit(solution)/shard_map/gate_b/pallas_call | solution.py:250
  41.8 1.5 %collective-permute-start.12 = (bf16[128,64]{1,0:T(8,128)(2,1)S(1)}, bf16[128,64]{1,0:T(8,128)(2,1)S(1)}, u32[]{:S(2)}, u32[]{:S(2)}) collective-permute-start(bf16[128,64]{1,0:T(8,128)(2,1)S(1)} %add.3.refs_0_.refs_2_), channel_id=1, source_target_pairs={{0,2},{1,3},{2,0},{3,1},{4,6},{5,7},{6,4},{7,5},{8,10},{9,11},{10,... | collective-permute-start | bytes 49160 | tf_op jit(solution)/shard_map/ppermute | solution.py:44
  43.3 4.2 %up_a.1 = (f32[128,1792]{1,0:T(8,128)S(1)}, bf16[1024,1792]{1,0:T(8,128)(2,1)S(1)}, bf16[2048,1792]{1,0:T(8,128)(2,1)S(1)}) custom-call(bf16[128,64]{1,0:T(8,128)(2,1)S(1)} %add.3.refs_0_.refs_2_, bf16[128,8192]{1,0:T(8,128)(2,1)S(1)} %get-tuple-element.16.refs_1_.tokens, bf16[1024,1792]{1,0:T(8,128)(2,1)S(1)} %get-tuple-element.18.refs_2_, ...), custom_call_target="tpu_custom_call" | custom-call | flops 1879048192 | bytes 16777216 | tf_op jit(solution)/shard_map/up_a/pallas_call | solution.py:250
  47.6 4.8 %finish.1 = bf16[128,1792]{1,0:T(8,128)(2,1)} custom-call(s32[1,128]{1,0:T(1,128)S(1)} %bitcast.14, bf16[128,8192]{1,0:T(8,128)(2,1)S(1)} %get-tuple-element.16.refs_1_.tokens, bf16[1024,1792]{1,0:T(8,128)(2,1)S(1)} %get-tuple-element.22.adapter_up, f32[128,1792]{1,0:T(8,128)S(1)} %get-tuple-element.23.gate_pre, f32[128,1792]{1,0:T(8,128)S(1)} %get-tuple-element.24.up_pre, ...), custom_call_target="tpu_custom_call" | custom-call | flops 1879048192 | bytes 4194304 | tf_op jit(solution)/shard_map/finish/pallas_call | solution.py:303
  (26 shorter events, 0.5 us)
Async XLA Ops:
  0.0 11.5 %collective-permute-start = (bf16[64,8192]{1,0:T(8,128)(2,1)}, bf16[64,8192]{1,0:T(8,128)(2,1)S(1)}, u32[]{:S(2)}, u32[]{:S(2)}) collective-permute-start(bf16[64,8192]{1,0:T(8,128)(2,1)} %bitcast.7), channel_id=1, source_target_pairs={{0,1},{1,0},{2,3},{3,2},{4,5},{5,4},{6,7},{7,6},{8,9},{9,8},{10,11... | collective-permute-start | bytes 3145736 | tf_op jit(solution)/shard_map/ppermute | solution.py:44
  0.5 9.9 %collective-permute-start.2 = (bf16[1,8,8192]{2,1,0:T(8,128)(2,1)}, bf16[1,8,8192]{2,1,0:T(8,128)(2,1)S(1)}, u32[]{:S(2)}, u32[]{:S(2)}) collective-permute-start(bf16[1,8,8192]{2,1,0:T(8,128)(2,1)} %bitcast.9), channel_id=1, source_target_pairs={{0,2},{1,3},{2,0},{3,1},{4,6},{5,7},{6,4},{7,5},{8,10},{9,11},{10,... | collective-permute-start | bytes 393224 | tf_op jit(solution)/shard_map/ppermute | solution.py:44
  3.0 8.3 %collective-permute-start.1 = (bf16[1,8,8192]{2,1,0:T(8,128)(2,1)}, bf16[1,8,8192]{2,1,0:T(8,128)(2,1)S(1)}, u32[]{:S(2)}, u32[]{:S(2)}) collective-permute-start(bf16[1,8,8192]{2,1,0:T(8,128)(2,1)} %bitcast.10), channel_id=1, source_target_pairs={{0,4},{1,5},{2,6},{3,7},{4,0},{5,1},{6,2},{7,3},{8,12},{9,13},{10,... | collective-permute-start | bytes 393224 | tf_op jit(solution)/shard_map/ppermute | solution.py:44
  4.5 10.1 %collective-permute-start.3 = (bf16[1,8,8192]{2,1,0:T(8,128)(2,1)}, bf16[1,8,8192]{2,1,0:T(8,128)(2,1)S(1)}, u32[]{:S(2)}, u32[]{:S(2)}) collective-permute-start(bf16[1,8,8192]{2,1,0:T(8,128)(2,1)} %bitcast.11), channel_id=1, source_target_pairs={{0,8},{1,9},{2,10},{3,11},{4,12},{5,13},{6,14},{7,15},{8,0},{9,1},... | collective-permute-start | bytes 393224 | tf_op jit(solution)/shard_map/ppermute | solution.py:44
  11.2 5.0 %collective-permute-start.4 = (bf16[1,8,8192]{2,1,0:T(8,128)(2,1)S(1)}, bf16[1,8,8192]{2,1,0:T(8,128)(2,1)S(1)}, u32[]{:S(2)}, u32[]{:S(2)}) collective-permute-start(bf16[1,8,8192]{2,1,0:T(8,128)(2,1)S(1)} %tie.3.refs_0_.refs_1_), channel_id=1, source_target_pairs={{0,2},{1,3},{2,0},{3,1},{4,6},{5,7},{6,4},{7,5},{8,10},{9,11},{10,... | collective-permute-start | bytes 393224 | tf_op jit(solution)/shard_map/ppermute | solution.py:44
  16.2 5.0 %collective-permute-start.6 = (bf16[1,8,8192]{2,1,0:T(8,128)(2,1)S(1)}, bf16[1,8,8192]{2,1,0:T(8,128)(2,1)S(1)}, u32[]{:S(2)}, u32[]{:S(2)}) collective-permute-start(bf16[1,8,8192]{2,1,0:T(8,128)(2,1)S(1)} %tie.4.refs_0_.refs_2_), channel_id=1, source_target_pairs={{0,2},{1,3},{2,0},{3,1},{4,6},{5,7},{6,4},{7,5},{8,10},{9,11},{10,... | collective-permute-start | bytes 393224 | tf_op jit(solution)/shard_map/ppermute | solution.py:44
  16.6 5.0 %collective-permute-start.5 = (bf16[1,8,8192]{2,1,0:T(8,128)(2,1)S(1)}, bf16[1,8,8192]{2,1,0:T(8,128)(2,1)S(1)}, u32[]{:S(2)}, u32[]{:S(2)}) collective-permute-start(bf16[1,8,8192]{2,1,0:T(8,128)(2,1)S(1)} %tie.4.refs_0_.refs_2_), channel_id=1, source_target_pairs={{0,4},{1,5},{2,6},{3,7},{4,0},{5,1},{6,2},{7,3},{8,12},{9,13},{10,... | collective-permute-start | bytes 393224 | tf_op jit(solution)/shard_map/ppermute | solution.py:44
  19.7 3.5 %copy-start.1 = (bf16[8,8192]{1,0:T(8,128)(2,1)S(1)}, bf16[8,8192]{1,0:T(8,128)(2,1)}, u32[]{:S(2)}) copy-start(bf16[8,8192]{1,0:T(8,128)(2,1)} %param.8) | copy-start | bytes 393220
  21.5 5.0 %collective-permute-start.7 = (bf16[1,8,8192]{2,1,0:T(8,128)(2,1)S(1)}, bf16[1,8,8192]{2,1,0:T(8,128)(2,1)S(1)}, u32[]{:S(2)}, u32[]{:S(2)}) collective-permute-start(bf16[1,8,8192]{2,1,0:T(8,128)(2,1)S(1)} %tie.5.refs_3_), channel_id=1, source_target_pairs={{0,2},{1,3},{2,0},{3,1},{4,6},{5,7},{6,4},{7,5},{8,10},{9,11},{10,... | collective-permute-start | bytes 393224 | tf_op jit(solution)/shard_map/ppermute | solution.py:44
  23.2 3.9 %collective-permute-start.8 = (bf16[4,8,8192]{2,1,0:T(8,128)(2,1)S(1)}, bf16[4,8,8192]{2,1,0:T(8,128)(2,1)S(1)}, u32[]{:S(2)}, u32[]{:S(2)}) collective-permute-start(bf16[4,8,8192]{2,1,0:T(8,128)(2,1)S(1)} %pack.2.refs_0_), channel_id=1, source_target_pairs={{0,1},{1,0},{2,3},{3,2},{4,5},{5,4},{6,7},{7,6},{8,9},{9,8},{10,11... | collective-permute-start | bytes 1572872 | tf_op jit(solution)/shard_map/ppermute | solution.py:44
  26.5 2.2 %copy-start = (bf16[1,8192,64]{1,2,0:T(8,128)(2,1)S(1)}, bf16[1,8192,64]{1,2,0:T(8,128)(2,1)}, u32[]{:S(2)}) copy-start(bf16[1,8192,64]{1,2,0:T(8,128)(2,1)} %param.11) | copy-start | bytes 3145732
  26.5 2.2 %copy-start.2 = (s32[128]{0:T(128)S(1)}, s32[128]{0:T(128)}, u32[]{:S(2)}) copy-start(s32[128]{0:T(128)} %param.13) | copy-start | bytes 1540
  26.5 2.2 %copy-start.3 = (s32[16]{0:T(128)S(1)}, s32[16]{0:T(128)}, u32[]{:S(2)}) copy-start(s32[16]{0:T(128)} %param.14) | copy-start | bytes 196
  26.6 2.1 %collective-permute-start.9 = (bf16[4,8,8192]{2,1,0:T(8,128)(2,1)S(1)}, bf16[4,8,8192]{2,1,0:T(8,128)(2,1)S(1)}, u32[]{:S(2)}, u32[]{:S(2)}) collective-permute-start(bf16[4,8,8192]{2,1,0:T(8,128)(2,1)S(1)} %pack.3.refs_1_), channel_id=1, source_target_pairs={{0,1},{1,0},{2,3},{3,2},{4,5},{5,4},{6,7},{7,6},{8,9},{9,8},{10,11... | collective-permute-start | bytes 1572872 | tf_op jit(solution)/shard_map/ppermute | solution.py:44
  31.0 5.4 %collective-permute-start.10 = (bf16[128,64]{1,0:T(8,128)(2,1)S(1)}, bf16[128,64]{1,0:T(8,128)(2,1)S(1)}, u32[]{:S(2)}, u32[]{:S(2)}) collective-permute-start(bf16[128,64]{1,0:T(8,128)(2,1)S(1)} %get-tuple-element.17.refs_0_), channel_id=1, source_target_pairs={{0,8},{1,9},{2,10},{3,11},{4,12},{5,13},{6,14},{7,15},{8,0},{9,1},... | collective-permute-start | bytes 49160 | tf_op jit(solution)/shard_map/ppermute | solution.py:44
  36.4 5.4 %collective-permute-start.11 = (bf16[128,64]{1,0:T(8,128)(2,1)S(1)}, bf16[128,64]{1,0:T(8,128)(2,1)S(1)}, u32[]{:S(2)}, u32[]{:S(2)}) collective-permute-start(bf16[128,64]{1,0:T(8,128)(2,1)S(1)} %add.2.refs_0_), channel_id=1, source_target_pairs={{0,4},{1,5},{2,6},{3,7},{4,0},{5,1},{6,2},{7,3},{8,12},{9,13},{10,... | collective-permute-start | bytes 49160 | tf_op jit(solution)/shard_map/ppermute | solution.py:44
  41.8 5.8 %collective-permute-start.12 = (bf16[128,64]{1,0:T(8,128)(2,1)S(1)}, bf16[128,64]{1,0:T(8,128)(2,1)S(1)}, u32[]{:S(2)}, u32[]{:S(2)}) collective-permute-start(bf16[128,64]{1,0:T(8,128)(2,1)S(1)} %add.3.refs_0_.refs_2_), channel_id=1, source_target_pairs={{0,2},{1,3},{2,0},{3,1},{4,6},{5,7},{6,4},{7,5},{8,10},{9,11},{10,... | collective-permute-start | bytes 49160 | tf_op jit(solution)/shard_map/ppermute | solution.py:44

commit v5 on v4

--- a/solution.py
+++ b/solution.py
@@ -8,6 +8,7 @@
 from jax.sharding import PartitionSpec as P
 
 TILE = 256
+WIDE = 512
 PIECES = 4
 NEAR = pl.BlockSpec(memory_space=pltpu.VMEM)
 FAR = pl.BlockSpec(memory_space=pl.ANY)
@@ -118,11 +119,9 @@
     )(value, *after)
 
 
-def collect_kernel(depth, width, sizes, first, placement, index, down, core_down, *refs):
+def collect_kernel(depth, width, sizes, placement, index, down, core_down, *refs):
     mine, theirs = refs[: len(sizes)], refs[len(sizes) : 2 * len(sizes)]
-    source, packed, low, target, sem = refs[2 * len(sizes) :]
-    copy = pltpu.make_async_copy(source.at[pl.ds(first, target.shape[0])], target, sem)
-    copy.start()
+    packed, low = refs[2 * len(sizes) :]
     own = lax.axis_index("tensor")
     c = own % 2
     rows = packed.shape[0] // (2 * depth * width)
@@ -147,24 +146,20 @@
         chosen = across(jnp.where(index[...] == owner, 1, 0))[:, : full.shape[1]]
         total = jnp.where(chosen == 1, full, 0.0 if total is None else total)
     low[...] = total.astype(low.dtype)
-    copy.wait()
-
-
-def collect(placement, index, downs, mine, theirs, depth, width, fetched):
+
+
+def collect(placement, index, downs, mine, theirs, depth, width):
     sizes = [v.shape[0] for v in mine]
     rows, model = mine[0].shape[1:]
     requests = 2 * depth * width * rows
-    source, first, fetched_rows = fetched
-    return pl.pallas_call(
-        functools.partial(collect_kernel, depth, width, sizes, first),
+    return pl.pallas_call(
+        functools.partial(collect_kernel, depth, width, sizes),
         out_shape=[
             pltpu.VMEM((requests, model), jnp.bfloat16),
             jax.ShapeDtypeStruct((requests, downs[0].shape[0]), jnp.bfloat16),
-            pltpu.VMEM((fetched_rows, source.shape[1]), source.dtype),
         ],
-        in_specs=[NEAR] * (4 + 2 * len(sizes)) + [STORED],
-        out_specs=[NEAR] * 3,
-        scratch_shapes=[pltpu.SemaphoreType.DMA],
+        in_specs=[NEAR] * (4 + 2 * len(sizes)),
+        out_specs=[NEAR] * 2,
         cost_estimate=pl.CostEstimate(
             flops=4 * requests * model * 64, bytes_accessed=1 << 20, transcendentals=0
         ),
@@ -176,7 +171,6 @@
         *downs,
         *[near(v) for v in mine],
         *[near(v) for v in theirs],
-        far(source),
     )
 
 
@@ -199,21 +193,27 @@
     )(*values)
 
 
+def split_pieces(pieces):
+    pieces = [p if isinstance(p, tuple) else (p, 0, p.shape[0]) for p in pieces]
+    return [p[0] for p in pieces], [p[1:] for p in pieces]
+
+
 def piecewise(tokens, pieces, start, here):
     total = None
-    for piece in pieces:
-        rows = piece.shape[0]
+    for piece, (first, rows) in pieces:
         term = jnp.dot(
-            tokens[:, start : start + rows], piece[:, here], preferred_element_type=jnp.float32
+            tokens[:, start : start + rows],
+            piece[first : first + rows, here],
+            preferred_element_type=jnp.float32,
         )
         total = term if total is None else total + term
         start += rows
     return total
 
 
-def multiply_kernel(start, n, begun, fetched, *refs):
+def multiply_kernel(start, parts, begun, fetched, *refs):
     tokens, refs = refs[1], refs[2:]
-    pieces, refs = refs[:n], refs[n:]
+    pieces, refs = list(zip(refs, parts)), refs[len(parts) :]
     before, refs = refs[:begun], refs[begun:]
     copies = []
     if fetched:
@@ -227,9 +227,8 @@
     for copy in copies:
         copy.start()
 
-    @pl.loop(0, out.shape[1] // TILE)
-    def _(i):
-        here = pl.ds(pl.multiple_of(i * TILE, TILE), TILE)
+    for first in range(0, out.shape[1], WIDE):
+        here = pl.ds(first, min(WIDE, out.shape[1] - first))
         total = piecewise(tokens, pieces, start, here)
         if begun:
             total = total + before[0][:, here]
@@ -241,6 +240,7 @@
 
 def multiply(after, tokens, pieces, start, begun, fetched, name):
     requests = tokens.shape[0]
+    pieces, parts = split_pieces(pieces)
     hidden = pieces[0].shape[1]
     out_shape = [pltpu.VMEM((requests, hidden), jnp.float32)]
     out_shape += [pltpu.VMEM((rows, hidden), source.dtype) for source, first, rows in fetched]
@@ -251,7 +251,7 @@
         functools.partial(
             multiply_kernel,
             start,
-            len(pieces),
+            parts,
             len(begun),
             [(first, rows) for source, first, rows in fetched],
         ),
@@ -260,7 +260,7 @@
         out_specs=[NEAR] * len(out_shape),
         scratch_shapes=[pltpu.SemaphoreType.DMA((len(fetched),))] if fetched else [],
         cost_estimate=pl.CostEstimate(
-            flops=2 * requests * sum(p.shape[0] for p in pieces) * hidden,
+            flops=2 * requests * sum(rows for first, rows in parts) * hidden,
             bytes_accessed=16 << 20,
             transcendentals=0,
         ),
@@ -269,8 +269,8 @@
     )(*operands)
 
 
-def finish_kernel(start, n, m, index, tokens, adapter_up, gate_pre, up_pre, *refs):
-    pieces, refs = refs[:n], refs[n:]
+def finish_kernel(start, parts, m, index, tokens, adapter_up, gate_pre, up_pre, *refs):
+    pieces, refs = list(zip(refs, parts)), refs[len(parts) :]
     lows, refs = refs[:m], refs[m:]
     out, expanded = refs
     rank = lows[0].shape[1]
@@ -288,9 +288,8 @@
             relative == i * group, wide, 0.0
         ).astype(jnp.bfloat16)
 
-    @pl.loop(0, out.shape[1] // TILE)
-    def _(i):
-        here = pl.ds(pl.multiple_of(i * TILE, TILE), TILE)
+    for first in range(0, out.shape[1], WIDE):
+        here = pl.ds(first, min(WIDE, out.shape[1] - first))
         up = up_pre[:, here] + piecewise(tokens, pieces, start, here)
         up = up + jnp.dot(expanded[...], adapter_up[:, here], preferred_element_type=jnp.float32)
         gate = gate_pre[:, here]
@@ -299,9 +298,10 @@
 
 def finish(index, tokens, adapter_up, gate_pre, up_pre, pieces, start, lows):
     requests = tokens.shape[0]
+    pieces, parts = split_pieces(pieces)
     hidden = adapter_up.shape[1]
     return pl.pallas_call(
-        functools.partial(finish_kernel, start, len(pieces), len(lows)),
+        functools.partial(finish_kernel, start, parts, len(lows)),
         out_shape=jax.ShapeDtypeStruct((requests, hidden), jnp.bfloat16),
         in_specs=[NEAR] * (5 + len(pieces) + len(lows)),
         out_specs=NEAR,
@@ -309,7 +309,7 @@
             pltpu.VMEM((requests, adapter_up.shape[0]), jnp.bfloat16),
         ],
         cost_estimate=pl.CostEstimate(
-            flops=2 * requests * sum(p.shape[0] for p in pieces) * hidden,
+            flops=2 * requests * sum(rows for first, rows in parts) * hidden,
             bytes_accessed=4 << 20,
             transcendentals=requests * hidden,
         ),
@@ -337,26 +337,24 @@
     own = tokens[None]
     core, column, line_1, line_2 = 1, 2, 2 * width, 4 * width
 
+    block_2 = swap(own, line_2)
     block_1 = swap(own, line_1)
-    block_2 = swap(own, line_2)
     column_0 = swap(own, column)
     core_down = swap(down, core)
-    gate_0 = fetch(gate_weight, 0, part, "fetch_0")
-    block_1 = tie(block_1, [gate_0, column_0])
-    column_1 = swap(block_1, column)
-    gate_1 = fetch(gate_weight, part, part, "fetch_1", [block_1, core_down])
-    block_2 = tie(block_2, [gate_1, column_1])
+    gate_0 = fetch(gate_weight, 0, 6 * unit, "fetch_0")
+    block_2 = tie(block_2, [gate_0])
     block_3 = swap(block_2, line_1)
-    column_2 = swap(block_2, column)
-    gate_2 = fetch(gate_weight, 2 * part, part, "fetch_2", [block_2])
-    block_3 = tie(block_3, [gate_2, column_2])
+    blocks_12 = pack([block_1, block_2], [gate_0, column_0, core_down])
+    columns_12 = swap(blocks_12, column)
+    gate_1 = fetch(gate_weight, 6 * unit, 4 * unit, "fetch_1", [blocks_12])
+    block_3 = tie(block_3, [gate_1])
     column_3 = swap(block_3, column)
-    line = pack([own, block_1, block_2, block_3], [])
+    line = pack([own, blocks_12, block_3], [])
     core_line = swap(line, core)
-    gate_3 = fetch(gate_weight, 3 * part, part, "fetch_3", [line])
-    columns = pack([column_0, column_1, column_2, column_3], [gate_3])
+    gate_2 = fetch(gate_weight, 10 * unit, 6 * unit, "fetch_2", [line])
+    columns = pack([column_0, columns_12, column_3], [gate_2])
     core_columns = swap(columns, core)
-    packed, low, up_0 = collect(
+    packed, low = collect(
         placement[None, :],
         index,
         [down, core_down],
@@ -364,34 +362,33 @@
         [core_line, core_columns],
         depth,
         width,
-        (up_weight, 0, 2 * unit),
     )
 
     low_1 = add(low, swap(low, line_2))
-    gate_pre, up_1 = multiply(
-        low, packed, [gate_0, gate_1], 0, [], [(up_weight, 2 * unit, 5 * unit)], "gate_a"
+    gate_pre, up_0 = multiply(
+        low, packed, [gate_0, (gate_1, 0, 2 * unit)], 0, [], [(up_weight, 0, 6 * unit)], "gate_a"
     )
     low_2 = add(low_1, swap(low_1, line_1))
-    gate_pre, up_2, up_3 = multiply(
+    gate_pre, up_1, up_2 = multiply(
         low_1,
         packed,
-        [gate_2, gate_3],
+        [(gate_1, 2 * unit, 2 * unit), gate_2],
         2 * part,
         [gate_pre],
-        [(up_weight, 7 * unit, unit), (up_weight, 8 * unit, part)],
+        [(up_weight, 6 * unit, 2 * unit), (up_weight, 8 * unit, 4 * unit)],
         "gate_b",
     )
     lows = [low_2, swap(low_2, column)]
-    up_pre, near_up, up_4 = multiply(
+    up_pre, near_up, up_3 = multiply(
         low_2,
         packed,
-        [up_0, up_1, up_2],
+        [up_0, up_1],
         0,
         [],
         [(up, 0, up.shape[0]), (up_weight, 3 * part, part)],
         "up_a",
     )
-    return finish(index, packed, near_up, gate_pre, up_pre, [up_3, up_4], 2 * part, lows)
+    return finish(index, packed, near_up, gate_pre, up_pre, [up_2, up_3], 2 * part, lows)
 
 
 def streamed(

time: 52.5 us -> 51 us (0.971)
  waiting for transfers between devices: 5.72 us -> 3.15 us
  Pallas kernels: 31.4 us -> 32.2 us
    ppermute x13 -> x12, waiting for transfers between devices: 5.72 us -> 3.15 us  [swap(): return lax.ppermute(value, 'tensor', pairs)]
    pallas_call x5, Pallas kernels: 18.5 us -> 20.4 us  [the longest x3 15.3 us: multiply(): pl.pallas_call(functools.partial(multiply_kernel, start, parts, len(begun...]
    pallas_call x4 -> x3, Pallas kernels: 12.7 us -> 11.7 us  [fetch(): pl.pallas_call(functools.partial(fetch_kernel, start, len(after)), out_sh...]
    ppermute x13 -> x12, starting transfers between devices: 15 us -> 15.2 us  [swap(): return lax.ppermute(value, 'tensor', pairs)]
  transfers between devices with their start and end apart: 13 -> 12, of which waited for: 5 -> 4; matrix products, arithmetic and copies ran while one was open for 0% -> 0% of each run, Pallas kernels for 46% -> 53%
where the time goes in v5:
time: 51 us; the launch traced here: 50.8 us
  Pallas kernels  32.2 us (63%)
  starting transfers between devices  15.2 us (30%)
  waiting for transfers between devices  3.15 us (6%)
    pallas_call x3, Pallas kernels, multiply(): pl.pallas_call(functools.partial(multiply_kernel, start, parts, len(begun...  15.3 us
    ppermute x12, starting transfers between devices, swap(): return lax.ppermute(value, 'tensor', pairs)  15.2 us
    pallas_call x3, Pallas kernels, fetch(): pl.pallas_call(functools.partial(fetch_kernel, start, len(after)), out_sh...  11.7 us
    pallas_call x1, Pallas kernels, finish(): pl.pallas_call(functools.partial(finish_kernel, start, parts, len(lows)),...  3.35 us
    ppermute x12, waiting for transfers between devices, swap(): return lax.ppermute(value, 'tensor', pairs)  3.15 us
    pallas_call x1, Pallas kernels, collect(): pl.pallas_call(functools.partial(collect_kernel, depth, width, sizes), ou...  1.72 us
  transfers between devices with their start and end apart: 12, of which 4 were waited for; matrix products, arithmetic and copies ran while one was open for 0% of the time, Pallas kernels for 53%

profile of v5, /device:TPU:0, one launch (start us, length us, event | category | flops | bytes accessed | tf_op | source)
XLA Modules:
  0.0 50.8 jit_solution(15062527606269895810)
XLA Ops:
  0.0 0.5 collective-permute-start
  0.5 3.6 %collective-permute-start.2 = (bf16[1,8,8192]{2,1,0:T(8,128)(2,1)}, bf16[1,8,8192]{2,1,0:T(8,128)(2,1)S(1)}, u32[]{:S(2)}, u32[]{:S(2)}) collective-permute-start(bf16[1,8,8192]{2,1,0:T(8,128)(2,1)} %bitcast.9), channel_id=1, source_target_pairs={{0,8},{1,9},{2,10},{3,11},{4,12},{5,13},{6,14},{7,15},{8,0},{9,1},... | collective-permute-start | bytes 393224 | tf_op jit(solution)/shard_map/ppermute | solution.py:45
  4.0 1.5 %collective-permute-start.3 = (bf16[1,8,8192]{2,1,0:T(8,128)(2,1)}, bf16[1,8,8192]{2,1,0:T(8,128)(2,1)S(1)}, u32[]{:S(2)}, u32[]{:S(2)}) collective-permute-start(bf16[1,8,8192]{2,1,0:T(8,128)(2,1)} %bitcast.10), channel_id=1, source_target_pairs={{0,2},{1,3},{2,0},{3,1},{4,6},{5,7},{6,4},{7,5},{8,10},{9,11},{10,... | collective-permute-start | bytes 393224 | tf_op jit(solution)/shard_map/ppermute | solution.py:45
  5.6 1.6 %collective-permute-start.1 = (bf16[1,8,8192]{2,1,0:T(8,128)(2,1)}, bf16[1,8,8192]{2,1,0:T(8,128)(2,1)S(1)}, u32[]{:S(2)}, u32[]{:S(2)}) collective-permute-start(bf16[1,8,8192]{2,1,0:T(8,128)(2,1)} %bitcast.11), channel_id=1, source_target_pairs={{0,4},{1,5},{2,6},{3,7},{4,0},{5,1},{6,2},{7,3},{8,12},{9,13},{10,... | collective-permute-start | bytes 393224 | tf_op jit(solution)/shard_map/ppermute | solution.py:45
  7.1 4.2 %fetch_0.1.refs_1_.refs_2_ = bf16[3072,1792]{1,0:T(8,128)(2,1)S(1)} custom-call(bf16[8192,1792]{1,0:T(8,128)(2,1)} %source.5), custom_call_target="tpu_custom_call" | custom-call | bytes 11010048 | tf_op jit(solution)/shard_map/fetch_0/pallas_call | solution.py:64
  11.4 0.7 %collective-permute-start.4 = (bf16[1,8,8192]{2,1,0:T(8,128)(2,1)S(1)}, bf16[1,8,8192]{2,1,0:T(8,128)(2,1)S(1)}, u32[]{:S(2)}, u32[]{:S(2)}) collective-permute-start(bf16[1,8,8192]{2,1,0:T(8,128)(2,1)S(1)} %tie.2.refs_1_), channel_id=1, source_target_pairs={{0,4},{1,5},{2,6},{3,7},{4,0},{5,1},{6,2},{7,3},{8,12},{9,13},{10,... | collective-permute-start | bytes 393224 | tf_op jit(solution)/shard_map/ppermute | solution.py:45
  12.1 0.7 %collective-permute-done.1.refs_0_ = bf16[1,8,8192]{2,1,0:T(8,128)(2,1)S(1)} collective-permute-done((bf16[1,8,8192]{2,1,0:T(8,128)(2,1)}, bf16[1,8,8192]{2,1,0:T(8,128)(2,1)S(1)}, u32[]{:S(2)}, u32[]{:S(2)}) %collective-permute-start.1) | collective-permute-done | bytes 131104 | tf_op jit(solution)/shard_map/ppermute | solution.py:45
  12.8 0.9 %collective-permute-start.5 = (bf16[2,8,8192]{2,1,0:T(8,128)(2,1)S(1)}, bf16[2,8,8192]{2,1,0:T(8,128)(2,1)S(1)}, u32[]{:S(2)}, u32[]{:S(2)}) collective-permute-start(bf16[2,8,8192]{2,1,0:T(8,128)(2,1)S(1)} %pack.3.refs_0_.refs_1_), channel_id=1, source_target_pairs={{0,2},{1,3},{2,0},{3,1},{4,6},{5,7},{6,4},{7,5},{8,10},{9,11},{10,... | collective-permute-start | bytes 786440 | tf_op jit(solution)/shard_map/ppermute | solution.py:45
  13.7 3.2 %fetch_1.1.refs_1_.refs_3_.refs_2_ = bf16[2048,1792]{1,0:T(8,128)(2,1)S(1)} custom-call(bf16[8192,1792]{1,0:T(8,128)(2,1)} %source.5, bf16[2,8,8192]{2,1,0:T(8,128)(2,1)S(1)} %pack.3.refs_0_.refs_1_), custom_call_target="tpu_custom_call" | custom-call | bytes 7340032 | tf_op jit(solution)/shard_map/fetch_1/pallas_call | solution.py:64
  16.9 1.3 %collective-permute-start.6 = (bf16[1,8,8192]{2,1,0:T(8,128)(2,1)S(1)}, bf16[1,8,8192]{2,1,0:T(8,128)(2,1)S(1)}, u32[]{:S(2)}, u32[]{:S(2)}) collective-permute-start(bf16[1,8,8192]{2,1,0:T(8,128)(2,1)S(1)} %tie.3.refs_2_), channel_id=1, source_target_pairs={{0,2},{1,3},{2,0},{3,1},{4,6},{5,7},{6,4},{7,5},{8,10},{9,11},{10,... | collective-permute-start | bytes 393224 | tf_op jit(solution)/shard_map/ppermute | solution.py:45
  18.2 4.2 %fetch_2.1.refs_3_ = bf16[3072,1792]{1,0:T(8,128)(2,1)S(1)} custom-call(bf16[8192,1792]{1,0:T(8,128)(2,1)} %source.5, bf16[4,8,8192]{2,1,0:T(8,128)(2,1)S(1)} %pack.4.refs_0_), custom_call_target="tpu_custom_call" | custom-call | bytes 11010048 | tf_op jit(solution)/shard_map/fetch_2/pallas_call | solution.py:64
  22.5 0.1 collective-permute-start.7
  22.6 0.4 collective-permute-done.6.refs_2_
  23.1 0.1 collective-permute-start.8
  23.2 1.3 %collective-permute-done.7.refs_2_ = bf16[4,8,8192]{2,1,0:T(8,128)(2,1)S(1)} collective-permute-done((bf16[4,8,8192]{2,1,0:T(8,128)(2,1)S(1)}, bf16[4,8,8192]{2,1,0:T(8,128)(2,1)S(1)}, u32[]{:S(2)}, u32[]{:S(2)}) %collective-permute-start.7) | collective-permute-done | bytes 524320 | tf_op jit(solution)/shard_map/ppermute | solution.py:45
  24.5 0.7 %collective-permute-done.8.refs_3_ = bf16[4,8,8192]{2,1,0:T(8,128)(2,1)S(1)} collective-permute-done((bf16[4,8,8192]{2,1,0:T(8,128)(2,1)S(1)}, bf16[4,8,8192]{2,1,0:T(8,128)(2,1)S(1)}, u32[]{:S(2)}, u32[]{:S(2)}) %collective-permute-start.8) | collective-permute-done | bytes 524320 | tf_op jit(solution)/shard_map/ppermute | solution.py:45
  25.2 1.7 %collect.1 = (bf16[128,8192]{1,0:T(8,128)(2,1)S(1)}, bf16[128,64]{1,0:T(8,128)(2,1)S(1)}) custom-call(s32[1,16]{1,0:T(1,128)S(1)} %bitcast.15, s32[1,128]{1,0:T(1,128)S(1)} %bitcast.13, bf16[64,8192]{1,0:T(8,128)(2,1)S(1)} %bitcast.8, bf16[64,8192]{1,0:T(8,128)(2,1)S(1)} %collective-permute-done.refs_4_.core_down, bf16[4,8,8192]{2,1,0:T(8,128)(2,1)S(1)} %pack.4.refs_0_, ...), custom_call_target="tpu_custom_call" | custom-call | flops 268435456 | bytes 1048576 | tf_op jit(solution)/shard_map/collect/pallas_call | solution.py:155
  27.0 3.1 %collective-permute-start.9 = (bf16[128,64]{1,0:T(8,128)(2,1)S(1)}, bf16[128,64]{1,0:T(8,128)(2,1)S(1)}, u32[]{:S(2)}, u32[]{:S(2)}) collective-permute-start(bf16[128,64]{1,0:T(8,128)(2,1)S(1)} %get-tuple-element.16.refs_0_), channel_id=1, source_target_pairs={{0,8},{1,9},{2,10},{3,11},{4,12},{5,13},{6,14},{7,15},{8,0},{9,1},... | collective-permute-start | bytes 49160 | tf_op jit(solution)/shard_map/ppermute | solution.py:45
  30.1 4.1 %gate_a.1 = (f32[128,1792]{1,0:T(8,128)S(1)}, bf16[3072,1792]{1,0:T(8,128)(2,1)S(1)}) custom-call(bf16[128,64]{1,0:T(8,128)(2,1)S(1)} %get-tuple-element.16.refs_0_, bf16[128,8192]{1,0:T(8,128)(2,1)S(1)} %get-tuple-element.15.refs_1_.tokens, bf16[3072,1792]{1,0:T(8,128)(2,1)S(1)} %fetch_0.1.refs_1_.refs_2_, ...), custom_call_target="tpu_custom_call" | custom-call | flops 1879048192 | bytes 16777216 | tf_op jit(solution)/shard_map/gate_a/pallas_call | solution.py:250
  34.3 1.1 %collective-permute-start.10 = (bf16[128,64]{1,0:T(8,128)(2,1)S(1)}, bf16[128,64]{1,0:T(8,128)(2,1)S(1)}, u32[]{:S(2)}, u32[]{:S(2)}) collective-permute-start(bf16[128,64]{1,0:T(8,128)(2,1)S(1)} %add.2.refs_0_), channel_id=1, source_target_pairs={{0,4},{1,5},{2,6},{3,7},{4,0},{5,1},{6,2},{7,3},{8,12},{9,13},{10,... | collective-permute-start | bytes 49160 | tf_op jit(solution)/shard_map/ppermute | solution.py:45
  35.4 6.1 %gate_b.1 = (f32[128,1792]{1,0:T(8,128)S(1)}, bf16[1024,1792]{1,0:T(8,128)(2,1)S(1)}, bf16[2048,1792]{1,0:T(8,128)(2,1)S(1)}) custom-call(bf16[128,64]{1,0:T(8,128)(2,1)S(1)} %add.2.refs_0_, bf16[128,8192]{1,0:T(8,128)(2,1)S(1)} %get-tuple-element.15.refs_1_.tokens, bf16[2048,1792]{1,0:T(8,128)(2,1)S(1)} %fetch_1.1.refs_1_.refs_3_.refs_2_, ...), custom_call_target="tpu_custom_call" | custom-call | flops 1879048192 | bytes 16777216 | tf_op jit(solution)/shard_map/gate_b/pallas_call | solution.py:250
  41.6 0.8 %collective-permute-start.11 = (bf16[128,64]{1,0:T(8,128)(2,1)S(1)}, bf16[128,64]{1,0:T(8,128)(2,1)S(1)}, u32[]{:S(2)}, u32[]{:S(2)}) collective-permute-start(bf16[128,64]{1,0:T(8,128)(2,1)S(1)} %add.3.refs_0_.refs_2_), channel_id=1, source_target_pairs={{0,2},{1,3},{2,0},{3,1},{4,6},{5,7},{6,4},{7,5},{8,10},{9,11},{10,... | collective-permute-start | bytes 49160 | tf_op jit(solution)/shard_map/ppermute | solution.py:45
  42.4 5.0 %up_a.1 = (f32[128,1792]{1,0:T(8,128)S(1)}, bf16[1024,1792]{1,0:T(8,128)(2,1)S(1)}, bf16[2048,1792]{1,0:T(8,128)(2,1)S(1)}) custom-call(bf16[128,64]{1,0:T(8,128)(2,1)S(1)} %add.3.refs_0_.refs_2_, bf16[128,8192]{1,0:T(8,128)(2,1)S(1)} %get-tuple-element.15.refs_1_.tokens, bf16[3072,1792]{1,0:T(8,128)(2,1)S(1)} %get-tuple-element.17.refs_2_, ...), custom_call_target="tpu_custom_call" | custom-call | flops 1879048192 | bytes 16777216 | tf_op jit(solution)/shard_map/up_a/pallas_call | solution.py:250
  47.4 3.4 %finish.1 = bf16[128,1792]{1,0:T(8,128)(2,1)} custom-call(s32[1,128]{1,0:T(1,128)S(1)} %bitcast.14, bf16[128,8192]{1,0:T(8,128)(2,1)S(1)} %get-tuple-element.15.refs_1_.tokens, bf16[1024,1792]{1,0:T(8,128)(2,1)S(1)} %get-tuple-element.20.adapter_up, f32[128,1792]{1,0:T(8,128)S(1)} %get-tuple-element.21.gate_pre, f32[128,1792]{1,0:T(8,128)S(1)} %get-tuple-element.22.up_pre, ...), custom_call_target="tpu_custom_call" | custom-call | flops 1879048192 | bytes 4194304 | tf_op jit(solution)/shard_map/finish/pallas_call | solution.py:303
  (23 shorter events, 0.2 us)
Async XLA Ops:
  0.0 12.8 %collective-permute-start = (bf16[64,8192]{1,0:T(8,128)(2,1)}, bf16[64,8192]{1,0:T(8,128)(2,1)S(1)}, u32[]{:S(2)}, u32[]{:S(2)}) collective-permute-start(bf16[64,8192]{1,0:T(8,128)(2,1)} %bitcast.7), channel_id=1, source_target_pairs={{0,1},{1,0},{2,3},{3,2},{4,5},{5,4},{6,7},{7,6},{8,9},{9,8},{10,11... | collective-permute-start | bytes 3145736 | tf_op jit(solution)/shard_map/ppermute | solution.py:45
  0.5 10.9 %collective-permute-start.2 = (bf16[1,8,8192]{2,1,0:T(8,128)(2,1)}, bf16[1,8,8192]{2,1,0:T(8,128)(2,1)S(1)}, u32[]{:S(2)}, u32[]{:S(2)}) collective-permute-start(bf16[1,8,8192]{2,1,0:T(8,128)(2,1)} %bitcast.9), channel_id=1, source_target_pairs={{0,8},{1,9},{2,10},{3,11},{4,12},{5,13},{6,14},{7,15},{8,0},{9,1},... | collective-permute-start | bytes 393224 | tf_op jit(solution)/shard_map/ppermute | solution.py:45
  4.0 8.1 %collective-permute-start.3 = (bf16[1,8,8192]{2,1,0:T(8,128)(2,1)}, bf16[1,8,8192]{2,1,0:T(8,128)(2,1)S(1)}, u32[]{:S(2)}, u32[]{:S(2)}) collective-permute-start(bf16[1,8,8192]{2,1,0:T(8,128)(2,1)} %bitcast.10), channel_id=1, source_target_pairs={{0,2},{1,3},{2,0},{3,1},{4,6},{5,7},{6,4},{7,5},{8,10},{9,11},{10,... | collective-permute-start | bytes 393224 | tf_op jit(solution)/shard_map/ppermute | solution.py:45
  5.6 7.2 %collective-permute-start.1 = (bf16[1,8,8192]{2,1,0:T(8,128)(2,1)}, bf16[1,8,8192]{2,1,0:T(8,128)(2,1)S(1)}, u32[]{:S(2)}, u32[]{:S(2)}) collective-permute-start(bf16[1,8,8192]{2,1,0:T(8,128)(2,1)} %bitcast.11), channel_id=1, source_target_pairs={{0,4},{1,5},{2,6},{3,7},{4,0},{5,1},{6,2},{7,3},{8,12},{9,13},{10,... | collective-permute-start | bytes 393224 | tf_op jit(solution)/shard_map/ppermute | solution.py:45
  11.4 5.5 %collective-permute-start.4 = (bf16[1,8,8192]{2,1,0:T(8,128)(2,1)S(1)}, bf16[1,8,8192]{2,1,0:T(8,128)(2,1)S(1)}, u32[]{:S(2)}, u32[]{:S(2)}) collective-permute-start(bf16[1,8,8192]{2,1,0:T(8,128)(2,1)S(1)} %tie.2.refs_1_), channel_id=1, source_target_pairs={{0,4},{1,5},{2,6},{3,7},{4,0},{5,1},{6,2},{7,3},{8,12},{9,13},{10,... | collective-permute-start | bytes 393224 | tf_op jit(solution)/shard_map/ppermute | solution.py:45
  12.8 10.2 %collective-permute-start.5 = (bf16[2,8,8192]{2,1,0:T(8,128)(2,1)S(1)}, bf16[2,8,8192]{2,1,0:T(8,128)(2,1)S(1)}, u32[]{:S(2)}, u32[]{:S(2)}) collective-permute-start(bf16[2,8,8192]{2,1,0:T(8,128)(2,1)S(1)} %pack.3.refs_0_.refs_1_), channel_id=1, source_target_pairs={{0,2},{1,3},{2,0},{3,1},{4,6},{5,7},{6,4},{7,5},{8,10},{9,11},{10,... | collective-permute-start | bytes 786440 | tf_op jit(solution)/shard_map/ppermute | solution.py:45
  16.9 1.3 %copy-start.1 = (bf16[8,8192]{1,0:T(8,128)(2,1)S(1)}, bf16[8,8192]{1,0:T(8,128)(2,1)}, u32[]{:S(2)}) copy-start(bf16[8,8192]{1,0:T(8,128)(2,1)} %param.8) | copy-start | bytes 393220
  16.9 6.1 %collective-permute-start.6 = (bf16[1,8,8192]{2,1,0:T(8,128)(2,1)S(1)}, bf16[1,8,8192]{2,1,0:T(8,128)(2,1)S(1)}, u32[]{:S(2)}, u32[]{:S(2)}) collective-permute-start(bf16[1,8,8192]{2,1,0:T(8,128)(2,1)S(1)} %tie.3.refs_2_), channel_id=1, source_target_pairs={{0,2},{1,3},{2,0},{3,1},{4,6},{5,7},{6,4},{7,5},{8,10},{9,11},{10,... | collective-permute-start | bytes 393224 | tf_op jit(solution)/shard_map/ppermute | solution.py:45
  22.5 2.8 %copy-start = (bf16[1,8192,64]{1,2,0:T(8,128)(2,1)S(1)}, bf16[1,8192,64]{1,2,0:T(8,128)(2,1)}, u32[]{:S(2)}) copy-start(bf16[1,8192,64]{1,2,0:T(8,128)(2,1)} %param.11) | copy-start | bytes 3145732
  22.5 2.8 %copy-start.2 = (s32[128]{0:T(128)S(1)}, s32[128]{0:T(128)}, u32[]{:S(2)}) copy-start(s32[128]{0:T(128)} %param.13) | copy-start | bytes 1540
  22.5 2.7 %copy-start.3 = (s32[16]{0:T(128)S(1)}, s32[16]{0:T(128)}, u32[]{:S(2)}) copy-start(s32[16]{0:T(128)} %param.14) | copy-start | bytes 196
  22.5 2.0 %collective-permute-start.7 = (bf16[4,8,8192]{2,1,0:T(8,128)(2,1)S(1)}, bf16[4,8,8192]{2,1,0:T(8,128)(2,1)S(1)}, u32[]{:S(2)}, u32[]{:S(2)}) collective-permute-start(bf16[4,8,8192]{2,1,0:T(8,128)(2,1)S(1)} %pack.4.refs_0_), channel_id=1, source_target_pairs={{0,1},{1,0},{2,3},{3,2},{4,5},{5,4},{6,7},{7,6},{8,9},{9,8},{10,11... | collective-permute-start | bytes 1572872 | tf_op jit(solution)/shard_map/ppermute | solution.py:45
  23.1 2.2 %collective-permute-start.8 = (bf16[4,8,8192]{2,1,0:T(8,128)(2,1)S(1)}, bf16[4,8,8192]{2,1,0:T(8,128)(2,1)S(1)}, u32[]{:S(2)}, u32[]{:S(2)}) collective-permute-start(bf16[4,8,8192]{2,1,0:T(8,128)(2,1)S(1)} %pack.5.refs_1_), channel_id=1, source_target_pairs={{0,1},{1,0},{2,3},{3,2},{4,5},{5,4},{6,7},{7,6},{8,9},{9,8},{10,11... | collective-permute-start | bytes 1572872 | tf_op jit(solution)/shard_map/ppermute | solution.py:45
  27.0 7.3 %collective-permute-start.9 = (bf16[128,64]{1,0:T(8,128)(2,1)S(1)}, bf16[128,64]{1,0:T(8,128)(2,1)S(1)}, u32[]{:S(2)}, u32[]{:S(2)}) collective-permute-start(bf16[128,64]{1,0:T(8,128)(2,1)S(1)} %get-tuple-element.16.refs_0_), channel_id=1, source_target_pairs={{0,8},{1,9},{2,10},{3,11},{4,12},{5,13},{6,14},{7,15},{8,0},{9,1},... | collective-permute-start | bytes 49160 | tf_op jit(solution)/shard_map/ppermute | solution.py:45
  34.3 7.3 %collective-permute-start.10 = (bf16[128,64]{1,0:T(8,128)(2,1)S(1)}, bf16[128,64]{1,0:T(8,128)(2,1)S(1)}, u32[]{:S(2)}, u32[]{:S(2)}) collective-permute-start(bf16[128,64]{1,0:T(8,128)(2,1)S(1)} %add.2.refs_0_), channel_id=1, source_target_pairs={{0,4},{1,5},{2,6},{3,7},{4,0},{5,1},{6,2},{7,3},{8,12},{9,13},{10,... | collective-permute-start | bytes 49160 | tf_op jit(solution)/shard_map/ppermute | solution.py:45
  41.6 5.8 %collective-permute-start.11 = (bf16[128,64]{1,0:T(8,128)(2,1)S(1)}, bf16[128,64]{1,0:T(8,128)(2,1)S(1)}, u32[]{:S(2)}, u32[]{:S(2)}) collective-permute-start(bf16[128,64]{1,0:T(8,128)(2,1)S(1)} %add.3.refs_0_.refs_2_), channel_id=1, source_target_pairs={{0,2},{1,3},{2,0},{3,1},{4,6},{5,7},{6,4},{7,5},{8,10},{9,11},{10,... | collective-permute-start | bytes 49160 | tf_op jit(solution)/shard_map/ppermute | solution.py:45

commit v6 on v5

--- a/solution.py
+++ b/solution.py
@@ -9,7 +9,7 @@
 
 TILE = 256
 WIDE = 512
-PIECES = 4
+PIECES = 8
 NEAR = pl.BlockSpec(memory_space=pltpu.VMEM)
 FAR = pl.BlockSpec(memory_space=pl.ANY)
 STORED = pl.BlockSpec(memory_space=pltpu.HBM)
@@ -45,30 +45,33 @@
     return lax.ppermute(value, "tensor", pairs)
 
 
-def fetch_kernel(start, skipped, source, *refs):
-    target, sems = refs[skipped:]
-    rows = target.shape[0] // sems.shape[0]
-    copies = [
-        pltpu.make_async_copy(
-            source.at[pl.ds(start + i * rows, rows)], target.at[pl.ds(i * rows, rows)], sems.at[i]
-        )
-        for i in range(sems.shape[0])
+def copies_of(sources, firsts, targets, sems):
+    return [
+        pltpu.make_async_copy(source.at[pl.ds(first, target.shape[0])], target, sems.at[i])
+        for i, (source, first, target) in enumerate(zip(sources, firsts, targets))
     ]
+
+
+def fetch_kernel(firsts, skipped, source, *refs):
+    *targets, sems = refs[skipped:]
+    copies = copies_of([source] * len(targets), firsts, targets, sems)
     for copy in copies:
         copy.start()
     for copy in copies:
         copy.wait()
 
 
-def fetch(weight, start, rows, name, after=()):
-    return pl.pallas_call(
-        functools.partial(fetch_kernel, start, len(after)),
-        out_shape=pltpu.VMEM((rows, weight.shape[1]), weight.dtype),
+def fetch(weight, firsts, rows, name, after=()):
+    return pl.pallas_call(
+        functools.partial(fetch_kernel, firsts, len(after)),
+        out_shape=[pltpu.VMEM((rows, weight.shape[1]), weight.dtype)] * len(firsts),
         in_specs=[STORED] + [FAR] * len(after),
-        out_specs=NEAR,
-        scratch_shapes=[pltpu.SemaphoreType.DMA((4,))],
+        out_specs=[NEAR] * len(firsts),
+        scratch_shapes=[pltpu.SemaphoreType.DMA((len(firsts),))],
         cost_estimate=pl.CostEstimate(
-            flops=0, bytes_accessed=rows * weight.shape[1] * 2, transcendentals=0
+            flops=0,
+            bytes_accessed=len(firsts) * rows * weight.shape[1] * 2,
+            transcendentals=0,
         ),
         compiler_params=pltpu.CompilerParams(vmem_limit_bytes=1 << 20),
         name=name,
@@ -119,9 +122,31 @@
     )(value, *after)
 
 
-def collect_kernel(depth, width, sizes, placement, index, down, core_down, *refs):
+def piecewise(tokens, pieces, start, here):
+    total = None
+    for piece in pieces:
+        rows = piece.shape[0]
+        term = jnp.dot(
+            tokens[:, start : start + rows], piece[:, here], preferred_element_type=jnp.float32
+        )
+        total = term if total is None else total + term
+        start += rows
+    return total
+
+
+def columns_of(ref):
+    width = ref.shape[1]
+    return [pl.ds(i, min(WIDE, width - i)) for i in range(0, width, WIDE)]
+
+
+def collect_kernel(depth, width, sizes, n, firsts, placement, index, down, core_down, *refs):
     mine, theirs = refs[: len(sizes)], refs[len(sizes) : 2 * len(sizes)]
-    packed, low = refs[2 * len(sizes) :]
+    refs = refs[2 * len(sizes) :]
+    pieces, refs = refs[:n], refs[n:]
+    source, packed, low, out, *targets, sems = refs
+    copies = copies_of([source] * len(targets), firsts, targets, sems)
+    for copy in copies:
+        copy.start()
     own = lax.axis_index("tensor")
     c = own % 2
     rows = packed.shape[0] // (2 * depth * width)
@@ -146,24 +171,35 @@
         chosen = across(jnp.where(index[...] == owner, 1, 0))[:, : full.shape[1]]
         total = jnp.where(chosen == 1, full, 0.0 if total is None else total)
     low[...] = total.astype(low.dtype)
-
-
-def collect(placement, index, downs, mine, theirs, depth, width):
+    for here in columns_of(out):
+        out[:, here] = piecewise(packed, pieces, 0, here)
+    for copy in copies:
+        copy.wait()
+
+
+def collect(placement, index, downs, mine, theirs, depth, width, pieces, fetched):
     sizes = [v.shape[0] for v in mine]
     rows, model = mine[0].shape[1:]
     requests = 2 * depth * width * rows
-    return pl.pallas_call(
-        functools.partial(collect_kernel, depth, width, sizes),
+    source, firsts, fetched_rows = fetched
+    hidden = source.shape[1]
+    return pl.pallas_call(
+        functools.partial(collect_kernel, depth, width, sizes, len(pieces), firsts),
         out_shape=[
             pltpu.VMEM((requests, model), jnp.bfloat16),
             jax.ShapeDtypeStruct((requests, downs[0].shape[0]), jnp.bfloat16),
-        ],
-        in_specs=[NEAR] * (4 + 2 * len(sizes)),
-        out_specs=[NEAR] * 2,
+            pltpu.VMEM((requests, hidden), jnp.float32),
+        ]
+        + [pltpu.VMEM((fetched_rows, hidden), source.dtype)] * len(firsts),
+        in_specs=[NEAR] * (4 + 2 * len(sizes) + len(pieces)) + [STORED],
+        out_specs=[NEAR] * (3 + len(firsts)),
+        scratch_shapes=[pltpu.SemaphoreType.DMA((len(firsts),))],
         cost_estimate=pl.CostEstimate(
-            flops=4 * requests * model * 64, bytes_accessed=1 << 20, transcendentals=0
+            flops=2 * requests * hidden * sum(p.shape[0] for p in pieces),
+            bytes_accessed=16 << 20,
+            transcendentals=0,
         ),
-        compiler_params=pltpu.CompilerParams(vmem_limit_bytes=4 << 20),
+        compiler_params=pltpu.CompilerParams(vmem_limit_bytes=2 << 20),
         name="collect",
     )(
         placement,
@@ -171,6 +207,8 @@
         *downs,
         *[near(v) for v in mine],
         *[near(v) for v in theirs],
+        *[near(p) for p in pieces],
+        far(source),
     )
 
 
@@ -193,74 +231,41 @@
     )(*values)
 
 
-def split_pieces(pieces):
-    pieces = [p if isinstance(p, tuple) else (p, 0, p.shape[0]) for p in pieces]
-    return [p[0] for p in pieces], [p[1:] for p in pieces]
-
-
-def piecewise(tokens, pieces, start, here):
-    total = None
-    for piece, (first, rows) in pieces:
-        term = jnp.dot(
-            tokens[:, start : start + rows],
-            piece[first : first + rows, here],
-            preferred_element_type=jnp.float32,
-        )
-        total = term if total is None else total + term
-        start += rows
-    return total
-
-
-def multiply_kernel(start, parts, begun, fetched, *refs):
+def multiply_kernel(start, n, begun, firsts, *refs):
     tokens, refs = refs[1], refs[2:]
-    pieces, refs = list(zip(refs, parts)), refs[len(parts) :]
+    pieces, refs = refs[:n], refs[n:]
     before, refs = refs[:begun], refs[begun:]
-    copies = []
-    if fetched:
-        sources, (out, *targets, sems) = refs[: len(fetched)], refs[len(fetched) :]
-        for i, ((first, rows), source, target) in enumerate(zip(fetched, sources, targets)):
-            copies.append(
-                pltpu.make_async_copy(source.at[pl.ds(first, rows)], target, sems.at[i])
-            )
-    else:
-        (out,) = refs
+    sources, (out, *targets) = refs[: len(firsts)], refs[len(firsts) :]
+    copies = copies_of(sources, firsts, targets[:-1], targets[-1]) if firsts else []
     for copy in copies:
         copy.start()
-
-    for first in range(0, out.shape[1], WIDE):
-        here = pl.ds(first, min(WIDE, out.shape[1] - first))
+    for here in columns_of(out):
         total = piecewise(tokens, pieces, start, here)
         if begun:
             total = total + before[0][:, here]
         out[:, here] = total
-
     for copy in copies:
         copy.wait()
 
 
-def multiply(after, tokens, pieces, start, begun, fetched, name):
+def multiply(after, tokens, pieces, start, begun, fetched, rows, name):
     requests = tokens.shape[0]
-    pieces, parts = split_pieces(pieces)
     hidden = pieces[0].shape[1]
-    out_shape = [pltpu.VMEM((requests, hidden), jnp.float32)]
-    out_shape += [pltpu.VMEM((rows, hidden), source.dtype) for source, first, rows in fetched]
+    n = len(fetched)
     operands = [after, near(tokens)] + [near(p) for p in pieces] + [near(b) for b in begun]
-    in_specs = [FAR] + [NEAR] * (len(operands) - 1) + [STORED] * len(fetched)
-    operands += [far(source) for source, first, rows in fetched]
+    in_specs = [FAR] + [NEAR] * (len(operands) - 1) + [STORED] * n
+    operands += [far(source) for source, first in fetched]
     return pl.pallas_call(
         functools.partial(
-            multiply_kernel,
-            start,
-            parts,
-            len(begun),
-            [(first, rows) for source, first, rows in fetched],
+            multiply_kernel, start, len(pieces), len(begun), [first for source, first in fetched]
         ),
-        out_shape=out_shape,
+        out_shape=[pltpu.VMEM((requests, hidden), jnp.float32)]
+        + [pltpu.VMEM((rows, hidden), tokens.dtype)] * n,
         in_specs=in_specs,
-        out_specs=[NEAR] * len(out_shape),
-        scratch_shapes=[pltpu.SemaphoreType.DMA((len(fetched),))] if fetched else [],
+        out_specs=[NEAR] * (1 + n),
+        scratch_shapes=[pltpu.SemaphoreType.DMA((n,))] if n else [],
         cost_estimate=pl.CostEstimate(
-            flops=2 * requests * sum(rows for first, rows in parts) * hidden,
+            flops=2 * requests * sum(p.shape[0] for p in pieces) * hidden,
             bytes_accessed=16 << 20,
             transcendentals=0,
         ),
@@ -269,10 +274,8 @@
     )(*operands)
 
 
-def finish_kernel(start, parts, m, index, tokens, adapter_up, gate_pre, up_pre, *refs):
-    pieces, refs = list(zip(refs, parts)), refs[len(parts) :]
-    lows, refs = refs[:m], refs[m:]
-    out, expanded = refs
+def finish_kernel(m, index, adapter_up, gate_pre, up_pre, *refs):
+    lows, (out, expanded) = refs[:m], refs[m:]
     rank = lows[0].shape[1]
     mixed = lows[0][...]
     for low in lows[1:]:
@@ -288,50 +291,36 @@
             relative == i * group, wide, 0.0
         ).astype(jnp.bfloat16)
 
-    for first in range(0, out.shape[1], WIDE):
-        here = pl.ds(first, min(WIDE, out.shape[1] - first))
-        up = up_pre[:, here] + piecewise(tokens, pieces, start, here)
-        up = up + jnp.dot(expanded[...], adapter_up[:, here], preferred_element_type=jnp.float32)
+    for here in columns_of(out):
+        delta = jnp.dot(expanded[...], adapter_up[:, here], preferred_element_type=jnp.float32)
         gate = gate_pre[:, here]
-        out[:, here] = (gate / (1.0 + jnp.exp(-gate)) * up).astype(out.dtype)
-
-
-def finish(index, tokens, adapter_up, gate_pre, up_pre, pieces, start, lows):
-    requests = tokens.shape[0]
-    pieces, parts = split_pieces(pieces)
-    hidden = adapter_up.shape[1]
-    return pl.pallas_call(
-        functools.partial(finish_kernel, start, parts, len(lows)),
+        out[:, here] = (gate / (1.0 + jnp.exp(-gate)) * (up_pre[:, here] + delta)).astype(out.dtype)
+
+
+def finish(index, adapter_up, gate_pre, up_pre, lows):
+    requests, hidden = gate_pre.shape
+    return pl.pallas_call(
+        functools.partial(finish_kernel, len(lows)),
         out_shape=jax.ShapeDtypeStruct((requests, hidden), jnp.bfloat16),
-        in_specs=[NEAR] * (5 + len(pieces) + len(lows)),
+        in_specs=[NEAR] * (4 + len(lows)),
         out_specs=NEAR,
-        scratch_shapes=[
-            pltpu.VMEM((requests, adapter_up.shape[0]), jnp.bfloat16),
-        ],
+        scratch_shapes=[pltpu.VMEM((requests, adapter_up.shape[0]), jnp.bfloat16)],
         cost_estimate=pl.CostEstimate(
-            flops=2 * requests * sum(rows for first, rows in parts) * hidden,
+            flops=2 * requests * adapter_up.shape[0] * hidden,
             bytes_accessed=4 << 20,
             transcendentals=requests * hidden,
         ),
-        compiler_params=pltpu.CompilerParams(vmem_limit_bytes=4 << 20),
+        compiler_params=pltpu.CompilerParams(vmem_limit_bytes=2 << 20),
         name="finish",
-    )(
-        index,
-        near(tokens),
-        near(adapter_up),
-        near(gate_pre),
-        near(up_pre),
-        *[near(p) for p in pieces],
-        *lows,
-    )
+    )(index, near(adapter_up), near(gate_pre), near(up_pre), *lows)
 
 
 def on_chip(tokens, gate_weight, up_weight, down, up, request_adapter_index, placement):
     depth, width = plan(lax.axis_size("tensor"))
     model, hidden = gate_weight.shape
     index = request_adapter_index[None, :]
-    part = model // PIECES
-    unit = part // 4
+    unit = model // PIECES
+    firsts = [i * unit for i in range(PIECES)]
     up = up.reshape(-1, hidden)
     down = jnp.swapaxes(down[0], 0, 1)
     own = tokens[None]
@@ -341,20 +330,20 @@
     block_1 = swap(own, line_1)
     column_0 = swap(own, column)
     core_down = swap(down, core)
-    gate_0 = fetch(gate_weight, 0, 6 * unit, "fetch_0")
+    gate_0, gate_1, gate_2 = fetch(gate_weight, firsts[:3], unit, "fetch_0")
     block_2 = tie(block_2, [gate_0])
     block_3 = swap(block_2, line_1)
     blocks_12 = pack([block_1, block_2], [gate_0, column_0, core_down])
     columns_12 = swap(blocks_12, column)
-    gate_1 = fetch(gate_weight, 6 * unit, 4 * unit, "fetch_1", [blocks_12])
-    block_3 = tie(block_3, [gate_1])
+    gate_3, gate_4 = fetch(gate_weight, firsts[3:5], unit, "fetch_1", [blocks_12])
+    block_3 = tie(block_3, [gate_3])
     column_3 = swap(block_3, column)
     line = pack([own, blocks_12, block_3], [])
     core_line = swap(line, core)
-    gate_2 = fetch(gate_weight, 10 * unit, 6 * unit, "fetch_2", [line])
-    columns = pack([column_0, columns_12, column_3], [gate_2])
+    gate_5, gate_6, gate_7 = fetch(gate_weight, firsts[5:], unit, "fetch_2", [line])
+    columns = pack([column_0, columns_12, column_3], [gate_5])
     core_columns = swap(columns, core)
-    packed, low = collect(
+    packed, low, gate_pre, up_0, up_1, up_2 = collect(
         placement[None, :],
         index,
         [down, core_down],
@@ -362,33 +351,35 @@
         [core_line, core_columns],
         depth,
         width,
+        [gate_0, gate_1, gate_2, gate_3],
+        (up_weight, firsts[:3], unit),
     )
 
     low_1 = add(low, swap(low, line_2))
-    gate_pre, up_0 = multiply(
-        low, packed, [gate_0, (gate_1, 0, 2 * unit)], 0, [], [(up_weight, 0, 6 * unit)], "gate_a"
+    gate_pre, up_3, up_4, up_5 = multiply(
+        low,
+        packed,
+        [gate_4, gate_5, gate_6, gate_7],
+        firsts[4],
+        [gate_pre],
+        [(up_weight, first) for first in firsts[3:6]],
+        unit,
+        "gate_b",
     )
     low_2 = add(low_1, swap(low_1, line_1))
-    gate_pre, up_1, up_2 = multiply(
+    up_pre, near_up, up_6, up_7 = multiply(
         low_1,
         packed,
-        [(gate_1, 2 * unit, 2 * unit), gate_2],
-        2 * part,
-        [gate_pre],
-        [(up_weight, 6 * unit, 2 * unit), (up_weight, 8 * unit, 4 * unit)],
-        "gate_b",
-    )
-    lows = [low_2, swap(low_2, column)]
-    up_pre, near_up, up_3 = multiply(
-        low_2,
-        packed,
-        [up_0, up_1],
+        [up_0, up_1, up_2, up_3, up_4, up_5],
         0,
         [],
-        [(up, 0, up.shape[0]), (up_weight, 3 * part, part)],
+        [(up, 0), (up_weight, firsts[6]), (up_weight, firsts[7])],
+        unit,
         "up_a",
     )
-    return finish(index, packed, near_up, gate_pre, up_pre, [up_2, up_3], 2 * part, lows)
+    lows = [low_2, swap(low_2, column)]
+    (up_pre,) = multiply(low_2, packed, [up_6, up_7], firsts[6], [up_pre], [], 0, "up_b")
+    return finish(index, near_up, gate_pre, up_pre, lows)
 
 
 def streamed(

time: 51 us -> 56.3 us (1.10)
  Pallas kernels: 32.2 us -> 36.1 us
  waiting for transfers between devices: 3.15 us -> 4.49 us
    pallas_call x8, Pallas kernels: 32.1 us -> 36 us  [the longest x3 14.8 us: multiply(): pl.pallas_call(functools.partial(multiply_kernel, start, len(pieces), len...]
    ppermute x12, waiting for transfers between devices: 3.15 us -> 4.49 us  [swap(): return lax.ppermute(value, 'tensor', pairs)]
  transfers between devices with their start and end apart: 12 -> 12, of which waited for: 4 -> 4; matrix products, arithmetic and copies ran while one was open for 0% -> 0% of each run, Pallas kernels for 53% -> 47%
where the time goes in v6:
time: 56.3 us; the launch traced here: 56.2 us
  Pallas kernels  36.1 us (64%)
  starting transfers between devices  15.4 us (27%)
  waiting for transfers between devices  4.49 us (8%)
    ppermute x12, starting transfers between devices, swap(): return lax.ppermute(value, 'tensor', pairs)  15.4 us
    pallas_call x3, Pallas kernels, multiply(): pl.pallas_call(functools.partial(multiply_kernel, start, len(pieces), len...  14.8 us
    pallas_call x3, Pallas kernels, fetch(): pl.pallas_call(functools.partial(fetch_kernel, firsts, len(after)), out_s...  11.6 us
    pallas_call x1, Pallas kernels, collect(): pl.pallas_call(functools.partial(collect_kernel, depth, width, sizes, len...  7.93 us
    ppermute x12, waiting for transfers between devices, swap(): return lax.ppermute(value, 'tensor', pairs)  4.49 us
    pallas_call x1, Pallas kernels, finish(): pl.pallas_call(functools.partial(finish_kernel, len(lows)), out_shape=jax...  1.56 us
  transfers between devices with their start and end apart: 12, of which 4 were waited for; matrix products, arithmetic and copies ran while one was open for 0% of the time, Pallas kernels for 47%

profile of v6, /device:TPU:0, one launch (start us, length us, event | category | flops | bytes accessed | tf_op | source)
XLA Modules:
  0.0 56.2 jit_solution(919035066693659863)
XLA Ops:
  0.0 0.5 collective-permute-start
  0.5 3.6 %collective-permute-start.2 = (bf16[1,8,8192]{2,1,0:T(8,128)(2,1)}, bf16[1,8,8192]{2,1,0:T(8,128)(2,1)S(1)}, u32[]{:S(2)}, u32[]{:S(2)}) collective-permute-start(bf16[1,8,8192]{2,1,0:T(8,128)(2,1)} %bitcast.9), channel_id=1, source_target_pairs={{0,8},{1,9},{2,10},{3,11},{4,12},{5,13},{6,14},{7,15},{8,0},{9,1},... | collective-permute-start | bytes 393224 | tf_op jit(solution)/shard_map/ppermute | solution.py:45
  4.0 1.5 %collective-permute-start.3 = (bf16[1,8,8192]{2,1,0:T(8,128)(2,1)}, bf16[1,8,8192]{2,1,0:T(8,128)(2,1)S(1)}, u32[]{:S(2)}, u32[]{:S(2)}) collective-permute-start(bf16[1,8,8192]{2,1,0:T(8,128)(2,1)} %bitcast.10), channel_id=1, source_target_pairs={{0,2},{1,3},{2,0},{3,1},{4,6},{5,7},{6,4},{7,5},{8,10},{9,11},{10,... | collective-permute-start | bytes 393224 | tf_op jit(solution)/shard_map/ppermute | solution.py:45
  5.6 1.6 %collective-permute-start.1 = (bf16[1,8,8192]{2,1,0:T(8,128)(2,1)}, bf16[1,8,8192]{2,1,0:T(8,128)(2,1)S(1)}, u32[]{:S(2)}, u32[]{:S(2)}) collective-permute-start(bf16[1,8,8192]{2,1,0:T(8,128)(2,1)} %bitcast.11), channel_id=1, source_target_pairs={{0,4},{1,5},{2,6},{3,7},{4,0},{5,1},{6,2},{7,3},{8,12},{9,13},{10,... | collective-permute-start | bytes 393224 | tf_op jit(solution)/shard_map/ppermute | solution.py:45
  7.1 4.2 %fetch_0.1 = (bf16[1024,1792]{1,0:T(8,128)(2,1)S(1)}, bf16[1024,1792]{1,0:T(8,128)(2,1)S(1)}, bf16[1024,1792]{1,0:T(8,128)(2,1)S(1)}) custom-call(bf16[8192,1792]{1,0:T(8,128)(2,1)} %source.5), custom_call_target="tpu_custom_call" | custom-call | bytes 11010048 | tf_op jit(solution)/shard_map/fetch_0/pallas_call | solution.py:65
  11.4 0.7 %collective-permute-start.4 = (bf16[1,8,8192]{2,1,0:T(8,128)(2,1)S(1)}, bf16[1,8,8192]{2,1,0:T(8,128)(2,1)S(1)}, u32[]{:S(2)}, u32[]{:S(2)}) collective-permute-start(bf16[1,8,8192]{2,1,0:T(8,128)(2,1)S(1)} %tie.2.refs_1_), channel_id=1, source_target_pairs={{0,4},{1,5},{2,6},{3,7},{4,0},{5,1},{6,2},{7,3},{8,12},{9,13},{10,... | collective-permute-start | bytes 393224 | tf_op jit(solution)/shard_map/ppermute | solution.py:45
  12.1 0.7 %collective-permute-done.1.refs_0_ = bf16[1,8,8192]{2,1,0:T(8,128)(2,1)S(1)} collective-permute-done((bf16[1,8,8192]{2,1,0:T(8,128)(2,1)}, bf16[1,8,8192]{2,1,0:T(8,128)(2,1)S(1)}, u32[]{:S(2)}, u32[]{:S(2)}) %collective-permute-start.1) | collective-permute-done | bytes 131104 | tf_op jit(solution)/shard_map/ppermute | solution.py:45
  12.8 0.9 %collective-permute-start.5 = (bf16[2,8,8192]{2,1,0:T(8,128)(2,1)S(1)}, bf16[2,8,8192]{2,1,0:T(8,128)(2,1)S(1)}, u32[]{:S(2)}, u32[]{:S(2)}) collective-permute-start(bf16[2,8,8192]{2,1,0:T(8,128)(2,1)S(1)} %pack.3.refs_0_.refs_1_), channel_id=1, source_target_pairs={{0,2},{1,3},{2,0},{3,1},{4,6},{5,7},{6,4},{7,5},{8,10},{9,11},{10,... | collective-permute-start | bytes 786440 | tf_op jit(solution)/shard_map/ppermute | solution.py:45
  13.7 3.2 %fetch_1.1 = (bf16[1024,1792]{1,0:T(8,128)(2,1)S(1)}, bf16[1024,1792]{1,0:T(8,128)(2,1)S(1)}) custom-call(bf16[8192,1792]{1,0:T(8,128)(2,1)} %source.5, bf16[2,8,8192]{2,1,0:T(8,128)(2,1)S(1)} %pack.3.refs_0_.refs_1_), custom_call_target="tpu_custom_call" | custom-call | bytes 7340032 | tf_op jit(solution)/shard_map/fetch_1/pallas_call | solution.py:65
  16.9 1.3 %collective-permute-start.6 = (bf16[1,8,8192]{2,1,0:T(8,128)(2,1)S(1)}, bf16[1,8,8192]{2,1,0:T(8,128)(2,1)S(1)}, u32[]{:S(2)}, u32[]{:S(2)}) collective-permute-start(bf16[1,8,8192]{2,1,0:T(8,128)(2,1)S(1)} %tie.3.refs_2_), channel_id=1, source_target_pairs={{0,2},{1,3},{2,0},{3,1},{4,6},{5,7},{6,4},{7,5},{8,10},{9,11},{10,... | collective-permute-start | bytes 393224 | tf_op jit(solution)/shard_map/ppermute | solution.py:45
  18.2 0.1 collective-permute-start.7
  18.3 4.2 %fetch_2.1 = (bf16[1024,1792]{1,0:T(8,128)(2,1)S(1)}, bf16[1024,1792]{1,0:T(8,128)(2,1)S(1)}, bf16[1024,1792]{1,0:T(8,128)(2,1)S(1)}) custom-call(bf16[8192,1792]{1,0:T(8,128)(2,1)} %source.5, bf16[4,8,8192]{2,1,0:T(8,128)(2,1)S(1)} %pack.4.refs_0_), custom_call_target="tpu_custom_call" | custom-call | bytes 11010048 | tf_op jit(solution)/shard_map/fetch_2/pallas_call | solution.py:65
  22.6 0.5 collective-permute-done.6.refs_2_
  23.1 0.1 collective-permute-start.8
  23.2 1.9 %collective-permute-done.8.refs_3_ = bf16[4,8,8192]{2,1,0:T(8,128)(2,1)S(1)} collective-permute-done((bf16[4,8,8192]{2,1,0:T(8,128)(2,1)S(1)}, bf16[4,8,8192]{2,1,0:T(8,128)(2,1)S(1)}, u32[]{:S(2)}, u32[]{:S(2)}) %collective-permute-start.8) | collective-permute-done | bytes 524320 | tf_op jit(solution)/shard_map/ppermute | solution.py:45
  25.0 7.9 %collect.1 = (bf16[128,8192]{1,0:T(8,128)(2,1)S(1)}, bf16[128,64]{1,0:T(8,128)(2,1)S(1)}, f32[128,1792]{1,0:T(8,128)S(1)}, bf16[1024,1792]{1,0:T(8,128)(2,1)S(1)...) custom-call(s32[1,16]{1,0:T(1,128)S(1)} %bitcast.15, s32[1,128]{1,0:T(1,128)S(1)} %bitcast.13, ...), custom_call_target="tpu_custom_call" | custom-call | flops 1879048192 | bytes 16777216 | tf_op jit(solution)/shard_map/collect/pallas_call | solution.py:186
  33.0 3.3 %collective-permute-start.9 = (bf16[128,64]{1,0:T(8,128)(2,1)S(1)}, bf16[128,64]{1,0:T(8,128)(2,1)S(1)}, u32[]{:S(2)}, u32[]{:S(2)}) collective-permute-start(bf16[128,64]{1,0:T(8,128)(2,1)S(1)} %get-tuple-element.32.refs_0_), channel_id=1, source_target_pairs={{0,8},{1,9},{2,10},{3,11},{4,12},{5,13},{6,14},{7,15},{8,0},{9,1},... | collective-permute-start | bytes 49160 | tf_op jit(solution)/shard_map/ppermute | solution.py:45
  36.3 6.4 %gate_b.1 = (f32[128,1792]{1,0:T(8,128)S(1)}, bf16[1024,1792]{1,0:T(8,128)(2,1)S(1)}, bf16[1024,1792]{1,0:T(8,128)(2,1)S(1)}, bf16[1024,1792]{1,0:T(8,128)(2,1)S(1)}) custom-call(bf16[128,64]{1,0:T(8,128)(2,1)S(1)} %get-tuple-element.32.refs_0_, bf16[128,8192]{1,0:T(8,128)(2,1)S(1)} %get-tuple-element.33.refs_1_, ...), custom_call_target="tpu_custom_call" | custom-call | flops 1879048192 | bytes 16777216 | tf_op jit(solution)/shard_map/gate_b/pallas_call | solution.py:258
  42.7 0.6 %collective-permute-start.10 = (bf16[128,64]{1,0:T(8,128)(2,1)S(1)}, bf16[128,64]{1,0:T(8,128)(2,1)S(1)}, u32[]{:S(2)}, u32[]{:S(2)}) collective-permute-start(bf16[128,64]{1,0:T(8,128)(2,1)S(1)} %add.2.refs_0_), channel_id=1, source_target_pairs={{0,4},{1,5},{2,6},{3,7},{4,0},{5,1},{6,2},{7,3},{8,12},{9,13},{10,... | collective-permute-start | bytes 49160 | tf_op jit(solution)/shard_map/ppermute | solution.py:45
  43.4 7.2 %up_a.1 = (f32[128,1792]{1,0:T(8,128)S(1)}, bf16[1024,1792]{1,0:T(8,128)(2,1)S(1)}, bf16[1024,1792]{1,0:T(8,128)(2,1)S(1)}, bf16[1024,1792]{1,0:T(8,128)(2,1)S(1)}) custom-call(bf16[128,64]{1,0:T(8,128)(2,1)S(1)} %add.2.refs_0_, bf16[128,8192]{1,0:T(8,128)(2,1)S(1)} %get-tuple-element.33.refs_1_, bf16[1024,1792]{1,0:T(8,128)(2,1)S(1)} %get-tuple-element.34.refs_2_, ...), custom_call_target="tpu_custom_call" | custom-call | flops 2818572288 | bytes 16777216 | tf_op jit(solution)/shard_map/up_a/pallas_call | solution.py:258
  50.6 1.2 %collective-permute-start.11 = (bf16[128,64]{1,0:T(8,128)(2,1)S(1)}, bf16[128,64]{1,0:T(8,128)(2,1)S(1)}, u32[]{:S(2)}, u32[]{:S(2)}) collective-permute-start(bf16[128,64]{1,0:T(8,128)(2,1)S(1)} %add.3.refs_0_), channel_id=1, source_target_pairs={{0,2},{1,3},{2,0},{3,1},{4,6},{5,7},{6,4},{7,5},{8,10},{9,11},{10,... | collective-permute-start | bytes 49160 | tf_op jit(solution)/shard_map/ppermute | solution.py:45
  51.9 1.2 %up_b.1.up_pre = f32[128,1792]{1,0:T(8,128)S(1)} custom-call(bf16[128,64]{1,0:T(8,128)(2,1)S(1)} %add.3.refs_0_, bf16[128,8192]{1,0:T(8,128)(2,1)S(1)} %get-tuple-element.33.refs_1_, bf16[1024,1792]{1,0:T(8,128)(2,1)S(1)} %get-tuple-element.46.refs_2_, bf16[1024,1792]{1,0:T(8,128)(2,1)S(1)} %get-tuple-element.47.refs_3_, ...), custom_call_target="tpu_custom_call" | custom-call | flops 939524096 | bytes 16777216 | tf_op jit(solution)/shard_map/up_b/pallas_call | solution.py:258
  53.1 1.5 %collective-permute-done.11.refs_1_ = bf16[128,64]{1,0:T(8,128)(2,1)S(1)} collective-permute-done((bf16[128,64]{1,0:T(8,128)(2,1)S(1)}, bf16[128,64]{1,0:T(8,128)(2,1)S(1)}, u32[]{:S(2)}, u32[]{:S(2)}) %collective-permute-start.11) | collective-permute-done | bytes 16416 | tf_op jit(solution)/shard_map/ppermute | solution.py:45
  54.6 1.6 %finish.1 = bf16[128,1792]{1,0:T(8,128)(2,1)} custom-call(s32[1,128]{1,0:T(1,128)S(1)} %bitcast.14, bf16[1024,1792]{1,0:T(8,128)(2,1)S(1)} %get-tuple-element.44.adapter_up, f32[128,1792]{1,0:T(8,128)S(1)} %get-tuple-element.45.gate_pre, f32[128,1792]{1,0:T(8,128)S(1)} %up_b.1.up_pre, bf16[128,64]{1,0:T(8,128)(2,1)S(1)} %add.3.refs_0_, ...), custom_call_target="tpu_custom_call" | custom-call | flops 469762048 | bytes 4194304 | tf_op jit(solution)/shard_map/finish/pallas_call | solution.py:302
  (23 shorter events, 0.2 us)
Async XLA Ops:
  0.0 12.8 %collective-permute-start = (bf16[64,8192]{1,0:T(8,128)(2,1)}, bf16[64,8192]{1,0:T(8,128)(2,1)S(1)}, u32[]{:S(2)}, u32[]{:S(2)}) collective-permute-start(bf16[64,8192]{1,0:T(8,128)(2,1)} %bitcast.7), channel_id=1, source_target_pairs={{0,1},{1,0},{2,3},{3,2},{4,5},{5,4},{6,7},{7,6},{8,9},{9,8},{10,11... | collective-permute-start | bytes 3145736 | tf_op jit(solution)/shard_map/ppermute | solution.py:45
  0.5 10.9 %collective-permute-start.2 = (bf16[1,8,8192]{2,1,0:T(8,128)(2,1)}, bf16[1,8,8192]{2,1,0:T(8,128)(2,1)S(1)}, u32[]{:S(2)}, u32[]{:S(2)}) collective-permute-start(bf16[1,8,8192]{2,1,0:T(8,128)(2,1)} %bitcast.9), channel_id=1, source_target_pairs={{0,8},{1,9},{2,10},{3,11},{4,12},{5,13},{6,14},{7,15},{8,0},{9,1},... | collective-permute-start | bytes 393224 | tf_op jit(solution)/shard_map/ppermute | solution.py:45
  4.0 8.1 %collective-permute-start.3 = (bf16[1,8,8192]{2,1,0:T(8,128)(2,1)}, bf16[1,8,8192]{2,1,0:T(8,128)(2,1)S(1)}, u32[]{:S(2)}, u32[]{:S(2)}) collective-permute-start(bf16[1,8,8192]{2,1,0:T(8,128)(2,1)} %bitcast.10), channel_id=1, source_target_pairs={{0,2},{1,3},{2,0},{3,1},{4,6},{5,7},{6,4},{7,5},{8,10},{9,11},{10,... | collective-permute-start | bytes 393224 | tf_op jit(solution)/shard_map/ppermute | solution.py:45
  5.6 7.2 %collective-permute-start.1 = (bf16[1,8,8192]{2,1,0:T(8,128)(2,1)}, bf16[1,8,8192]{2,1,0:T(8,128)(2,1)S(1)}, u32[]{:S(2)}, u32[]{:S(2)}) collective-permute-start(bf16[1,8,8192]{2,1,0:T(8,128)(2,1)} %bitcast.11), channel_id=1, source_target_pairs={{0,4},{1,5},{2,6},{3,7},{4,0},{5,1},{6,2},{7,3},{8,12},{9,13},{10,... | collective-permute-start | bytes 393224 | tf_op jit(solution)/shard_map/ppermute | solution.py:45
  11.4 5.5 %collective-permute-start.4 = (bf16[1,8,8192]{2,1,0:T(8,128)(2,1)S(1)}, bf16[1,8,8192]{2,1,0:T(8,128)(2,1)S(1)}, u32[]{:S(2)}, u32[]{:S(2)}) collective-permute-start(bf16[1,8,8192]{2,1,0:T(8,128)(2,1)S(1)} %tie.2.refs_1_), channel_id=1, source_target_pairs={{0,4},{1,5},{2,6},{3,7},{4,0},{5,1},{6,2},{7,3},{8,12},{9,13},{10,... | collective-permute-start | bytes 393224 | tf_op jit(solution)/shard_map/ppermute | solution.py:45
  12.8 10.2 %collective-permute-start.5 = (bf16[2,8,8192]{2,1,0:T(8,128)(2,1)S(1)}, bf16[2,8,8192]{2,1,0:T(8,128)(2,1)S(1)}, u32[]{:S(2)}, u32[]{:S(2)}) collective-permute-start(bf16[2,8,8192]{2,1,0:T(8,128)(2,1)S(1)} %pack.3.refs_0_.refs_1_), channel_id=1, source_target_pairs={{0,2},{1,3},{2,0},{3,1},{4,6},{5,7},{6,4},{7,5},{8,10},{9,11},{10,... | collective-permute-start | bytes 786440 | tf_op jit(solution)/shard_map/ppermute | solution.py:45
  16.9 1.3 %copy-start.1 = (bf16[8,8192]{1,0:T(8,128)(2,1)S(1)}, bf16[8,8192]{1,0:T(8,128)(2,1)}, u32[]{:S(2)}) copy-start(bf16[8,8192]{1,0:T(8,128)(2,1)} %param.8) | copy-start | bytes 393220
  16.9 6.1 %collective-permute-start.6 = (bf16[1,8,8192]{2,1,0:T(8,128)(2,1)S(1)}, bf16[1,8,8192]{2,1,0:T(8,128)(2,1)S(1)}, u32[]{:S(2)}, u32[]{:S(2)}) collective-permute-start(bf16[1,8,8192]{2,1,0:T(8,128)(2,1)S(1)} %tie.3.refs_2_), channel_id=1, source_target_pairs={{0,2},{1,3},{2,0},{3,1},{4,6},{5,7},{6,4},{7,5},{8,10},{9,11},{10,... | collective-permute-start | bytes 393224 | tf_op jit(solution)/shard_map/ppermute | solution.py:45
  18.2 5.0 %collective-permute-start.7 = (bf16[4,8,8192]{2,1,0:T(8,128)(2,1)S(1)}, bf16[4,8,8192]{2,1,0:T(8,128)(2,1)S(1)}, u32[]{:S(2)}, u32[]{:S(2)}) collective-permute-start(bf16[4,8,8192]{2,1,0:T(8,128)(2,1)S(1)} %pack.4.refs_0_), channel_id=1, source_target_pairs={{0,1},{1,0},{2,3},{3,2},{4,5},{5,4},{6,7},{7,6},{8,9},{9,8},{10,11... | collective-permute-start | bytes 1572872 | tf_op jit(solution)/shard_map/ppermute | solution.py:45
  22.5 2.5 %copy-start = (bf16[1,8192,64]{1,2,0:T(8,128)(2,1)S(1)}, bf16[1,8192,64]{1,2,0:T(8,128)(2,1)}, u32[]{:S(2)}) copy-start(bf16[1,8192,64]{1,2,0:T(8,128)(2,1)} %param.11) | copy-start | bytes 3145732
  22.5 2.5 %copy-start.2 = (s32[128]{0:T(128)S(1)}, s32[128]{0:T(128)}, u32[]{:S(2)}) copy-start(s32[128]{0:T(128)} %param.13) | copy-start | bytes 1540
  22.5 2.5 %copy-start.3 = (s32[16]{0:T(128)S(1)}, s32[16]{0:T(128)}, u32[]{:S(2)}) copy-start(s32[16]{0:T(128)} %param.14) | copy-start | bytes 196
  23.1 2.0 %collective-permute-start.8 = (bf16[4,8,8192]{2,1,0:T(8,128)(2,1)S(1)}, bf16[4,8,8192]{2,1,0:T(8,128)(2,1)S(1)}, u32[]{:S(2)}, u32[]{:S(2)}) collective-permute-start(bf16[4,8,8192]{2,1,0:T(8,128)(2,1)S(1)} %pack.5.refs_1_), channel_id=1, source_target_pairs={{0,1},{1,0},{2,3},{3,2},{4,5},{5,4},{6,7},{7,6},{8,9},{9,8},{10,11... | collective-permute-start | bytes 1572872 | tf_op jit(solution)/shard_map/ppermute | solution.py:45
  33.0 9.7 %collective-permute-start.9 = (bf16[128,64]{1,0:T(8,128)(2,1)S(1)}, bf16[128,64]{1,0:T(8,128)(2,1)S(1)}, u32[]{:S(2)}, u32[]{:S(2)}) collective-permute-start(bf16[128,64]{1,0:T(8,128)(2,1)S(1)} %get-tuple-element.32.refs_0_), channel_id=1, source_target_pairs={{0,8},{1,9},{2,10},{3,11},{4,12},{5,13},{6,14},{7,15},{8,0},{9,1},... | collective-permute-start | bytes 49160 | tf_op jit(solution)/shard_map/ppermute | solution.py:45
  42.7 7.9 %collective-permute-start.10 = (bf16[128,64]{1,0:T(8,128)(2,1)S(1)}, bf16[128,64]{1,0:T(8,128)(2,1)S(1)}, u32[]{:S(2)}, u32[]{:S(2)}) collective-permute-start(bf16[128,64]{1,0:T(8,128)(2,1)S(1)} %add.2.refs_0_), channel_id=1, source_target_pairs={{0,4},{1,5},{2,6},{3,7},{4,0},{5,1},{6,2},{7,3},{8,12},{9,13},{10,... | collective-permute-start | bytes 49160 | tf_op jit(solution)/shard_map/ppermute | solution.py:45
  50.6 4.0 %collective-permute-start.11 = (bf16[128,64]{1,0:T(8,128)(2,1)S(1)}, bf16[128,64]{1,0:T(8,128)(2,1)S(1)}, u32[]{:S(2)}, u32[]{:S(2)}) collective-permute-start(bf16[128,64]{1,0:T(8,128)(2,1)S(1)} %add.3.refs_0_), channel_id=1, source_target_pairs={{0,2},{1,3},{2,0},{3,1},{4,6},{5,7},{6,4},{7,5},{8,10},{9,11},{10,... | collective-permute-start | bytes 49160 | tf_op jit(solution)/shard_map/ppermute | solution.py:45

commit v7 on v6

--- a/solution.py
+++ b/solution.py
@@ -52,30 +52,32 @@
     ]
 
 
-def fetch_kernel(firsts, skipped, source, *refs):
-    *targets, sems = refs[skipped:]
-    copies = copies_of([source] * len(targets), firsts, targets, sems)
+def fetch_kernel(firsts, skipped, *refs):
+    n = len(firsts)
+    sources, (*targets, sems) = refs[:n], refs[n + skipped :]
+    copies = copies_of(sources, firsts, targets, sems)
     for copy in copies:
         copy.start()
     for copy in copies:
         copy.wait()
 
 
-def fetch(weight, firsts, rows, name, after=()):
-    return pl.pallas_call(
-        functools.partial(fetch_kernel, firsts, len(after)),
-        out_shape=[pltpu.VMEM((rows, weight.shape[1]), weight.dtype)] * len(firsts),
-        in_specs=[STORED] + [FAR] * len(after),
-        out_specs=[NEAR] * len(firsts),
-        scratch_shapes=[pltpu.SemaphoreType.DMA((len(firsts),))],
+def fetch(fetched, rows, name, after=()):
+    n = len(fetched)
+    width = fetched[0][0].shape[1]
+    arrived = pl.pallas_call(
+        functools.partial(fetch_kernel, [first for source, first in fetched], len(after)),
+        out_shape=[pltpu.VMEM((rows, width), fetched[0][0].dtype)] * n,
+        in_specs=[STORED] * n + [FAR] * len(after),
+        out_specs=[NEAR] * n,
+        scratch_shapes=[pltpu.SemaphoreType.DMA((n,))],
         cost_estimate=pl.CostEstimate(
-            flops=0,
-            bytes_accessed=len(firsts) * rows * weight.shape[1] * 2,
-            transcendentals=0,
+            flops=0, bytes_accessed=n * rows * width * 2, transcendentals=0
         ),
         compiler_params=pltpu.CompilerParams(vmem_limit_bytes=1 << 20),
         name=name,
-    )(far(weight), *after)
+    )(*[far(source) for source, first in fetched], *after)
+    return list(arrived)
 
 
 def across(row):
@@ -134,19 +136,18 @@
     return total
 
 
-def columns_of(ref):
-    width = ref.shape[1]
-    return [pl.ds(i, min(WIDE, width - i)) for i in range(0, width, WIDE)]
-
-
-def collect_kernel(depth, width, sizes, n, firsts, placement, index, down, core_down, *refs):
+def for_columns(width, tile):
+    @pl.loop(0, width // WIDE)
+    def _(i):
+        tile(pl.ds(pl.multiple_of(i * WIDE, WIDE), WIDE))
+
+    if width % WIDE:
+        tile(pl.ds(width // WIDE * WIDE, width % WIDE))
+
+
+def collect_kernel(depth, width, sizes, placement, index, down, core_down, *refs):
     mine, theirs = refs[: len(sizes)], refs[len(sizes) : 2 * len(sizes)]
-    refs = refs[2 * len(sizes) :]
-    pieces, refs = refs[:n], refs[n:]
-    source, packed, low, out, *targets, sems = refs
-    copies = copies_of([source] * len(targets), firsts, targets, sems)
-    for copy in copies:
-        copy.start()
+    packed, low = refs[2 * len(sizes) :]
     own = lax.axis_index("tensor")
     c = own % 2
     rows = packed.shape[0] // (2 * depth * width)
@@ -171,45 +172,26 @@
         chosen = across(jnp.where(index[...] == owner, 1, 0))[:, : full.shape[1]]
         total = jnp.where(chosen == 1, full, 0.0 if total is None else total)
     low[...] = total.astype(low.dtype)
-    for here in columns_of(out):
-        out[:, here] = piecewise(packed, pieces, 0, here)
-    for copy in copies:
-        copy.wait()
-
-
-def collect(placement, index, downs, mine, theirs, depth, width, pieces, fetched):
+
+
+def collect(placement, index, downs, mine, theirs, depth, width):
     sizes = [v.shape[0] for v in mine]
     rows, model = mine[0].shape[1:]
     requests = 2 * depth * width * rows
-    source, firsts, fetched_rows = fetched
-    hidden = source.shape[1]
-    return pl.pallas_call(
-        functools.partial(collect_kernel, depth, width, sizes, len(pieces), firsts),
+    return pl.pallas_call(
+        functools.partial(collect_kernel, depth, width, sizes),
         out_shape=[
             pltpu.VMEM((requests, model), jnp.bfloat16),
             jax.ShapeDtypeStruct((requests, downs[0].shape[0]), jnp.bfloat16),
-            pltpu.VMEM((requests, hidden), jnp.float32),
-        ]
-        + [pltpu.VMEM((fetched_rows, hidden), source.dtype)] * len(firsts),
-        in_specs=[NEAR] * (4 + 2 * len(sizes) + len(pieces)) + [STORED],
-        out_specs=[NEAR] * (3 + len(firsts)),
-        scratch_shapes=[pltpu.SemaphoreType.DMA((len(firsts),))],
+        ],
+        in_specs=[NEAR] * (4 + 2 * len(sizes)),
+        out_specs=[NEAR] * 2,
         cost_estimate=pl.CostEstimate(
-            flops=2 * requests * hidden * sum(p.shape[0] for p in pieces),
-            bytes_accessed=16 << 20,
-            transcendentals=0,
+            flops=4 * requests * model * 64, bytes_accessed=1 << 20, transcendentals=0
         ),
         compiler_params=pltpu.CompilerParams(vmem_limit_bytes=2 << 20),
         name="collect",
-    )(
-        placement,
-        index,
-        *downs,
-        *[near(v) for v in mine],
-        *[near(v) for v in theirs],
-        *[near(p) for p in pieces],
-        far(source),
-    )
+    )(placement, index, *downs, *[near(v) for v in mine], *[near(v) for v in theirs])
 
 
 def add_kernel(*refs):
@@ -239,11 +221,14 @@
     copies = copies_of(sources, firsts, targets[:-1], targets[-1]) if firsts else []
     for copy in copies:
         copy.start()
-    for here in columns_of(out):
+
+    def tile(here):
         total = piecewise(tokens, pieces, start, here)
         if begun:
             total = total + before[0][:, here]
         out[:, here] = total
+
+    for_columns(out.shape[1], tile)
     for copy in copies:
         copy.wait()
 
@@ -274,7 +259,8 @@
     )(*operands)
 
 
-def finish_kernel(m, index, adapter_up, gate_pre, up_pre, *refs):
+def finish_kernel(start, n, m, index, tokens, adapter_up, gate_pre, up_pre, *refs):
+    pieces, refs = refs[:n], refs[n:]
     lows, (out, expanded) = refs[:m], refs[m:]
     rank = lows[0].shape[1]
     mixed = lows[0][...]
@@ -291,28 +277,39 @@
             relative == i * group, wide, 0.0
         ).astype(jnp.bfloat16)
 
-    for here in columns_of(out):
-        delta = jnp.dot(expanded[...], adapter_up[:, here], preferred_element_type=jnp.float32)
+    def tile(here):
+        up = up_pre[:, here] + piecewise(tokens, pieces, start, here)
+        up = up + jnp.dot(expanded[...], adapter_up[:, here], preferred_element_type=jnp.float32)
         gate = gate_pre[:, here]
-        out[:, here] = (gate / (1.0 + jnp.exp(-gate)) * (up_pre[:, here] + delta)).astype(out.dtype)
-
-
-def finish(index, adapter_up, gate_pre, up_pre, lows):
+        out[:, here] = (gate / (1.0 + jnp.exp(-gate)) * up).astype(out.dtype)
+
+    for_columns(out.shape[1], tile)
+
+
+def finish(index, tokens, adapter_up, gate_pre, up_pre, pieces, start, lows):
     requests, hidden = gate_pre.shape
     return pl.pallas_call(
-        functools.partial(finish_kernel, len(lows)),
+        functools.partial(finish_kernel, start, len(pieces), len(lows)),
         out_shape=jax.ShapeDtypeStruct((requests, hidden), jnp.bfloat16),
-        in_specs=[NEAR] * (4 + len(lows)),
+        in_specs=[NEAR] * (5 + len(pieces) + len(lows)),
         out_specs=NEAR,
         scratch_shapes=[pltpu.VMEM((requests, adapter_up.shape[0]), jnp.bfloat16)],
         cost_estimate=pl.CostEstimate(
-            flops=2 * requests * adapter_up.shape[0] * hidden,
+            flops=2 * requests * (adapter_up.shape[0] + sum(p.shape[0] for p in pieces)) * hidden,
             bytes_accessed=4 << 20,
             transcendentals=requests * hidden,
         ),
-        compiler_params=pltpu.CompilerParams(vmem_limit_bytes=2 << 20),
+        compiler_params=pltpu.CompilerParams(vmem_limit_bytes=3 << 20),
         name="finish",
-    )(index, near(adapter_up), near(gate_pre), near(up_pre), *lows)
+    )(
+        index,
+        near(tokens),
+        near(adapter_up),
+        near(gate_pre),
+        near(up_pre),
+        *[near(p) for p in pieces],
+        *lows,
+    )
 
 
 def on_chip(tokens, gate_weight, up_weight, down, up, request_adapter_index, placement):
@@ -330,20 +327,22 @@
     block_1 = swap(own, line_1)
     column_0 = swap(own, column)
     core_down = swap(down, core)
-    gate_0, gate_1, gate_2 = fetch(gate_weight, firsts[:3], unit, "fetch_0")
-    block_2 = tie(block_2, [gate_0])
+    gates = fetch([(gate_weight, first) for first in firsts[:4]], unit, "fetch_0")
+    block_2 = tie(block_2, gates[:1])
     block_3 = swap(block_2, line_1)
-    blocks_12 = pack([block_1, block_2], [gate_0, column_0, core_down])
+    blocks_12 = pack([block_1, block_2], [gates[0], column_0, core_down])
     columns_12 = swap(blocks_12, column)
-    gate_3, gate_4 = fetch(gate_weight, firsts[3:5], unit, "fetch_1", [blocks_12])
-    block_3 = tie(block_3, [gate_3])
+    gates += fetch([(gate_weight, first) for first in firsts[4:6]], unit, "fetch_1", [blocks_12])
+    block_3 = tie(block_3, gates[4:5])
     column_3 = swap(block_3, column)
     line = pack([own, blocks_12, block_3], [])
     core_line = swap(line, core)
-    gate_5, gate_6, gate_7 = fetch(gate_weight, firsts[5:], unit, "fetch_2", [line])
-    columns = pack([column_0, columns_12, column_3], [gate_5])
+    more = [(gate_weight, firsts[6]), (gate_weight, firsts[7]), (up_weight, firsts[0])]
+    *last_gates, up_0 = fetch(more, unit, "fetch_2", [line])
+    gates += last_gates
+    columns = pack([column_0, columns_12, column_3], [up_0])
     core_columns = swap(columns, core)
-    packed, low, gate_pre, up_0, up_1, up_2 = collect(
+    packed, low = collect(
         placement[None, :],
         index,
         [down, core_down],
@@ -351,35 +350,38 @@
         [core_line, core_columns],
         depth,
         width,
-        [gate_0, gate_1, gate_2, gate_3],
-        (up_weight, firsts[:3], unit),
     )
 
     low_1 = add(low, swap(low, line_2))
-    gate_pre, up_3, up_4, up_5 = multiply(
+    gate_pre, *ups = multiply(
         low,
         packed,
-        [gate_4, gate_5, gate_6, gate_7],
+        gates[:4],
+        0,
+        [],
+        [(up_weight, first) for first in firsts[1:4]],
+        unit,
+        "gate_a",
+    )
+    ups = [up_0] + ups
+    low_2 = add(low_1, swap(low_1, line_1))
+    gate_pre, *more_ups = multiply(
+        low_1,
+        packed,
+        gates[4:],
         firsts[4],
         [gate_pre],
-        [(up_weight, first) for first in firsts[3:6]],
+        [(up_weight, first) for first in firsts[4:7]],
         unit,
         "gate_b",
     )
-    low_2 = add(low_1, swap(low_1, line_1))
-    up_pre, near_up, up_6, up_7 = multiply(
-        low_1,
-        packed,
-        [up_0, up_1, up_2, up_3, up_4, up_5],
-        0,
-        [],
-        [(up, 0), (up_weight, firsts[6]), (up_weight, firsts[7])],
-        unit,
-        "up_a",
-    )
     lows = [low_2, swap(low_2, column)]
-    (up_pre,) = multiply(low_2, packed, [up_6, up_7], firsts[6], [up_pre], [], 0, "up_b")
-    return finish(index, near_up, gate_pre, up_pre, lows)
+    up_pre, near_up, last_up = multiply(
+        low_2, packed, ups, 0, [], [(up, 0), (up_weight, firsts[7])], unit, "up_a"
+    )
+    return finish(
+        index, packed, near_up, gate_pre, up_pre, more_ups + [last_up], firsts[4], lows
+    )
 
 
 def streamed(

time: 56.3 us -> 47.9 us (0.85)
  Pallas kernels: 36.1 us -> 30.2 us
  starting transfers between devices: 15.4 us -> 14 us
  waiting for transfers between devices: 4.49 us -> 3.32 us
    pallas_call x3, Pallas kernels: 14.8 us -> 11.6 us  [multiply(): pl.pallas_call(functools.partial(multiply_kernel, start, len(pieces), len...]
    pallas_call x5, Pallas kernels: 21.1 us -> 18.5 us  [the longest x3 12.7 us: fetch(): pl.pallas_call(functools.partial(fetch_kernel, [first for source, first i...]
    ppermute x12, starting transfers between devices: 15.4 us -> 14 us  [swap(): return lax.ppermute(value, 'tensor', pairs)]
    ppermute x12, waiting for transfers between devices: 4.49 us -> 3.32 us  [swap(): return lax.ppermute(value, 'tensor', pairs)]
  transfers between devices with their start and end apart: 12 -> 12, of which waited for: 4 -> 3; matrix products, arithmetic and copies ran while one was open for 0% -> 0% of each run, Pallas kernels for 47% -> 51%
where the time goes in v7:
time: 47.9 us; the launch traced here: 47.8 us
  Pallas kernels  30.2 us (63%)
  starting transfers between devices  14 us (29%)
  waiting for transfers between devices  3.32 us (7%)
    ppermute x12, starting transfers between devices, swap(): return lax.ppermute(value, 'tensor', pairs)  14 us
    pallas_call x3, Pallas kernels, fetch(): pl.pallas_call(functools.partial(fetch_kernel, [first for source, first i...  12.7 us
    pallas_call x3, Pallas kernels, multiply(): pl.pallas_call(functools.partial(multiply_kernel, start, len(pieces), len...  11.6 us
    pallas_call x1, Pallas kernels, finish(): pl.pallas_call(functools.partial(finish_kernel, start, len(pieces), len(l...  4.08 us
    ppermute x12, waiting for transfers between devices, swap(): return lax.ppermute(value, 'tensor', pairs)  3.32 us
    pallas_call x1, Pallas kernels, collect(): pl.pallas_call(functools.partial(collect_kernel, depth, width, sizes), ou...  1.71 us
  transfers between devices with their start and end apart: 12, of which 3 were waited for; matrix products, arithmetic and copies ran while one was open for 0% of the time, Pallas kernels for 51%

profile of v7, /device:TPU:0, one launch (start us, length us, event | category | flops | bytes accessed | tf_op | source)
XLA Modules:
  0.0 47.8 jit_solution(8464116398817227846)
XLA Ops:
  0.0 0.5 collective-permute-start
  0.5 3.6 %collective-permute-start.2 = (bf16[1,8,8192]{2,1,0:T(8,128)(2,1)}, bf16[1,8,8192]{2,1,0:T(8,128)(2,1)S(1)}, u32[]{:S(2)}, u32[]{:S(2)}) collective-permute-start(bf16[1,8,8192]{2,1,0:T(8,128)(2,1)} %bitcast.9), channel_id=1, source_target_pairs={{0,8},{1,9},{2,10},{3,11},{4,12},{5,13},{6,14},{7,15},{8,0},{9,1},... | collective-permute-start | bytes 393224 | tf_op jit(solution)/shard_map/ppermute | solution.py:45
  4.0 1.5 %collective-permute-start.3 = (bf16[1,8,8192]{2,1,0:T(8,128)(2,1)}, bf16[1,8,8192]{2,1,0:T(8,128)(2,1)S(1)}, u32[]{:S(2)}, u32[]{:S(2)}) collective-permute-start(bf16[1,8,8192]{2,1,0:T(8,128)(2,1)} %bitcast.10), channel_id=1, source_target_pairs={{0,2},{1,3},{2,0},{3,1},{4,6},{5,7},{6,4},{7,5},{8,10},{9,11},{10,... | collective-permute-start | bytes 393224 | tf_op jit(solution)/shard_map/ppermute | solution.py:45
  5.6 1.6 %collective-permute-start.1 = (bf16[1,8,8192]{2,1,0:T(8,128)(2,1)}, bf16[1,8,8192]{2,1,0:T(8,128)(2,1)S(1)}, u32[]{:S(2)}, u32[]{:S(2)}) collective-permute-start(bf16[1,8,8192]{2,1,0:T(8,128)(2,1)} %bitcast.11), channel_id=1, source_target_pairs={{0,4},{1,5},{2,6},{3,7},{4,0},{5,1},{6,2},{7,3},{8,12},{9,13},{10,... | collective-permute-start | bytes 393224 | tf_op jit(solution)/shard_map/ppermute | solution.py:45
  7.1 5.3 %fetch_0.1 = (bf16[1024,1792]{1,0:T(8,128)(2,1)S(1)}, bf16[1024,1792]{1,0:T(8,128)(2,1)S(1)}, bf16[1024,1792]{1,0:T(8,128)(2,1)S(1)}, bf16[1024,1792]{1,0:T(8,128)(2,1)S(1)}) custom-call(bf16[8192,1792]{1,0:T(8,128)(2,1)} %refs_1_.5, bf16[8192,1792]{1,0:T(8,128)(2,1)} %refs_1_.5, bf16[8192,1792]{1,0:T(8,128)(2,1)} %refs_1_.5, bf16[8192,1792]{1,0:T(8,128)(2,1)} %refs_1_.5), custom_call_target="tpu_custom_call" | custom-call | bytes 14680064 | tf_op jit(solution)/shard_map/fetch_0/pallas_call | solution.py:68
  12.4 0.5 %collective-permute-start.4 = (bf16[1,8,8192]{2,1,0:T(8,128)(2,1)S(1)}, bf16[1,8,8192]{2,1,0:T(8,128)(2,1)S(1)}, u32[]{:S(2)}, u32[]{:S(2)}) collective-permute-start(bf16[1,8,8192]{2,1,0:T(8,128)(2,1)S(1)} %tie.2.refs_1_), channel_id=1, source_target_pairs={{0,4},{1,5},{2,6},{3,7},{4,0},{5,1},{6,2},{7,3},{8,12},{9,13},{10,... | collective-permute-start | bytes 393224 | tf_op jit(solution)/shard_map/ppermute | solution.py:45
  13.0 0.7 %collective-permute-start.5 = (bf16[2,8,8192]{2,1,0:T(8,128)(2,1)S(1)}, bf16[2,8,8192]{2,1,0:T(8,128)(2,1)S(1)}, u32[]{:S(2)}, u32[]{:S(2)}) collective-permute-start(bf16[2,8,8192]{2,1,0:T(8,128)(2,1)S(1)} %pack.3.refs_2_.refs_1_), channel_id=1, source_target_pairs={{0,2},{1,3},{2,0},{3,1},{4,6},{5,7},{6,4},{7,5},{8,10},{9,11},{10,... | collective-permute-start | bytes 786440 | tf_op jit(solution)/shard_map/ppermute | solution.py:45
  13.7 3.2 %fetch_1.1 = (bf16[1024,1792]{1,0:T(8,128)(2,1)S(1)}, bf16[1024,1792]{1,0:T(8,128)(2,1)S(1)}) custom-call(bf16[8192,1792]{1,0:T(8,128)(2,1)} %refs_1_.5, bf16[8192,1792]{1,0:T(8,128)(2,1)} %refs_1_.5, bf16[2,8,8192]{2,1,0:T(8,128)(2,1)S(1)} %pack.3.refs_2_.refs_1_), custom_call_target="tpu_custom_call" | custom-call | bytes 7340032 | tf_op jit(solution)/shard_map/fetch_1/pallas_call | solution.py:68
  16.9 0.0 copy-start.1
  16.9 0.7 %collective-permute-done.4.refs_0_ = bf16[1,8,8192]{2,1,0:T(8,128)(2,1)S(1)} collective-permute-done((bf16[1,8,8192]{2,1,0:T(8,128)(2,1)S(1)}, bf16[1,8,8192]{2,1,0:T(8,128)(2,1)S(1)}, u32[]{:S(2)}, u32[]{:S(2)}) %collective-permute-start.4) | collective-permute-done | bytes 131104 | tf_op jit(solution)/shard_map/ppermute | solution.py:45
  17.6 0.8 %collective-permute-start.6 = (bf16[1,8,8192]{2,1,0:T(8,128)(2,1)S(1)}, bf16[1,8,8192]{2,1,0:T(8,128)(2,1)S(1)}, u32[]{:S(2)}, u32[]{:S(2)}) collective-permute-start(bf16[1,8,8192]{2,1,0:T(8,128)(2,1)S(1)} %tie.3.refs_2_), channel_id=1, source_target_pairs={{0,2},{1,3},{2,0},{3,1},{4,6},{5,7},{6,4},{7,5},{8,10},{9,11},{10,... | collective-permute-start | bytes 393224 | tf_op jit(solution)/shard_map/ppermute | solution.py:45
  18.4 0.1 collective-permute-start.7
  18.5 4.2 %fetch_2.1 = (bf16[1024,1792]{1,0:T(8,128)(2,1)S(1)}, bf16[1024,1792]{1,0:T(8,128)(2,1)S(1)}, bf16[1024,1792]{1,0:T(8,128)(2,1)S(1)}) custom-call(bf16[8192,1792]{1,0:T(8,128)(2,1)} %refs_1_.5, bf16[8192,1792]{1,0:T(8,128)(2,1)} %refs_1_.5, bf16[8192,1792]{1,0:T(8,128)(2,1)} %refs_9_.1, bf16[4,8,8192]{2,1,0:T(8,128)(2,1)S(1)} %pack.4.refs_3_.refs_0_), custom_call_target="tpu_custom_call" | custom-call | bytes 11010048 | tf_op jit(solution)/shard_map/fetch_2/pallas_call | solution.py:68
  22.8 0.7 %collective-permute-done.6.refs_2_ = bf16[1,8,8192]{2,1,0:T(8,128)(2,1)S(1)} collective-permute-done((bf16[1,8,8192]{2,1,0:T(8,128)(2,1)S(1)}, bf16[1,8,8192]{2,1,0:T(8,128)(2,1)S(1)}, u32[]{:S(2)}, u32[]{:S(2)}) %collective-permute-start.6) | collective-permute-done | bytes 131104 | tf_op jit(solution)/shard_map/ppermute | solution.py:45
  23.5 0.1 collective-permute-start.8
  23.6 1.9 %collective-permute-done.8.refs_3_ = bf16[4,8,8192]{2,1,0:T(8,128)(2,1)S(1)} collective-permute-done((bf16[4,8,8192]{2,1,0:T(8,128)(2,1)S(1)}, bf16[4,8,8192]{2,1,0:T(8,128)(2,1)S(1)}, u32[]{:S(2)}, u32[]{:S(2)}) %collective-permute-start.8) | collective-permute-done | bytes 524320 | tf_op jit(solution)/shard_map/ppermute | solution.py:45
  25.5 1.7 %collect.1 = (bf16[128,8192]{1,0:T(8,128)(2,1)S(1)}, bf16[128,64]{1,0:T(8,128)(2,1)S(1)}) custom-call(s32[1,16]{1,0:T(1,128)S(1)} %bitcast.15, s32[1,128]{1,0:T(1,128)S(1)} %bitcast.13, bf16[64,8192]{1,0:T(8,128)(2,1)S(1)} %bitcast.8, bf16[64,8192]{1,0:T(8,128)(2,1)S(1)} %collective-permute-done.refs_4_.core_down, ...), custom_call_target="tpu_custom_call" | custom-call | flops 268435456 | bytes 1048576 | tf_op jit(solution)/shard_map/collect/pallas_call | solution.py:181
  27.2 2.9 %collective-permute-start.9 = (bf16[128,64]{1,0:T(8,128)(2,1)S(1)}, bf16[128,64]{1,0:T(8,128)(2,1)S(1)}, u32[]{:S(2)}, u32[]{:S(2)}) collective-permute-start(bf16[128,64]{1,0:T(8,128)(2,1)S(1)} %get-tuple-element.31.refs_0_), channel_id=1, source_target_pairs={{0,8},{1,9},{2,10},{3,11},{4,12},{5,13},{6,14},{7,15},{8,0},{9,1},... | collective-permute-start | bytes 49160 | tf_op jit(solution)/shard_map/ppermute | solution.py:45
  30.1 4.2 %gate_a.1 = (f32[128,1792]{1,0:T(8,128)S(1)}, bf16[1024,1792]{1,0:T(8,128)(2,1)S(1)}, bf16[1024,1792]{1,0:T(8,128)(2,1)S(1)}, bf16[1024,1792]{1,0:T(8,128)(2,1)S(1)}) custom-call(bf16[128,64]{1,0:T(8,128)(2,1)S(1)} %get-tuple-element.31.refs_0_, bf16[128,8192]{1,0:T(8,128)(2,1)S(1)} %get-tuple-element.30.refs_1_.tokens, ...), custom_call_target="tpu_custom_call" | custom-call | flops 1879048192 | bytes 16777216 | tf_op jit(solution)/shard_map/gate_a/pallas_call | solution.py:243
  34.4 0.6 %collective-permute-start.10 = (bf16[128,64]{1,0:T(8,128)(2,1)S(1)}, bf16[128,64]{1,0:T(8,128)(2,1)S(1)}, u32[]{:S(2)}, u32[]{:S(2)}) collective-permute-start(bf16[128,64]{1,0:T(8,128)(2,1)S(1)} %add.2.refs_0_), channel_id=1, source_target_pairs={{0,4},{1,5},{2,6},{3,7},{4,0},{5,1},{6,2},{7,3},{8,12},{9,13},{10,... | collective-permute-start | bytes 49160 | tf_op jit(solution)/shard_map/ppermute | solution.py:45
  35.0 4.2 %gate_b.1 = (f32[128,1792]{1,0:T(8,128)S(1)}, bf16[1024,1792]{1,0:T(8,128)(2,1)S(1)}, bf16[1024,1792]{1,0:T(8,128)(2,1)S(1)}, bf16[1024,1792]{1,0:T(8,128)(2,1)S(1)}) custom-call(bf16[128,64]{1,0:T(8,128)(2,1)S(1)} %add.2.refs_0_, bf16[128,8192]{1,0:T(8,128)(2,1)S(1)} %get-tuple-element.30.refs_1_.tokens, ...), custom_call_target="tpu_custom_call" | custom-call | flops 1879048192 | bytes 16777216 | tf_op jit(solution)/shard_map/gate_b/pallas_call | solution.py:243
  39.3 1.2 %collective-permute-start.11 = (bf16[128,64]{1,0:T(8,128)(2,1)S(1)}, bf16[128,64]{1,0:T(8,128)(2,1)S(1)}, u32[]{:S(2)}, u32[]{:S(2)}) collective-permute-start(bf16[128,64]{1,0:T(8,128)(2,1)S(1)} %add.3.refs_0_.refs_4_), channel_id=1, source_target_pairs={{0,2},{1,3},{2,0},{3,1},{4,6},{5,7},{6,4},{7,5},{8,10},{9,11},{10,... | collective-permute-start | bytes 49160 | tf_op jit(solution)/shard_map/ppermute | solution.py:45
  40.5 3.2 %up_a.1 = (f32[128,1792]{1,0:T(8,128)S(1)}, bf16[1024,1792]{1,0:T(8,128)(2,1)S(1)}, bf16[1024,1792]{1,0:T(8,128)(2,1)S(1)}) custom-call(bf16[128,64]{1,0:T(8,128)(2,1)S(1)} %add.3.refs_0_.refs_4_, bf16[128,8192]{1,0:T(8,128)(2,1)S(1)} %get-tuple-element.30.refs_1_.tokens, bf16[1024,1792]{1,0:T(8,128)(2,1)S(1)} %get-tuple-element.29.refs_3_.refs_2_, ...), custom_call_target="tpu_custom_call" | custom-call | flops 1879048192 | bytes 16777216 | tf_op jit(solution)/shard_map/up_a/pallas_call | solution.py:243
  43.7 4.1 %finish.1 = bf16[128,1792]{1,0:T(8,128)(2,1)} custom-call(s32[1,128]{1,0:T(1,128)S(1)} %bitcast.14, bf16[128,8192]{1,0:T(8,128)(2,1)S(1)} %get-tuple-element.30.refs_1_.tokens, bf16[1024,1792]{1,0:T(8,128)(2,1)S(1)} %get-tuple-element.38.adapter_up, f32[128,1792]{1,0:T(8,128)S(1)} %get-tuple-element.43.gate_pre, f32[128,1792]{1,0:T(8,128)S(1)} %get-tuple-element.44.up_pre, ...), custom_call_target="tpu_custom_call" | custom-call | flops 2348810240 | bytes 4194304 | tf_op jit(solution)/shard_map/finish/pallas_call | solution.py:291
  (23 shorter events, 0.2 us)
Async XLA Ops:
  0.0 13.0 %collective-permute-start = (bf16[64,8192]{1,0:T(8,128)(2,1)}, bf16[64,8192]{1,0:T(8,128)(2,1)S(1)}, u32[]{:S(2)}, u32[]{:S(2)}) collective-permute-start(bf16[64,8192]{1,0:T(8,128)(2,1)} %bitcast.7), channel_id=1, source_target_pairs={{0,1},{1,0},{2,3},{3,2},{4,5},{5,4},{6,7},{7,6},{8,9},{9,8},{10,11... | collective-permute-start | bytes 3145736 | tf_op jit(solution)/shard_map/ppermute | solution.py:45
  0.5 12.0 %collective-permute-start.2 = (bf16[1,8,8192]{2,1,0:T(8,128)(2,1)}, bf16[1,8,8192]{2,1,0:T(8,128)(2,1)S(1)}, u32[]{:S(2)}, u32[]{:S(2)}) collective-permute-start(bf16[1,8,8192]{2,1,0:T(8,128)(2,1)} %bitcast.9), channel_id=1, source_target_pairs={{0,8},{1,9},{2,10},{3,11},{4,12},{5,13},{6,14},{7,15},{8,0},{9,1},... | collective-permute-start | bytes 393224 | tf_op jit(solution)/shard_map/ppermute | solution.py:45
  4.0 8.9 %collective-permute-start.3 = (bf16[1,8,8192]{2,1,0:T(8,128)(2,1)}, bf16[1,8,8192]{2,1,0:T(8,128)(2,1)S(1)}, u32[]{:S(2)}, u32[]{:S(2)}) collective-permute-start(bf16[1,8,8192]{2,1,0:T(8,128)(2,1)} %bitcast.10), channel_id=1, source_target_pairs={{0,2},{1,3},{2,0},{3,1},{4,6},{5,7},{6,4},{7,5},{8,10},{9,11},{10,... | collective-permute-start | bytes 393224 | tf_op jit(solution)/shard_map/ppermute | solution.py:45
  5.6 7.4 %collective-permute-start.1 = (bf16[1,8,8192]{2,1,0:T(8,128)(2,1)}, bf16[1,8,8192]{2,1,0:T(8,128)(2,1)S(1)}, u32[]{:S(2)}, u32[]{:S(2)}) collective-permute-start(bf16[1,8,8192]{2,1,0:T(8,128)(2,1)} %bitcast.11), channel_id=1, source_target_pairs={{0,4},{1,5},{2,6},{3,7},{4,0},{5,1},{6,2},{7,3},{8,12},{9,13},{10,... | collective-permute-start | bytes 393224 | tf_op jit(solution)/shard_map/ppermute | solution.py:45
  12.4 5.1 %collective-permute-start.4 = (bf16[1,8,8192]{2,1,0:T(8,128)(2,1)S(1)}, bf16[1,8,8192]{2,1,0:T(8,128)(2,1)S(1)}, u32[]{:S(2)}, u32[]{:S(2)}) collective-permute-start(bf16[1,8,8192]{2,1,0:T(8,128)(2,1)S(1)} %tie.2.refs_1_), channel_id=1, source_target_pairs={{0,4},{1,5},{2,6},{3,7},{4,0},{5,1},{6,2},{7,3},{8,12},{9,13},{10,... | collective-permute-start | bytes 393224 | tf_op jit(solution)/shard_map/ppermute | solution.py:45
  13.0 10.5 %collective-permute-start.5 = (bf16[2,8,8192]{2,1,0:T(8,128)(2,1)S(1)}, bf16[2,8,8192]{2,1,0:T(8,128)(2,1)S(1)}, u32[]{:S(2)}, u32[]{:S(2)}) collective-permute-start(bf16[2,8,8192]{2,1,0:T(8,128)(2,1)S(1)} %pack.3.refs_2_.refs_1_), channel_id=1, source_target_pairs={{0,2},{1,3},{2,0},{3,1},{4,6},{5,7},{6,4},{7,5},{8,10},{9,11},{10,... | collective-permute-start | bytes 786440 | tf_op jit(solution)/shard_map/ppermute | solution.py:45
  16.9 1.5 %copy-start.1 = (bf16[8,8192]{1,0:T(8,128)(2,1)S(1)}, bf16[8,8192]{1,0:T(8,128)(2,1)}, u32[]{:S(2)}) copy-start(bf16[8,8192]{1,0:T(8,128)(2,1)} %param.8) | copy-start | bytes 393220
  17.6 5.9 %collective-permute-start.6 = (bf16[1,8,8192]{2,1,0:T(8,128)(2,1)S(1)}, bf16[1,8,8192]{2,1,0:T(8,128)(2,1)S(1)}, u32[]{:S(2)}, u32[]{:S(2)}) collective-permute-start(bf16[1,8,8192]{2,1,0:T(8,128)(2,1)S(1)} %tie.3.refs_2_), channel_id=1, source_target_pairs={{0,2},{1,3},{2,0},{3,1},{4,6},{5,7},{6,4},{7,5},{8,10},{9,11},{10,... | collective-permute-start | bytes 393224 | tf_op jit(solution)/shard_map/ppermute | solution.py:45
  18.4 5.2 %collective-permute-start.7 = (bf16[4,8,8192]{2,1,0:T(8,128)(2,1)S(1)}, bf16[4,8,8192]{2,1,0:T(8,128)(2,1)S(1)}, u32[]{:S(2)}, u32[]{:S(2)}) collective-permute-start(bf16[4,8,8192]{2,1,0:T(8,128)(2,1)S(1)} %pack.4.refs_3_.refs_0_), channel_id=1, source_target_pairs={{0,1},{1,0},{2,3},{3,2},{4,5},{5,4},{6,7},{7,6},{8,9},{9,8},{10,11... | collective-permute-start | bytes 1572872 | tf_op jit(solution)/shard_map/ppermute | solution.py:45
  22.7 2.8 %copy-start = (bf16[1,8192,64]{1,2,0:T(8,128)(2,1)S(1)}, bf16[1,8192,64]{1,2,0:T(8,128)(2,1)}, u32[]{:S(2)}) copy-start(bf16[1,8192,64]{1,2,0:T(8,128)(2,1)} %param.11) | copy-start | bytes 3145732
  22.7 2.8 %copy-start.2 = (s32[128]{0:T(128)S(1)}, s32[128]{0:T(128)}, u32[]{:S(2)}) copy-start(s32[128]{0:T(128)} %param.13) | copy-start | bytes 1540
  22.8 2.7 %copy-start.3 = (s32[16]{0:T(128)S(1)}, s32[16]{0:T(128)}, u32[]{:S(2)}) copy-start(s32[16]{0:T(128)} %param.14) | copy-start | bytes 196
  23.5 2.0 %collective-permute-start.8 = (bf16[4,8,8192]{2,1,0:T(8,128)(2,1)S(1)}, bf16[4,8,8192]{2,1,0:T(8,128)(2,1)S(1)}, u32[]{:S(2)}, u32[]{:S(2)}) collective-permute-start(bf16[4,8,8192]{2,1,0:T(8,128)(2,1)S(1)} %pack.5.refs_1_), channel_id=1, source_target_pairs={{0,1},{1,0},{2,3},{3,2},{4,5},{5,4},{6,7},{7,6},{8,9},{9,8},{10,11... | collective-permute-start | bytes 1572872 | tf_op jit(solution)/shard_map/ppermute | solution.py:45
  27.2 7.1 %collective-permute-start.9 = (bf16[128,64]{1,0:T(8,128)(2,1)S(1)}, bf16[128,64]{1,0:T(8,128)(2,1)S(1)}, u32[]{:S(2)}, u32[]{:S(2)}) collective-permute-start(bf16[128,64]{1,0:T(8,128)(2,1)S(1)} %get-tuple-element.31.refs_0_), channel_id=1, source_target_pairs={{0,8},{1,9},{2,10},{3,11},{4,12},{5,13},{6,14},{7,15},{8,0},{9,1},... | collective-permute-start | bytes 49160 | tf_op jit(solution)/shard_map/ppermute | solution.py:45
  34.4 4.9 %collective-permute-start.10 = (bf16[128,64]{1,0:T(8,128)(2,1)S(1)}, bf16[128,64]{1,0:T(8,128)(2,1)S(1)}, u32[]{:S(2)}, u32[]{:S(2)}) collective-permute-start(bf16[128,64]{1,0:T(8,128)(2,1)S(1)} %add.2.refs_0_), channel_id=1, source_target_pairs={{0,4},{1,5},{2,6},{3,7},{4,0},{5,1},{6,2},{7,3},{8,12},{9,13},{10,... | collective-permute-start | bytes 49160 | tf_op jit(solution)/shard_map/ppermute | solution.py:45
  39.3 4.4 %collective-permute-start.11 = (bf16[128,64]{1,0:T(8,128)(2,1)S(1)}, bf16[128,64]{1,0:T(8,128)(2,1)S(1)}, u32[]{:S(2)}, u32[]{:S(2)}) collective-permute-start(bf16[128,64]{1,0:T(8,128)(2,1)S(1)} %add.3.refs_0_.refs_4_), channel_id=1, source_target_pairs={{0,2},{1,3},{2,0},{3,1},{4,6},{5,7},{6,4},{7,5},{8,10},{9,11},{10,... | collective-permute-start | bytes 49160 | tf_op jit(solution)/shard_map/ppermute | solution.py:45

commit v8 on v7

--- a/solution.py
+++ b/solution.py
@@ -277,13 +277,13 @@
             relative == i * group, wide, 0.0
         ).astype(jnp.bfloat16)
 
-    def tile(here):
+    width = out.shape[1]
+    for first in range(0, width, WIDE):
+        here = pl.ds(first, min(WIDE, width - first))
         up = up_pre[:, here] + piecewise(tokens, pieces, start, here)
         up = up + jnp.dot(expanded[...], adapter_up[:, here], preferred_element_type=jnp.float32)
         gate = gate_pre[:, here]
         out[:, here] = (gate / (1.0 + jnp.exp(-gate)) * up).astype(out.dtype)
-
-    for_columns(out.shape[1], tile)
 
 
 def finish(index, tokens, adapter_up, gate_pre, up_pre, pieces, start, lows):
@@ -327,19 +327,19 @@
     block_1 = swap(own, line_1)
     column_0 = swap(own, column)
     core_down = swap(down, core)
-    gates = fetch([(gate_weight, first) for first in firsts[:4]], unit, "fetch_0")
+    gates = fetch([(gate_weight, first) for first in firsts[:5]], unit, "fetch_0")
     block_2 = tie(block_2, gates[:1])
     block_3 = swap(block_2, line_1)
     blocks_12 = pack([block_1, block_2], [gates[0], column_0, core_down])
     columns_12 = swap(blocks_12, column)
-    gates += fetch([(gate_weight, first) for first in firsts[4:6]], unit, "fetch_1", [blocks_12])
-    block_3 = tie(block_3, gates[4:5])
+    gates += fetch([(gate_weight, first) for first in firsts[5:7]], unit, "fetch_1", [blocks_12])
+    block_3 = tie(block_3, gates[5:6])
     column_3 = swap(block_3, column)
     line = pack([own, blocks_12, block_3], [])
     core_line = swap(line, core)
-    more = [(gate_weight, firsts[6]), (gate_weight, firsts[7]), (up_weight, firsts[0])]
-    *last_gates, up_0 = fetch(more, unit, "fetch_2", [line])
-    gates += last_gates
+    more = [(gate_weight, firsts[7]), (up_weight, firsts[0]), (up_weight, firsts[1])]
+    last_gate, up_0, up_1 = fetch(more, unit, "fetch_2", [line])
+    gates.append(last_gate)
     columns = pack([column_0, columns_12, column_3], [up_0])
     core_columns = swap(columns, core)
     packed, low = collect(
@@ -359,11 +359,11 @@
         gates[:4],
         0,
         [],
-        [(up_weight, first) for first in firsts[1:4]],
+        [(up_weight, first) for first in firsts[2:4]],
         unit,
         "gate_a",
     )
-    ups = [up_0] + ups
+    ups = [up_0, up_1] + ups
     low_2 = add(low_1, swap(low_1, line_1))
     gate_pre, *more_ups = multiply(
         low_1,

time: 47.9 us -> 46.5 us (0.971)
  starting transfers between devices: 14 us -> 12.9 us
  Pallas kernels: 30.2 us -> 29.5 us
  waiting for transfers between devices: 3.32 us -> 3.86 us
    ppermute x12, starting transfers between devices: 14 us -> 12.9 us  [swap(): return lax.ppermute(value, 'tensor', pairs)]
    pallas_call x3, Pallas kernels: 12.7 us -> 13.7 us  [fetch(): pl.pallas_call(functools.partial(fetch_kernel, [first for source, first i...]
    pallas_call x3, Pallas kernels: 11.6 us -> 10.6 us  [multiply(): pl.pallas_call(functools.partial(multiply_kernel, start, len(pieces), len...]
    pallas_call x1, Pallas kernels: 4.08 us -> 3.32 us  [finish(): pl.pallas_call(functools.partial(finish_kernel, start, len(pieces), len(l...]
    ppermute x12, waiting for transfers between devices: 3.32 us -> 3.86 us  [swap(): return lax.ppermute(value, 'tensor', pairs)]
  transfers between devices with their start and end apart: 12 -> 12, of which waited for: 3 -> 5; matrix products, arithmetic and copies ran while one was open for 0% -> 0% of each run, Pallas kernels for 51% -> 53%
where the time goes in v8:
time: 46.5 us; the launch traced here: 46.4 us
  Pallas kernels  29.5 us (63%)
  starting transfers between devices  12.9 us (28%)
  waiting for transfers between devices  3.86 us (8%)
    pallas_call x3, Pallas kernels, fetch(): pl.pallas_call(functools.partial(fetch_kernel, [first for source, first i...  13.7 us
    ppermute x12, starting transfers between devices, swap(): return lax.ppermute(value, 'tensor', pairs)  12.9 us
    pallas_call x3, Pallas kernels, multiply(): pl.pallas_call(functools.partial(multiply_kernel, start, len(pieces), len...  10.6 us
    ppermute x12, waiting for transfers between devices, swap(): return lax.ppermute(value, 'tensor', pairs)  3.86 us
    pallas_call x1, Pallas kernels, finish(): pl.pallas_call(functools.partial(finish_kernel, start, len(pieces), len(l...  3.32 us
    pallas_call x1, Pallas kernels, collect(): pl.pallas_call(functools.partial(collect_kernel, depth, width, sizes), ou...  1.71 us
  transfers between devices with their start and end apart: 12, of which 5 were waited for; matrix products, arithmetic and copies ran while one was open for 0% of the time, Pallas kernels for 53%

profile of v8, /device:TPU:0, one launch (start us, length us, event | category | flops | bytes accessed | tf_op | source)
XLA Modules:
  0.0 46.4 jit_solution(581656975802322575)
XLA Ops:
  0.0 0.5 collective-permute-start
  0.5 3.6 %collective-permute-start.2 = (bf16[1,8,8192]{2,1,0:T(8,128)(2,1)}, bf16[1,8,8192]{2,1,0:T(8,128)(2,1)S(1)}, u32[]{:S(2)}, u32[]{:S(2)}) collective-permute-start(bf16[1,8,8192]{2,1,0:T(8,128)(2,1)} %bitcast.9), channel_id=1, source_target_pairs={{0,8},{1,9},{2,10},{3,11},{4,12},{5,13},{6,14},{7,15},{8,0},{9,1},... | collective-permute-start | bytes 393224 | tf_op jit(solution)/shard_map/ppermute | solution.py:45
  4.0 1.5 %collective-permute-start.3 = (bf16[1,8,8192]{2,1,0:T(8,128)(2,1)}, bf16[1,8,8192]{2,1,0:T(8,128)(2,1)S(1)}, u32[]{:S(2)}, u32[]{:S(2)}) collective-permute-start(bf16[1,8,8192]{2,1,0:T(8,128)(2,1)} %bitcast.10), channel_id=1, source_target_pairs={{0,2},{1,3},{2,0},{3,1},{4,6},{5,7},{6,4},{7,5},{8,10},{9,11},{10,... | collective-permute-start | bytes 393224 | tf_op jit(solution)/shard_map/ppermute | solution.py:45
  5.6 1.6 %collective-permute-start.1 = (bf16[1,8,8192]{2,1,0:T(8,128)(2,1)}, bf16[1,8,8192]{2,1,0:T(8,128)(2,1)S(1)}, u32[]{:S(2)}, u32[]{:S(2)}) collective-permute-start(bf16[1,8,8192]{2,1,0:T(8,128)(2,1)} %bitcast.11), channel_id=1, source_target_pairs={{0,4},{1,5},{2,6},{3,7},{4,0},{5,1},{6,2},{7,3},{8,12},{9,13},{10,... | collective-permute-start | bytes 393224 | tf_op jit(solution)/shard_map/ppermute | solution.py:45
  7.1 6.3 %fetch_0.1 = (bf16[1024,1792]{1,0:T(8,128)(2,1)S(1)}, bf16[1024,1792]{1,0:T(8,128)(2,1)S(1)}, bf16[1024,1792]{1,0:T(8,128)(2,1)S(1)}, bf16[1024,1792]{1,0:T(8,128)(2,1)S(1)}, bf16[1024,1792]{1,0:T(8,128)(2,1)S(1)}) custom-call(bf16[8192,1792]{1,0:T(8,128)(2,1)} %refs_0_.5, bf16[8192,1792]{1,0:T(8,128)(2,1)} %refs_0_.5, bf16[8192,1792]{1,0:T(8,128)(2,1)} %refs_0_.5, ...), custom_call_target="tpu_custom_call" | custom-call | bytes 18350080 | tf_op jit(solution)/shard_map/fetch_0/pallas_call | solution.py:68
  13.5 0.5 %collective-permute-start.4 = (bf16[1,8,8192]{2,1,0:T(8,128)(2,1)S(1)}, bf16[1,8,8192]{2,1,0:T(8,128)(2,1)S(1)}, u32[]{:S(2)}, u32[]{:S(2)}) collective-permute-start(bf16[1,8,8192]{2,1,0:T(8,128)(2,1)S(1)} %tie.2.refs_1_), channel_id=1, source_target_pairs={{0,4},{1,5},{2,6},{3,7},{4,0},{5,1},{6,2},{7,3},{8,12},{9,13},{10,... | collective-permute-start | bytes 393224 | tf_op jit(solution)/shard_map/ppermute | solution.py:45
  14.1 0.6 %collective-permute-start.5 = (bf16[2,8,8192]{2,1,0:T(8,128)(2,1)S(1)}, bf16[2,8,8192]{2,1,0:T(8,128)(2,1)S(1)}, u32[]{:S(2)}, u32[]{:S(2)}) collective-permute-start(bf16[2,8,8192]{2,1,0:T(8,128)(2,1)S(1)} %pack.3.refs_2_.refs_1_), channel_id=1, source_target_pairs={{0,2},{1,3},{2,0},{3,1},{4,6},{5,7},{6,4},{7,5},{8,10},{9,11},{10,... | collective-permute-start | bytes 786440 | tf_op jit(solution)/shard_map/ppermute | solution.py:45
  14.6 3.2 %fetch_1.1 = (bf16[1024,1792]{1,0:T(8,128)(2,1)S(1)}, bf16[1024,1792]{1,0:T(8,128)(2,1)S(1)}) custom-call(bf16[8192,1792]{1,0:T(8,128)(2,1)} %refs_0_.5, bf16[8192,1792]{1,0:T(8,128)(2,1)} %refs_0_.5, bf16[2,8,8192]{2,1,0:T(8,128)(2,1)S(1)} %pack.3.refs_2_.refs_1_), custom_call_target="tpu_custom_call" | custom-call | bytes 7340032 | tf_op jit(solution)/shard_map/fetch_1/pallas_call | solution.py:68
  17.8 0.8 %collective-permute-done.4.refs_0_ = bf16[1,8,8192]{2,1,0:T(8,128)(2,1)S(1)} collective-permute-done((bf16[1,8,8192]{2,1,0:T(8,128)(2,1)S(1)}, bf16[1,8,8192]{2,1,0:T(8,128)(2,1)S(1)}, u32[]{:S(2)}, u32[]{:S(2)}) %collective-permute-start.4) | collective-permute-done | bytes 131104 | tf_op jit(solution)/shard_map/ppermute | solution.py:45
  18.6 0.8 %collective-permute-start.6 = (bf16[1,8,8192]{2,1,0:T(8,128)(2,1)S(1)}, bf16[1,8,8192]{2,1,0:T(8,128)(2,1)S(1)}, u32[]{:S(2)}, u32[]{:S(2)}) collective-permute-start(bf16[1,8,8192]{2,1,0:T(8,128)(2,1)S(1)} %tie.3.refs_2_), channel_id=1, source_target_pairs={{0,2},{1,3},{2,0},{3,1},{4,6},{5,7},{6,4},{7,5},{8,10},{9,11},{10,... | collective-permute-start | bytes 393224 | tf_op jit(solution)/shard_map/ppermute | solution.py:45
  19.5 0.1 collective-permute-start.7
  19.5 4.2 %fetch_2.1 = (bf16[1024,1792]{1,0:T(8,128)(2,1)S(1)}, bf16[1024,1792]{1,0:T(8,128)(2,1)S(1)}, bf16[1024,1792]{1,0:T(8,128)(2,1)S(1)}) custom-call(bf16[8192,1792]{1,0:T(8,128)(2,1)} %refs_0_.5, bf16[8192,1792]{1,0:T(8,128)(2,1)} %refs_9_.1, bf16[8192,1792]{1,0:T(8,128)(2,1)} %refs_9_.1, bf16[4,8,8192]{2,1,0:T(8,128)(2,1)S(1)} %pack.4.refs_3_.refs_0_), custom_call_target="tpu_custom_call" | custom-call | bytes 11010048 | tf_op jit(solution)/shard_map/fetch_2/pallas_call | solution.py:68
  23.8 0.7 %collective-permute-done.6.refs_2_ = bf16[1,8,8192]{2,1,0:T(8,128)(2,1)S(1)} collective-permute-done((bf16[1,8,8192]{2,1,0:T(8,128)(2,1)S(1)}, bf16[1,8,8192]{2,1,0:T(8,128)(2,1)S(1)}, u32[]{:S(2)}, u32[]{:S(2)}) %collective-permute-start.6) | collective-permute-done | bytes 131104 | tf_op jit(solution)/shard_map/ppermute | solution.py:45
  24.7 1.9 %collective-permute-done.8.refs_3_ = bf16[4,8,8192]{2,1,0:T(8,128)(2,1)S(1)} collective-permute-done((bf16[4,8,8192]{2,1,0:T(8,128)(2,1)S(1)}, bf16[4,8,8192]{2,1,0:T(8,128)(2,1)S(1)}, u32[]{:S(2)}, u32[]{:S(2)}) %collective-permute-start.8) | collective-permute-done | bytes 524320 | tf_op jit(solution)/shard_map/ppermute | solution.py:45
  26.6 1.7 %collect.1 = (bf16[128,8192]{1,0:T(8,128)(2,1)S(1)}, bf16[128,64]{1,0:T(8,128)(2,1)S(1)}) custom-call(s32[1,16]{1,0:T(1,128)S(1)} %bitcast.15, s32[1,128]{1,0:T(1,128)S(1)} %bitcast.13, bf16[64,8192]{1,0:T(8,128)(2,1)S(1)} %bitcast.8, bf16[64,8192]{1,0:T(8,128)(2,1)S(1)} %collective-permute-done.refs_4_.core_down, ...), custom_call_target="tpu_custom_call" | custom-call | flops 268435456 | bytes 1048576 | tf_op jit(solution)/shard_map/collect/pallas_call | solution.py:181
  28.3 1.8 %collective-permute-start.9 = (bf16[128,64]{1,0:T(8,128)(2,1)S(1)}, bf16[128,64]{1,0:T(8,128)(2,1)S(1)}, u32[]{:S(2)}, u32[]{:S(2)}) collective-permute-start(bf16[128,64]{1,0:T(8,128)(2,1)S(1)} %get-tuple-element.31.refs_0_), channel_id=1, source_target_pairs={{0,8},{1,9},{2,10},{3,11},{4,12},{5,13},{6,14},{7,15},{8,0},{9,1},... | collective-permute-start | bytes 49160 | tf_op jit(solution)/shard_map/ppermute | solution.py:45
  30.1 3.2 %gate_a.1 = (f32[128,1792]{1,0:T(8,128)S(1)}, bf16[1024,1792]{1,0:T(8,128)(2,1)S(1)}, bf16[1024,1792]{1,0:T(8,128)(2,1)S(1)}) custom-call(bf16[128,64]{1,0:T(8,128)(2,1)S(1)} %get-tuple-element.31.refs_0_, bf16[128,8192]{1,0:T(8,128)(2,1)S(1)} %get-tuple-element.30.refs_1_.tokens, bf16[1024,1792]{1,0:T(8,128)(2,1)S(1)} %get-tuple-element.27.refs_1_.refs_2_, ...), custom_call_target="tpu_custom_call" | custom-call | flops 1879048192 | bytes 16777216 | tf_op jit(solution)/shard_map/gate_a/pallas_call | solution.py:243
  33.3 0.2 collective-permute-done.9.refs_1_
  33.5 1.3 %collective-permute-start.10 = (bf16[128,64]{1,0:T(8,128)(2,1)S(1)}, bf16[128,64]{1,0:T(8,128)(2,1)S(1)}, u32[]{:S(2)}, u32[]{:S(2)}) collective-permute-start(bf16[128,64]{1,0:T(8,128)(2,1)S(1)} %add.2.refs_0_), channel_id=1, source_target_pairs={{0,4},{1,5},{2,6},{3,7},{4,0},{5,1},{6,2},{7,3},{8,12},{9,13},{10,... | collective-permute-start | bytes 49160 | tf_op jit(solution)/shard_map/ppermute | solution.py:45
  34.8 4.2 %gate_b.1 = (f32[128,1792]{1,0:T(8,128)S(1)}, bf16[1024,1792]{1,0:T(8,128)(2,1)S(1)}, bf16[1024,1792]{1,0:T(8,128)(2,1)S(1)}, bf16[1024,1792]{1,0:T(8,128)(2,1)S(1)}) custom-call(bf16[128,64]{1,0:T(8,128)(2,1)S(1)} %add.2.refs_0_, bf16[128,8192]{1,0:T(8,128)(2,1)S(1)} %get-tuple-element.30.refs_1_.tokens, bf16[1024,1792]{1,0:T(8,128)(2,1)S(1)} %get-tuple-element.39.refs_2_, ...), custom_call_target="tpu_custom_call" | custom-call | flops 1879048192 | bytes 16777216 | tf_op jit(solution)/shard_map/gate_b/pallas_call | solution.py:243
  39.1 0.6 %collective-permute-start.11 = (bf16[128,64]{1,0:T(8,128)(2,1)S(1)}, bf16[128,64]{1,0:T(8,128)(2,1)S(1)}, u32[]{:S(2)}, u32[]{:S(2)}) collective-permute-start(bf16[128,64]{1,0:T(8,128)(2,1)S(1)} %add.3.refs_0_.refs_4_), channel_id=1, source_target_pairs={{0,2},{1,3},{2,0},{3,1},{4,6},{5,7},{6,4},{7,5},{8,10},{9,11},{10,... | collective-permute-start | bytes 49160 | tf_op jit(solution)/shard_map/ppermute | solution.py:45
  39.6 3.2 %up_a.1 = (f32[128,1792]{1,0:T(8,128)S(1)}, bf16[1024,1792]{1,0:T(8,128)(2,1)S(1)}, bf16[1024,1792]{1,0:T(8,128)(2,1)S(1)}) custom-call(bf16[128,64]{1,0:T(8,128)(2,1)S(1)} %add.3.refs_0_.refs_4_, bf16[128,8192]{1,0:T(8,128)(2,1)S(1)} %get-tuple-element.30.refs_1_.tokens, bf16[1024,1792]{1,0:T(8,128)(2,1)S(1)} %get-tuple-element.29.refs_3_.refs_2_, ...), custom_call_target="tpu_custom_call" | custom-call | flops 1879048192 | bytes 16777216 | tf_op jit(solution)/shard_map/up_a/pallas_call | solution.py:243
  42.8 0.2 collective-permute-done.11.refs_5_
  43.1 3.3 %finish.1 = bf16[128,1792]{1,0:T(8,128)(2,1)} custom-call(s32[1,128]{1,0:T(1,128)S(1)} %bitcast.14, bf16[128,8192]{1,0:T(8,128)(2,1)S(1)} %get-tuple-element.30.refs_1_.tokens, bf16[1024,1792]{1,0:T(8,128)(2,1)S(1)} %get-tuple-element.38.adapter_up, f32[128,1792]{1,0:T(8,128)S(1)} %get-tuple-element.43.gate_pre, f32[128,1792]{1,0:T(8,128)S(1)} %get-tuple-element.44.up_pre, ...), custom_call_target="tpu_custom_call" | custom-call | flops 2348810240 | bytes 4194304 | tf_op jit(solution)/shard_map/finish/pallas_call | solution.py:291
  (23 shorter events, 0.2 us)
Async XLA Ops:
  0.0 14.0 %collective-permute-start = (bf16[64,8192]{1,0:T(8,128)(2,1)}, bf16[64,8192]{1,0:T(8,128)(2,1)S(1)}, u32[]{:S(2)}, u32[]{:S(2)}) collective-permute-start(bf16[64,8192]{1,0:T(8,128)(2,1)} %bitcast.7), channel_id=1, source_target_pairs={{0,1},{1,0},{2,3},{3,2},{4,5},{5,4},{6,7},{7,6},{8,9},{9,8},{10,11... | collective-permute-start | bytes 3145736 | tf_op jit(solution)/shard_map/ppermute | solution.py:45
  0.5 13.0 %collective-permute-start.2 = (bf16[1,8,8192]{2,1,0:T(8,128)(2,1)}, bf16[1,8,8192]{2,1,0:T(8,128)(2,1)S(1)}, u32[]{:S(2)}, u32[]{:S(2)}) collective-permute-start(bf16[1,8,8192]{2,1,0:T(8,128)(2,1)} %bitcast.9), channel_id=1, source_target_pairs={{0,8},{1,9},{2,10},{3,11},{4,12},{5,13},{6,14},{7,15},{8,0},{9,1},... | collective-permute-start | bytes 393224 | tf_op jit(solution)/shard_map/ppermute | solution.py:45
  4.0 10.0 %collective-permute-start.3 = (bf16[1,8,8192]{2,1,0:T(8,128)(2,1)}, bf16[1,8,8192]{2,1,0:T(8,128)(2,1)S(1)}, u32[]{:S(2)}, u32[]{:S(2)}) collective-permute-start(bf16[1,8,8192]{2,1,0:T(8,128)(2,1)} %bitcast.10), channel_id=1, source_target_pairs={{0,2},{1,3},{2,0},{3,1},{4,6},{5,7},{6,4},{7,5},{8,10},{9,11},{10,... | collective-permute-start | bytes 393224 | tf_op jit(solution)/shard_map/ppermute | solution.py:45
  5.6 8.5 %collective-permute-start.1 = (bf16[1,8,8192]{2,1,0:T(8,128)(2,1)}, bf16[1,8,8192]{2,1,0:T(8,128)(2,1)S(1)}, u32[]{:S(2)}, u32[]{:S(2)}) collective-permute-start(bf16[1,8,8192]{2,1,0:T(8,128)(2,1)} %bitcast.11), channel_id=1, source_target_pairs={{0,4},{1,5},{2,6},{3,7},{4,0},{5,1},{6,2},{7,3},{8,12},{9,13},{10,... | collective-permute-start | bytes 393224 | tf_op jit(solution)/shard_map/ppermute | solution.py:45
  13.5 5.1 %collective-permute-start.4 = (bf16[1,8,8192]{2,1,0:T(8,128)(2,1)S(1)}, bf16[1,8,8192]{2,1,0:T(8,128)(2,1)S(1)}, u32[]{:S(2)}, u32[]{:S(2)}) collective-permute-start(bf16[1,8,8192]{2,1,0:T(8,128)(2,1)S(1)} %tie.2.refs_1_), channel_id=1, source_target_pairs={{0,4},{1,5},{2,6},{3,7},{4,0},{5,1},{6,2},{7,3},{8,12},{9,13},{10,... | collective-permute-start | bytes 393224 | tf_op jit(solution)/shard_map/ppermute | solution.py:45
  14.1 10.5 %collective-permute-start.5 = (bf16[2,8,8192]{2,1,0:T(8,128)(2,1)S(1)}, bf16[2,8,8192]{2,1,0:T(8,128)(2,1)S(1)}, u32[]{:S(2)}, u32[]{:S(2)}) collective-permute-start(bf16[2,8,8192]{2,1,0:T(8,128)(2,1)S(1)} %pack.3.refs_2_.refs_1_), channel_id=1, source_target_pairs={{0,2},{1,3},{2,0},{3,1},{4,6},{5,7},{6,4},{7,5},{8,10},{9,11},{10,... | collective-permute-start | bytes 786440 | tf_op jit(solution)/shard_map/ppermute | solution.py:45
  17.8 1.6 %copy-start.1 = (bf16[8,8192]{1,0:T(8,128)(2,1)S(1)}, bf16[8,8192]{1,0:T(8,128)(2,1)}, u32[]{:S(2)}) copy-start(bf16[8,8192]{1,0:T(8,128)(2,1)} %param.8) | copy-start | bytes 393220
  18.6 5.9 %collective-permute-start.6 = (bf16[1,8,8192]{2,1,0:T(8,128)(2,1)S(1)}, bf16[1,8,8192]{2,1,0:T(8,128)(2,1)S(1)}, u32[]{:S(2)}, u32[]{:S(2)}) collective-permute-start(bf16[1,8,8192]{2,1,0:T(8,128)(2,1)S(1)} %tie.3.refs_2_), channel_id=1, source_target_pairs={{0,2},{1,3},{2,0},{3,1},{4,6},{5,7},{6,4},{7,5},{8,10},{9,11},{10,... | collective-permute-start | bytes 393224 | tf_op jit(solution)/shard_map/ppermute | solution.py:45
  19.5 5.2 %collective-permute-start.7 = (bf16[4,8,8192]{2,1,0:T(8,128)(2,1)S(1)}, bf16[4,8,8192]{2,1,0:T(8,128)(2,1)S(1)}, u32[]{:S(2)}, u32[]{:S(2)}) collective-permute-start(bf16[4,8,8192]{2,1,0:T(8,128)(2,1)S(1)} %pack.4.refs_3_.refs_0_), channel_id=1, source_target_pairs={{0,1},{1,0},{2,3},{3,2},{4,5},{5,4},{6,7},{7,6},{8,9},{9,8},{10,11... | collective-permute-start | bytes 1572872 | tf_op jit(solution)/shard_map/ppermute | solution.py:45
  23.8 2.8 %copy-start = (bf16[1,8192,64]{1,2,0:T(8,128)(2,1)S(1)}, bf16[1,8192,64]{1,2,0:T(8,128)(2,1)}, u32[]{:S(2)}) copy-start(bf16[1,8192,64]{1,2,0:T(8,128)(2,1)} %param.11) | copy-start | bytes 3145732
  23.8 2.8 %copy-start.2 = (s32[128]{0:T(128)S(1)}, s32[128]{0:T(128)}, u32[]{:S(2)}) copy-start(s32[128]{0:T(128)} %param.13) | copy-start | bytes 1540
  23.8 2.7 %copy-start.3 = (s32[16]{0:T(128)S(1)}, s32[16]{0:T(128)}, u32[]{:S(2)}) copy-start(s32[16]{0:T(128)} %param.14) | copy-start | bytes 196
  24.6 2.0 %collective-permute-start.8 = (bf16[4,8,8192]{2,1,0:T(8,128)(2,1)S(1)}, bf16[4,8,8192]{2,1,0:T(8,128)(2,1)S(1)}, u32[]{:S(2)}, u32[]{:S(2)}) collective-permute-start(bf16[4,8,8192]{2,1,0:T(8,128)(2,1)S(1)} %pack.5.refs_1_), channel_id=1, source_target_pairs={{0,1},{1,0},{2,3},{3,2},{4,5},{5,4},{6,7},{7,6},{8,9},{9,8},{10,11... | collective-permute-start | bytes 1572872 | tf_op jit(solution)/shard_map/ppermute | solution.py:45
  28.3 5.2 %collective-permute-start.9 = (bf16[128,64]{1,0:T(8,128)(2,1)S(1)}, bf16[128,64]{1,0:T(8,128)(2,1)S(1)}, u32[]{:S(2)}, u32[]{:S(2)}) collective-permute-start(bf16[128,64]{1,0:T(8,128)(2,1)S(1)} %get-tuple-element.31.refs_0_), channel_id=1, source_target_pairs={{0,8},{1,9},{2,10},{3,11},{4,12},{5,13},{6,14},{7,15},{8,0},{9,1},... | collective-permute-start | bytes 49160 | tf_op jit(solution)/shard_map/ppermute | solution.py:45
  33.5 5.5 %collective-permute-start.10 = (bf16[128,64]{1,0:T(8,128)(2,1)S(1)}, bf16[128,64]{1,0:T(8,128)(2,1)S(1)}, u32[]{:S(2)}, u32[]{:S(2)}) collective-permute-start(bf16[128,64]{1,0:T(8,128)(2,1)S(1)} %add.2.refs_0_), channel_id=1, source_target_pairs={{0,4},{1,5},{2,6},{3,7},{4,0},{5,1},{6,2},{7,3},{8,12},{9,13},{10,... | collective-permute-start | bytes 49160 | tf_op jit(solution)/shard_map/ppermute | solution.py:45
  39.1 4.0 %collective-permute-start.11 = (bf16[128,64]{1,0:T(8,128)(2,1)S(1)}, bf16[128,64]{1,0:T(8,128)(2,1)S(1)}, u32[]{:S(2)}, u32[]{:S(2)}) collective-permute-start(bf16[128,64]{1,0:T(8,128)(2,1)S(1)} %add.3.refs_0_.refs_4_), channel_id=1, source_target_pairs={{0,2},{1,3},{2,0},{3,1},{4,6},{5,7},{6,4},{7,5},{8,10},{9,11},{10,... | collective-permute-start | bytes 49160 | tf_op jit(solution)/shard_map/ppermute | solution.py:45

commit v9 on v8

--- a/solution.py
+++ b/solution.py
@@ -52,31 +52,44 @@
     ]
 
 
-def fetch_kernel(firsts, skipped, *refs):
+def fetch_kernel(firsts, joined, skipped, *refs):
     n = len(firsts)
-    sources, (*targets, sems) = refs[:n], refs[n + skipped :]
+    sources, parts, refs = refs[:n], refs[n : n + joined], refs[n + joined + skipped :]
+    targets, sems = refs[:n], refs[-1]
     copies = copies_of(sources, firsts, targets, sems)
     for copy in copies:
         copy.start()
+    row = 0
+    for part in parts:
+        rows = part.shape[0]
+        refs[n][row : row + rows, :] = part[...]
+        row += rows
     for copy in copies:
         copy.wait()
 
 
-def fetch(fetched, rows, name, after=()):
+def fetch(fetched, rows, name, after=(), join=()):
     n = len(fetched)
     width = fetched[0][0].shape[1]
+    out_shape = [pltpu.VMEM((rows, width), fetched[0][0].dtype)] * n
+    if join:
+        out_shape.append(
+            pltpu.VMEM((sum(v.shape[0] for v in join), join[0].shape[1]), join[0].dtype)
+        )
     arrived = pl.pallas_call(
-        functools.partial(fetch_kernel, [first for source, first in fetched], len(after)),
-        out_shape=[pltpu.VMEM((rows, width), fetched[0][0].dtype)] * n,
-        in_specs=[STORED] * n + [FAR] * len(after),
-        out_specs=[NEAR] * n,
+        functools.partial(
+            fetch_kernel, [first for source, first in fetched], len(join), len(after)
+        ),
+        out_shape=out_shape,
+        in_specs=[STORED] * n + [NEAR] * len(join) + [FAR] * len(after),
+        out_specs=[NEAR] * len(out_shape),
         scratch_shapes=[pltpu.SemaphoreType.DMA((n,))],
         cost_estimate=pl.CostEstimate(
             flops=0, bytes_accessed=n * rows * width * 2, transcendentals=0
         ),
-        compiler_params=pltpu.CompilerParams(vmem_limit_bytes=1 << 20),
+        compiler_params=pltpu.CompilerParams(vmem_limit_bytes=3 << 20 if join else 1 << 20),
         name=name,
-    )(*[far(source) for source, first in fetched], *after)
+    )(*[far(source) for source, first in fetched], *[near(v) for v in join], *after)
     return list(arrived)
 
 
@@ -145,7 +158,7 @@
         tile(pl.ds(width // WIDE * WIDE, width % WIDE))
 
 
-def collect_kernel(depth, width, sizes, placement, index, down, core_down, *refs):
+def collect_kernel(depth, width, sizes, placement, index, downs, *refs):
     mine, theirs = refs[: len(sizes)], refs[len(sizes) : 2 * len(sizes)]
     packed, low = refs[2 * len(sizes) :]
     own = lax.axis_index("tensor")
@@ -162,16 +175,18 @@
                 jnp.concatenate([before, after], 0)
             )
             place += 1
+    full = lax.dot_general(
+        packed[...], downs[...], (((1,), (1,)), ((), ())), preferred_element_type=jnp.float32
+    )
+    rank = low.shape[1]
     ids = lax.broadcasted_iota(jnp.int32, placement.shape, 1)
-    total = None
-    for slot, weight in ((own, down), (own ^ 1, core_down)):
-        full = lax.dot_general(
-            packed[...], weight[...], (((1,), (1,)), ((), ())), preferred_element_type=jnp.float32
-        )
-        owner = jnp.sum(jnp.where(placement[...] == slot, ids, 0), axis=1, keepdims=True)
-        chosen = across(jnp.where(index[...] == owner, 1, 0))[:, : full.shape[1]]
-        total = jnp.where(chosen == 1, full, 0.0 if total is None else total)
-    low[...] = total.astype(low.dtype)
+    owners = [
+        jnp.sum(jnp.where(placement[...] == slot, ids, 0), axis=1, keepdims=True)
+        for slot in (own, own ^ 1)
+    ]
+    adapter = across(index[...])[:, :rank]
+    kept = jnp.where(adapter == owners[0], full[:, :rank], 0.0)
+    low[...] = jnp.where(adapter == owners[1], full[:, rank:], kept).astype(low.dtype)
 
 
 def collect(placement, index, downs, mine, theirs, depth, width):
@@ -182,16 +197,16 @@
         functools.partial(collect_kernel, depth, width, sizes),
         out_shape=[
             pltpu.VMEM((requests, model), jnp.bfloat16),
-            jax.ShapeDtypeStruct((requests, downs[0].shape[0]), jnp.bfloat16),
+            jax.ShapeDtypeStruct((requests, downs.shape[0] // 2), jnp.bfloat16),
         ],
-        in_specs=[NEAR] * (4 + 2 * len(sizes)),
+        in_specs=[NEAR] * (3 + 2 * len(sizes)),
         out_specs=[NEAR] * 2,
         cost_estimate=pl.CostEstimate(
             flops=4 * requests * model * 64, bytes_accessed=1 << 20, transcendentals=0
         ),
         compiler_params=pltpu.CompilerParams(vmem_limit_bytes=2 << 20),
         name="collect",
-    )(placement, index, *downs, *[near(v) for v in mine], *[near(v) for v in theirs])
+    )(placement, index, near(downs), *[near(v) for v in mine], *[near(v) for v in theirs])
 
 
 def add_kernel(*refs):
@@ -213,7 +228,7 @@
     )(*values)
 
 
-def multiply_kernel(start, n, begun, firsts, *refs):
+def multiply_kernel(start, n, begun, firsts, gating, *refs):
     tokens, refs = refs[1], refs[2:]
     pieces, refs = refs[:n], refs[n:]
     before, refs = refs[:begun], refs[begun:]
@@ -226,14 +241,14 @@
         total = piecewise(tokens, pieces, start, here)
         if begun:
             total = total + before[0][:, here]
-        out[:, here] = total
+        out[:, here] = total / (1.0 + jnp.exp(-total)) if gating else total
 
     for_columns(out.shape[1], tile)
     for copy in copies:
         copy.wait()
 
 
-def multiply(after, tokens, pieces, start, begun, fetched, rows, name):
+def multiply(after, tokens, pieces, start, begun, fetched, rows, name, gating=False):
     requests = tokens.shape[0]
     hidden = pieces[0].shape[1]
     n = len(fetched)
@@ -242,7 +257,12 @@
     operands += [far(source) for source, first in fetched]
     return pl.pallas_call(
         functools.partial(
-            multiply_kernel, start, len(pieces), len(begun), [first for source, first in fetched]
+            multiply_kernel,
+            start,
+            len(pieces),
+            len(begun),
+            [first for source, first in fetched],
+            gating,
         ),
         out_shape=[pltpu.VMEM((requests, hidden), jnp.float32)]
         + [pltpu.VMEM((rows, hidden), tokens.dtype)] * n,
@@ -259,9 +279,9 @@
     )(*operands)
 
 
-def finish_kernel(start, n, m, index, tokens, adapter_up, gate_pre, up_pre, *refs):
+def finish_kernel(start, n, m, index, tokens, adapter_up, gate, up_pre, *refs):
     pieces, refs = refs[:n], refs[n:]
-    lows, (out, expanded) = refs[:m], refs[m:]
+    lows, (stored, expanded, out, sems) = refs[:m], refs[m:]
     rank = lows[0].shape[1]
     mixed = lows[0][...]
     for low in lows[1:]:
@@ -278,22 +298,32 @@
         ).astype(jnp.bfloat16)
 
     width = out.shape[1]
+    copies = []
     for first in range(0, width, WIDE):
         here = pl.ds(first, min(WIDE, width - first))
         up = up_pre[:, here] + piecewise(tokens, pieces, start, here)
         up = up + jnp.dot(expanded[...], adapter_up[:, here], preferred_element_type=jnp.float32)
-        gate = gate_pre[:, here]
-        out[:, here] = (gate / (1.0 + jnp.exp(-gate)) * up).astype(out.dtype)
-
-
-def finish(index, tokens, adapter_up, gate_pre, up_pre, pieces, start, lows):
-    requests, hidden = gate_pre.shape
+        out[:, here] = (gate[:, here] * up).astype(out.dtype)
+        copies.append(
+            pltpu.make_async_copy(out.at[:, here], stored.at[:, here], sems.at[len(copies)])
+        )
+        copies[-1].start()
+    for copy in copies:
+        copy.wait()
+
+
+def finish(index, tokens, adapter_up, gate, up_pre, pieces, start, lows):
+    requests, hidden = gate.shape
     return pl.pallas_call(
         functools.partial(finish_kernel, start, len(pieces), len(lows)),
         out_shape=jax.ShapeDtypeStruct((requests, hidden), jnp.bfloat16),
         in_specs=[NEAR] * (5 + len(pieces) + len(lows)),
-        out_specs=NEAR,
-        scratch_shapes=[pltpu.VMEM((requests, adapter_up.shape[0]), jnp.bfloat16)],
+        out_specs=STORED,
+        scratch_shapes=[
+            pltpu.VMEM((requests, adapter_up.shape[0]), jnp.bfloat16),
+            pltpu.VMEM((requests, hidden), jnp.bfloat16),
+            pltpu.SemaphoreType.DMA((-(-hidden // WIDE),)),
+        ],
         cost_estimate=pl.CostEstimate(
             flops=2 * requests * (adapter_up.shape[0] + sum(p.shape[0] for p in pieces)) * hidden,
             bytes_accessed=4 << 20,
@@ -305,7 +335,7 @@
         index,
         near(tokens),
         near(adapter_up),
-        near(gate_pre),
+        near(gate),
         near(up_pre),
         *[near(p) for p in pieces],
         *lows,
@@ -332,20 +362,31 @@
     block_3 = swap(block_2, line_1)
     blocks_12 = pack([block_1, block_2], [gates[0], column_0, core_down])
     columns_12 = swap(blocks_12, column)
-    gates += fetch([(gate_weight, first) for first in firsts[5:7]], unit, "fetch_1", [blocks_12])
+    *more_gates, downs = fetch(
+        [(gate_weight, first) for first in firsts[5:7]],
+        unit,
+        "fetch_1",
+        [blocks_12],
+        [down, core_down],
+    )
+    gates += more_gates
     block_3 = tie(block_3, gates[5:6])
     column_3 = swap(block_3, column)
     line = pack([own, blocks_12, block_3], [])
     core_line = swap(line, core)
-    more = [(gate_weight, firsts[7]), (up_weight, firsts[0]), (up_weight, firsts[1])]
-    last_gate, up_0, up_1 = fetch(more, unit, "fetch_2", [line])
+    last_gate, *ups = fetch(
+        [(gate_weight, firsts[7])] + [(up_weight, first) for first in firsts[:3]],
+        unit,
+        "fetch_2",
+        [line],
+    )
     gates.append(last_gate)
-    columns = pack([column_0, columns_12, column_3], [up_0])
+    columns = pack([column_0, columns_12, column_3], ups[:1])
     core_columns = swap(columns, core)
     packed, low = collect(
         placement[None, :],
         index,
-        [down, core_down],
+        downs,
         [line, columns],
         [core_line, core_columns],
         depth,
@@ -353,35 +394,36 @@
     )
 
     low_1 = add(low, swap(low, line_2))
-    gate_pre, *ups = multiply(
+    gate, *more_ups = multiply(
         low,
         packed,
         gates[:4],
         0,
         [],
-        [(up_weight, first) for first in firsts[2:4]],
+        [(up_weight, first) for first in firsts[3:5]],
         unit,
         "gate_a",
     )
-    ups = [up_0, up_1] + ups
+    ups += more_ups
     low_2 = add(low_1, swap(low_1, line_1))
-    gate_pre, *more_ups = multiply(
+    gate, *more_ups = multiply(
         low_1,
         packed,
         gates[4:],
         firsts[4],
-        [gate_pre],
-        [(up_weight, first) for first in firsts[4:7]],
+        [gate],
+        [(up_weight, first) for first in firsts[5:7]],
         unit,
         "gate_b",
-    )
+        gating=True,
+    )
+    ups += more_ups
     lows = [low_2, swap(low_2, column)]
     up_pre, near_up, last_up = multiply(
-        low_2, packed, ups, 0, [], [(up, 0), (up_weight, firsts[7])], unit, "up_a"
-    )
-    return finish(
-        index, packed, near_up, gate_pre, up_pre, more_ups + [last_up], firsts[4], lows
-    )
+        low_2, packed, ups[:4], 0, [], [(up, 0), (up_weight, firsts[7])], unit, "up_a"
+    )
+    ups.append(last_up)
+    return finish(index, packed, near_up, gate, up_pre, ups[4:], firsts[4], lows)
 
 
 def streamed(

time: 46.5 us -> 45.8 us (0.985)
  waiting for transfers between devices: 3.86 us -> 2.32 us
  starting transfers between devices: 12.9 us -> 14.1 us
  Pallas kernels: 29.5 us -> 29 us
    ppermute x12, waiting for transfers between devices: 3.86 us -> 2.32 us  [swap(): return lax.ppermute(value, 'tensor', pairs)]
    ppermute x12, starting transfers between devices: 12.9 us -> 14.1 us  [swap(): return lax.ppermute(value, 'tensor', pairs)]
    pallas_call x3, Pallas kernels: 13.7 us -> 14.8 us  [fetch(): pl.pallas_call(functools.partial(fetch_kernel, [first for source, first i...]
    pallas_call x3, Pallas kernels: 10.6 us -> 9.52 us  [multiply(): pl.pallas_call(functools.partial(multiply_kernel, start, len(pieces), len...]
  transfers between devices with their start and end apart: 12 -> 12, of which waited for: 5 -> 2; matrix products, arithmetic and copies ran while one was open for 0% -> 0% of each run, Pallas kernels for 53% -> 53%
where the time goes in v9:
time: 45.8 us; the launch traced here: 45.7 us
  Pallas kernels  29 us (63%)
  starting transfers between devices  14.1 us (31%)
  waiting for transfers between devices  2.32 us (5%)
    pallas_call x3, Pallas kernels, fetch(): pl.pallas_call(functools.partial(fetch_kernel, [first for source, first i...  14.8 us
    ppermute x12, starting transfers between devices, swap(): return lax.ppermute(value, 'tensor', pairs)  14.1 us
    pallas_call x3, Pallas kernels, multiply(): pl.pallas_call(functools.partial(multiply_kernel, start, len(pieces), len...  9.52 us
    pallas_call x1, Pallas kernels, finish(): pl.pallas_call(functools.partial(finish_kernel, start, len(pieces), len(l...  3.27 us
    ppermute x12, waiting for transfers between devices, swap(): return lax.ppermute(value, 'tensor', pairs)  2.32 us
    pallas_call x1, Pallas kernels, collect(): pl.pallas_call(functools.partial(collect_kernel, depth, width, sizes), ou...  1.27 us
  transfers between devices with their start and end apart: 12, of which 2 were waited for; matrix products, arithmetic and copies ran while one was open for 0% of the time, Pallas kernels for 53%

profile of v9, /device:TPU:0, one launch (start us, length us, event | category | flops | bytes accessed | tf_op | source)
XLA Modules:
  0.0 45.7 jit_solution(18011365178495345457)
XLA Ops:
  0.0 0.5 collective-permute-start
  0.5 3.6 %collective-permute-start.2 = (bf16[1,8,8192]{2,1,0:T(8,128)(2,1)}, bf16[1,8,8192]{2,1,0:T(8,128)(2,1)S(1)}, u32[]{:S(2)}, u32[]{:S(2)}) collective-permute-start(bf16[1,8,8192]{2,1,0:T(8,128)(2,1)} %bitcast.9), channel_id=1, source_target_pairs={{0,8},{1,9},{2,10},{3,11},{4,12},{5,13},{6,14},{7,15},{8,0},{9,1},... | collective-permute-start | bytes 393224 | tf_op jit(solution)/shard_map/ppermute | solution.py:45
  4.0 1.5 %collective-permute-start.3 = (bf16[1,8,8192]{2,1,0:T(8,128)(2,1)}, bf16[1,8,8192]{2,1,0:T(8,128)(2,1)S(1)}, u32[]{:S(2)}, u32[]{:S(2)}) collective-permute-start(bf16[1,8,8192]{2,1,0:T(8,128)(2,1)} %bitcast.10), channel_id=1, source_target_pairs={{0,2},{1,3},{2,0},{3,1},{4,6},{5,7},{6,4},{7,5},{8,10},{9,11},{10,... | collective-permute-start | bytes 393224 | tf_op jit(solution)/shard_map/ppermute | solution.py:45
  5.6 1.6 %collective-permute-start.1 = (bf16[1,8,8192]{2,1,0:T(8,128)(2,1)}, bf16[1,8,8192]{2,1,0:T(8,128)(2,1)S(1)}, u32[]{:S(2)}, u32[]{:S(2)}) collective-permute-start(bf16[1,8,8192]{2,1,0:T(8,128)(2,1)} %bitcast.11), channel_id=1, source_target_pairs={{0,4},{1,5},{2,6},{3,7},{4,0},{5,1},{6,2},{7,3},{8,12},{9,13},{10,... | collective-permute-start | bytes 393224 | tf_op jit(solution)/shard_map/ppermute | solution.py:45
  7.1 6.3 %fetch_0.1 = (bf16[1024,1792]{1,0:T(8,128)(2,1)S(1)}, bf16[1024,1792]{1,0:T(8,128)(2,1)S(1)}, bf16[1024,1792]{1,0:T(8,128)(2,1)S(1)}, bf16[1024,1792]{1,0:T(8,128)(2,1)S(1)}, bf16[1024,1792]{1,0:T(8,128)(2,1)S(1)}) custom-call(bf16[8192,1792]{1,0:T(8,128)(2,1)} %refs_0_.5, bf16[8192,1792]{1,0:T(8,128)(2,1)} %refs_0_.5, bf16[8192,1792]{1,0:T(8,128)(2,1)} %refs_0_.5, ...), custom_call_target="tpu_custom_call" | custom-call | bytes 18350080 | tf_op jit(solution)/shard_map/fetch_0/pallas_call | solution.py:79
  13.5 0.5 %collective-permute-start.4 = (bf16[1,8,8192]{2,1,0:T(8,128)(2,1)S(1)}, bf16[1,8,8192]{2,1,0:T(8,128)(2,1)S(1)}, u32[]{:S(2)}, u32[]{:S(2)}) collective-permute-start(bf16[1,8,8192]{2,1,0:T(8,128)(2,1)S(1)} %tie.2.refs_1_), channel_id=1, source_target_pairs={{0,4},{1,5},{2,6},{3,7},{4,0},{5,1},{6,2},{7,3},{8,12},{9,13},{10,... | collective-permute-start | bytes 393224 | tf_op jit(solution)/shard_map/ppermute | solution.py:45
  14.1 0.6 %collective-permute-start.5 = (bf16[2,8,8192]{2,1,0:T(8,128)(2,1)S(1)}, bf16[2,8,8192]{2,1,0:T(8,128)(2,1)S(1)}, u32[]{:S(2)}, u32[]{:S(2)}) collective-permute-start(bf16[2,8,8192]{2,1,0:T(8,128)(2,1)S(1)} %pack.3.refs_4_.refs_1_), channel_id=1, source_target_pairs={{0,2},{1,3},{2,0},{3,1},{4,6},{5,7},{6,4},{7,5},{8,10},{9,11},{10,... | collective-permute-start | bytes 786440 | tf_op jit(solution)/shard_map/ppermute | solution.py:45
  14.6 0.1 copy-done
  14.7 3.2 %fetch_1.1 = (bf16[1024,1792]{1,0:T(8,128)(2,1)S(1)}, bf16[1024,1792]{1,0:T(8,128)(2,1)S(1)}, bf16[128,8192]{1,0:T(8,128)(2,1)S(1)}) custom-call(bf16[8192,1792]{1,0:T(8,128)(2,1)} %refs_0_.5, bf16[8192,1792]{1,0:T(8,128)(2,1)} %refs_0_.5, bf16[64,8192]{1,0:T(8,128)(2,1)S(1)} %bitcast.8, bf16[64,8192]{1,0:T(8,128)(2,1)S(1)} %collective-permute-done.refs_4_.refs_3_, ...), custom_call_target="tpu_custom_call" | custom-call | bytes 7340032 | tf_op jit(solution)/shard_map/fetch_1/pallas_call | solution.py:79
  17.9 0.7 %collective-permute-done.4.refs_0_ = bf16[1,8,8192]{2,1,0:T(8,128)(2,1)S(1)} collective-permute-done((bf16[1,8,8192]{2,1,0:T(8,128)(2,1)S(1)}, bf16[1,8,8192]{2,1,0:T(8,128)(2,1)S(1)}, u32[]{:S(2)}, u32[]{:S(2)}) %collective-permute-start.4) | collective-permute-done | bytes 131104 | tf_op jit(solution)/shard_map/ppermute | solution.py:45
  18.6 0.8 %collective-permute-start.6 = (bf16[1,8,8192]{2,1,0:T(8,128)(2,1)S(1)}, bf16[1,8,8192]{2,1,0:T(8,128)(2,1)S(1)}, u32[]{:S(2)}, u32[]{:S(2)}) collective-permute-start(bf16[1,8,8192]{2,1,0:T(8,128)(2,1)S(1)} %tie.3.refs_2_), channel_id=1, source_target_pairs={{0,2},{1,3},{2,0},{3,1},{4,6},{5,7},{6,4},{7,5},{8,10},{9,11},{10,... | collective-permute-start | bytes 393224 | tf_op jit(solution)/shard_map/ppermute | solution.py:45
  19.5 0.1 collective-permute-start.7
  19.6 5.3 %fetch_2.1 = (bf16[1024,1792]{1,0:T(8,128)(2,1)S(1)}, bf16[1024,1792]{1,0:T(8,128)(2,1)S(1)}, bf16[1024,1792]{1,0:T(8,128)(2,1)S(1)}, bf16[1024,1792]{1,0:T(8,128)(2,1)S(1)}) custom-call(bf16[8192,1792]{1,0:T(8,128)(2,1)} %refs_0_.5, bf16[8192,1792]{1,0:T(8,128)(2,1)} %refs_8_.1, bf16[8192,1792]{1,0:T(8,128)(2,1)} %refs_8_.1, bf16[8192,1792]{1,0:T(8,128)(2,1)} %refs_8_.1, ...), custom_call_target="tpu_custom_call" | custom-call | bytes 14680064 | tf_op jit(solution)/shard_map/fetch_2/pallas_call | solution.py:79
  24.9 0.6 %collective-permute-start.8 = (bf16[4,8,8192]{2,1,0:T(8,128)(2,1)S(1)}, bf16[4,8,8192]{2,1,0:T(8,128)(2,1)S(1)}, u32[]{:S(2)}, u32[]{:S(2)}) collective-permute-start(bf16[4,8,8192]{2,1,0:T(8,128)(2,1)S(1)} %pack.5.refs_1_), channel_id=1, source_target_pairs={{0,1},{1,0},{2,3},{3,2},{4,5},{5,4},{6,7},{7,6},{8,9},{9,8},{10,11... | collective-permute-start | bytes 1572872 | tf_op jit(solution)/shard_map/ppermute | solution.py:45
  25.5 1.5 %collective-permute-done.8.refs_3_ = bf16[4,8,8192]{2,1,0:T(8,128)(2,1)S(1)} collective-permute-done((bf16[4,8,8192]{2,1,0:T(8,128)(2,1)S(1)}, bf16[4,8,8192]{2,1,0:T(8,128)(2,1)S(1)}, u32[]{:S(2)}, u32[]{:S(2)}) %collective-permute-start.8) | collective-permute-done | bytes 524320 | tf_op jit(solution)/shard_map/ppermute | solution.py:45
  27.0 1.3 %collect.1 = (bf16[128,8192]{1,0:T(8,128)(2,1)S(1)}, bf16[128,64]{1,0:T(8,128)(2,1)S(1)}) custom-call(s32[1,16]{1,0:T(1,128)S(1)} %bitcast.15, s32[1,128]{1,0:T(1,128)S(1)} %bitcast.13, bf16[128,8192]{1,0:T(8,128)(2,1)S(1)} %get-tuple-element.29.downs, bf16[4,8,8192]{2,1,0:T(8,128)(2,1)S(1)} %pack.4.refs_4_.refs_0_, bf16[4,8,8192]{2,1,0:T(8,128)(2,1)S(1)} %pack.5.refs_1_, ...), custom_call_target="tpu_custom_call" | custom-call | flops 268435456 | bytes 1048576 | tf_op jit(solution)/shard_map/collect/pallas_call | solution.py:196
  28.3 1.7 %collective-permute-start.9 = (bf16[128,64]{1,0:T(8,128)(2,1)S(1)}, bf16[128,64]{1,0:T(8,128)(2,1)S(1)}, u32[]{:S(2)}, u32[]{:S(2)}) collective-permute-start(bf16[128,64]{1,0:T(8,128)(2,1)S(1)} %get-tuple-element.33.refs_0_), channel_id=1, source_target_pairs={{0,8},{1,9},{2,10},{3,11},{4,12},{5,13},{6,14},{7,15},{8,0},{9,1},... | collective-permute-start | bytes 49160 | tf_op jit(solution)/shard_map/ppermute | solution.py:45
  30.0 3.2 %gate_a.1 = (f32[128,1792]{1,0:T(8,128)S(1)}, bf16[1024,1792]{1,0:T(8,128)(2,1)S(1)}, bf16[1024,1792]{1,0:T(8,128)(2,1)S(1)}) custom-call(bf16[128,64]{1,0:T(8,128)(2,1)S(1)} %get-tuple-element.33.refs_0_, bf16[128,8192]{1,0:T(8,128)(2,1)S(1)} %get-tuple-element.32.refs_1_.tokens, bf16[1024,1792]{1,0:T(8,128)(2,1)S(1)} %get-tuple-element.28.refs_1_.refs_2_, ...), custom_call_target="tpu_custom_call" | custom-call | flops 1879048192 | bytes 16777216 | tf_op jit(solution)/shard_map/gate_a/pallas_call | solution.py:258
  33.2 0.0 collective-permute-done.9.refs_1_
  33.2 1.6 %collective-permute-start.10 = (bf16[128,64]{1,0:T(8,128)(2,1)S(1)}, bf16[128,64]{1,0:T(8,128)(2,1)S(1)}, u32[]{:S(2)}, u32[]{:S(2)}) collective-permute-start(bf16[128,64]{1,0:T(8,128)(2,1)S(1)} %add.2.refs_0_), channel_id=1, source_target_pairs={{0,4},{1,5},{2,6},{3,7},{4,0},{5,1},{6,2},{7,3},{8,12},{9,13},{10,... | collective-permute-start | bytes 49160 | tf_op jit(solution)/shard_map/ppermute | solution.py:45
  34.9 3.2 %gate_b.1 = (f32[128,1792]{1,0:T(8,128)S(1)}, bf16[1024,1792]{1,0:T(8,128)(2,1)S(1)}, bf16[1024,1792]{1,0:T(8,128)(2,1)S(1)}) custom-call(bf16[128,64]{1,0:T(8,128)(2,1)S(1)} %add.2.refs_0_, bf16[128,8192]{1,0:T(8,128)(2,1)S(1)} %get-tuple-element.32.refs_1_.tokens, bf16[1024,1792]{1,0:T(8,128)(2,1)S(1)} %get-tuple-element.41.refs_2_, ...), custom_call_target="tpu_custom_call" | custom-call | flops 1879048192 | bytes 16777216 | tf_op jit(solution)/shard_map/gate_b/pallas_call | solution.py:258
  38.1 1.1 %collective-permute-start.11 = (bf16[128,64]{1,0:T(8,128)(2,1)S(1)}, bf16[128,64]{1,0:T(8,128)(2,1)S(1)}, u32[]{:S(2)}, u32[]{:S(2)}) collective-permute-start(bf16[128,64]{1,0:T(8,128)(2,1)S(1)} %add.3.refs_0_.refs_4_), channel_id=1, source_target_pairs={{0,2},{1,3},{2,0},{3,1},{4,6},{5,7},{6,4},{7,5},{8,10},{9,11},{10,... | collective-permute-start | bytes 49160 | tf_op jit(solution)/shard_map/ppermute | solution.py:45
  39.2 3.2 %up_a.1 = (f32[128,1792]{1,0:T(8,128)S(1)}, bf16[1024,1792]{1,0:T(8,128)(2,1)S(1)}, bf16[1024,1792]{1,0:T(8,128)(2,1)S(1)}) custom-call(bf16[128,64]{1,0:T(8,128)(2,1)S(1)} %add.3.refs_0_.refs_4_, bf16[128,8192]{1,0:T(8,128)(2,1)S(1)} %get-tuple-element.32.refs_1_.tokens, bf16[1024,1792]{1,0:T(8,128)(2,1)S(1)} %get-tuple-element.31.refs_3_.refs_2_, ...), custom_call_target="tpu_custom_call" | custom-call | flops 1879048192 | bytes 16777216 | tf_op jit(solution)/shard_map/up_a/pallas_call | solution.py:258
  42.4 3.3 %finish.1 = bf16[128,1792]{1,0:T(8,128)(2,1)} custom-call(s32[1,128]{1,0:T(1,128)S(1)} %bitcast.14, bf16[128,8192]{1,0:T(8,128)(2,1)S(1)} %get-tuple-element.32.refs_1_.tokens, bf16[1024,1792]{1,0:T(8,128)(2,1)S(1)} %get-tuple-element.40.adapter_up, f32[128,1792]{1,0:T(8,128)S(1)} %get-tuple-element.45.gate, f32[128,1792]{1,0:T(8,128)S(1)} %get-tuple-element.46.up_pre, ...), custom_call_target="tpu_custom_call" | custom-call | flops 2348810240 | bytes 4194304 | tf_op jit(solution)/shard_map/finish/pallas_call | solution.py:317
  (23 shorter events, 0.2 us)
Async XLA Ops:
  0.0 14.0 %collective-permute-start = (bf16[64,8192]{1,0:T(8,128)(2,1)}, bf16[64,8192]{1,0:T(8,128)(2,1)S(1)}, u32[]{:S(2)}, u32[]{:S(2)}) collective-permute-start(bf16[64,8192]{1,0:T(8,128)(2,1)} %bitcast.7), channel_id=1, source_target_pairs={{0,1},{1,0},{2,3},{3,2},{4,5},{5,4},{6,7},{7,6},{8,9},{9,8},{10,11... | collective-permute-start | bytes 3145736 | tf_op jit(solution)/shard_map/ppermute | solution.py:45
  0.5 13.0 %collective-permute-start.2 = (bf16[1,8,8192]{2,1,0:T(8,128)(2,1)}, bf16[1,8,8192]{2,1,0:T(8,128)(2,1)S(1)}, u32[]{:S(2)}, u32[]{:S(2)}) collective-permute-start(bf16[1,8,8192]{2,1,0:T(8,128)(2,1)} %bitcast.9), channel_id=1, source_target_pairs={{0,8},{1,9},{2,10},{3,11},{4,12},{5,13},{6,14},{7,15},{8,0},{9,1},... | collective-permute-start | bytes 393224 | tf_op jit(solution)/shard_map/ppermute | solution.py:45
  4.0 10.0 %collective-permute-start.3 = (bf16[1,8,8192]{2,1,0:T(8,128)(2,1)}, bf16[1,8,8192]{2,1,0:T(8,128)(2,1)S(1)}, u32[]{:S(2)}, u32[]{:S(2)}) collective-permute-start(bf16[1,8,8192]{2,1,0:T(8,128)(2,1)} %bitcast.10), channel_id=1, source_target_pairs={{0,2},{1,3},{2,0},{3,1},{4,6},{5,7},{6,4},{7,5},{8,10},{9,11},{10,... | collective-permute-start | bytes 393224 | tf_op jit(solution)/shard_map/ppermute | solution.py:45
  5.6 8.5 %collective-permute-start.1 = (bf16[1,8,8192]{2,1,0:T(8,128)(2,1)}, bf16[1,8,8192]{2,1,0:T(8,128)(2,1)S(1)}, u32[]{:S(2)}, u32[]{:S(2)}) collective-permute-start(bf16[1,8,8192]{2,1,0:T(8,128)(2,1)} %bitcast.11), channel_id=1, source_target_pairs={{0,4},{1,5},{2,6},{3,7},{4,0},{5,1},{6,2},{7,3},{8,12},{9,13},{10,... | collective-permute-start | bytes 393224 | tf_op jit(solution)/shard_map/ppermute | solution.py:45
  13.5 1.2 %copy-start = (bf16[1,8192,64]{1,2,0:T(8,128)(2,1)S(1)}, bf16[1,8192,64]{1,2,0:T(8,128)(2,1)}, u32[]{:S(2)}) copy-start(bf16[1,8192,64]{1,2,0:T(8,128)(2,1)} %param.11) | copy-start | bytes 3145732
  13.5 5.1 %collective-permute-start.4 = (bf16[1,8,8192]{2,1,0:T(8,128)(2,1)S(1)}, bf16[1,8,8192]{2,1,0:T(8,128)(2,1)S(1)}, u32[]{:S(2)}, u32[]{:S(2)}) collective-permute-start(bf16[1,8,8192]{2,1,0:T(8,128)(2,1)S(1)} %tie.2.refs_1_), channel_id=1, source_target_pairs={{0,4},{1,5},{2,6},{3,7},{4,0},{5,1},{6,2},{7,3},{8,12},{9,13},{10,... | collective-permute-start | bytes 393224 | tf_op jit(solution)/shard_map/ppermute | solution.py:45
  14.1 10.8 %collective-permute-start.5 = (bf16[2,8,8192]{2,1,0:T(8,128)(2,1)S(1)}, bf16[2,8,8192]{2,1,0:T(8,128)(2,1)S(1)}, u32[]{:S(2)}, u32[]{:S(2)}) collective-permute-start(bf16[2,8,8192]{2,1,0:T(8,128)(2,1)S(1)} %pack.3.refs_4_.refs_1_), channel_id=1, source_target_pairs={{0,2},{1,3},{2,0},{3,1},{4,6},{5,7},{6,4},{7,5},{8,10},{9,11},{10,... | collective-permute-start | bytes 786440 | tf_op jit(solution)/shard_map/ppermute | solution.py:45
  17.9 1.5 %copy-start.1 = (bf16[8,8192]{1,0:T(8,128)(2,1)S(1)}, bf16[8,8192]{1,0:T(8,128)(2,1)}, u32[]{:S(2)}) copy-start(bf16[8,8192]{1,0:T(8,128)(2,1)} %param.8) | copy-start | bytes 393220
  18.6 6.2 %collective-permute-start.6 = (bf16[1,8,8192]{2,1,0:T(8,128)(2,1)S(1)}, bf16[1,8,8192]{2,1,0:T(8,128)(2,1)S(1)}, u32[]{:S(2)}, u32[]{:S(2)}) collective-permute-start(bf16[1,8,8192]{2,1,0:T(8,128)(2,1)S(1)} %tie.3.refs_2_), channel_id=1, source_target_pairs={{0,2},{1,3},{2,0},{3,1},{4,6},{5,7},{6,4},{7,5},{8,10},{9,11},{10,... | collective-permute-start | bytes 393224 | tf_op jit(solution)/shard_map/ppermute | solution.py:45
  19.5 6.0 %collective-permute-start.7 = (bf16[4,8,8192]{2,1,0:T(8,128)(2,1)S(1)}, bf16[4,8,8192]{2,1,0:T(8,128)(2,1)S(1)}, u32[]{:S(2)}, u32[]{:S(2)}) collective-permute-start(bf16[4,8,8192]{2,1,0:T(8,128)(2,1)S(1)} %pack.4.refs_4_.refs_0_), channel_id=1, source_target_pairs={{0,1},{1,0},{2,3},{3,2},{4,5},{5,4},{6,7},{7,6},{8,9},{9,8},{10,11... | collective-permute-start | bytes 1572872 | tf_op jit(solution)/shard_map/ppermute | solution.py:45
  24.9 2.2 %copy-start.2 = (s32[128]{0:T(128)S(1)}, s32[128]{0:T(128)}, u32[]{:S(2)}) copy-start(s32[128]{0:T(128)} %param.13) | copy-start | bytes 1540
  24.9 2.2 %copy-start.3 = (s32[16]{0:T(128)S(1)}, s32[16]{0:T(128)}, u32[]{:S(2)}) copy-start(s32[16]{0:T(128)} %param.14) | copy-start | bytes 196
  24.9 2.1 %collective-permute-start.8 = (bf16[4,8,8192]{2,1,0:T(8,128)(2,1)S(1)}, bf16[4,8,8192]{2,1,0:T(8,128)(2,1)S(1)}, u32[]{:S(2)}, u32[]{:S(2)}) collective-permute-start(bf16[4,8,8192]{2,1,0:T(8,128)(2,1)S(1)} %pack.5.refs_1_), channel_id=1, source_target_pairs={{0,1},{1,0},{2,3},{3,2},{4,5},{5,4},{6,7},{7,6},{8,9},{9,8},{10,11... | collective-permute-start | bytes 1572872 | tf_op jit(solution)/shard_map/ppermute | solution.py:45
  28.3 4.9 %collective-permute-start.9 = (bf16[128,64]{1,0:T(8,128)(2,1)S(1)}, bf16[128,64]{1,0:T(8,128)(2,1)S(1)}, u32[]{:S(2)}, u32[]{:S(2)}) collective-permute-start(bf16[128,64]{1,0:T(8,128)(2,1)S(1)} %get-tuple-element.33.refs_0_), channel_id=1, source_target_pairs={{0,8},{1,9},{2,10},{3,11},{4,12},{5,13},{6,14},{7,15},{8,0},{9,1},... | collective-permute-start | bytes 49160 | tf_op jit(solution)/shard_map/ppermute | solution.py:45
  33.2 4.8 %collective-permute-start.10 = (bf16[128,64]{1,0:T(8,128)(2,1)S(1)}, bf16[128,64]{1,0:T(8,128)(2,1)S(1)}, u32[]{:S(2)}, u32[]{:S(2)}) collective-permute-start(bf16[128,64]{1,0:T(8,128)(2,1)S(1)} %add.2.refs_0_), channel_id=1, source_target_pairs={{0,4},{1,5},{2,6},{3,7},{4,0},{5,1},{6,2},{7,3},{8,12},{9,13},{10,... | collective-permute-start | bytes 49160 | tf_op jit(solution)/shard_map/ppermute | solution.py:45
  38.1 4.3 %collective-permute-start.11 = (bf16[128,64]{1,0:T(8,128)(2,1)S(1)}, bf16[128,64]{1,0:T(8,128)(2,1)S(1)}, u32[]{:S(2)}, u32[]{:S(2)}) collective-permute-start(bf16[128,64]{1,0:T(8,128)(2,1)S(1)} %add.3.refs_0_.refs_4_), channel_id=1, source_target_pairs={{0,2},{1,3},{2,0},{3,1},{4,6},{5,7},{6,4},{7,5},{8,10},{9,11},{10,... | collective-permute-start | bytes 49160 | tf_op jit(solution)/shard_map/ppermute | solution.py:45

commit v10 on v9

--- a/solution.py
+++ b/solution.py
@@ -228,7 +228,7 @@
     )(*values)
 
 
-def multiply_kernel(start, n, begun, firsts, gating, *refs):
+def multiply_kernel(start, n, begun, firsts, gating, looped, *refs):
     tokens, refs = refs[1], refs[2:]
     pieces, refs = refs[:n], refs[n:]
     before, refs = refs[:begun], refs[begun:]
@@ -243,12 +243,16 @@
             total = total + before[0][:, here]
         out[:, here] = total / (1.0 + jnp.exp(-total)) if gating else total
 
-    for_columns(out.shape[1], tile)
+    if looped:
+        for_columns(out.shape[1], tile)
+    else:
+        for column in range(0, out.shape[1], WIDE):
+            tile(pl.ds(column, min(WIDE, out.shape[1] - column)))
     for copy in copies:
         copy.wait()
 
 
-def multiply(after, tokens, pieces, start, begun, fetched, rows, name, gating=False):
+def multiply(after, tokens, pieces, start, begun, fetched, rows, name, gating=False, looped=True):
     requests = tokens.shape[0]
     hidden = pieces[0].shape[1]
     n = len(fetched)
@@ -263,6 +267,7 @@
             len(begun),
             [first for source, first in fetched],
             gating,
+            looped,
         ),
         out_shape=[pltpu.VMEM((requests, hidden), jnp.float32)]
         + [pltpu.VMEM((rows, hidden), tokens.dtype)] * n,
@@ -419,11 +424,11 @@
     )
     ups += more_ups
     lows = [low_2, swap(low_2, column)]
-    up_pre, near_up, last_up = multiply(
-        low_2, packed, ups[:4], 0, [], [(up, 0), (up_weight, firsts[7])], unit, "up_a"
+    up_pre, last_up = multiply(
+        low_2, packed, ups[:5], 0, [], [(up_weight, firsts[7])], unit, "up_a", looped=False
     )
     ups.append(last_up)
-    return finish(index, packed, near_up, gate, up_pre, ups[4:], firsts[4], lows)
+    return finish(index, packed, up, gate, up_pre, ups[5:], firsts[5], lows)
 
 
 def streamed(

time: 45.8 us -> 46.7 us (1.020)
  Pallas kernels: 29 us -> 29.8 us
    pallas_call x3, Pallas kernels: 9.52 us -> 10.9 us  [multiply(): pl.pallas_call(functools.partial(multiply_kernel, start, len(pieces), len...]
    pallas_call x1, Pallas kernels: 3.27 us -> 2.76 us  [finish(): pl.pallas_call(functools.partial(finish_kernel, start, len(pieces), len(l...]
  transfers between devices with their start and end apart: 12 -> 12, of which waited for: 2 -> 2; matrix products, arithmetic and copies ran while one was open for 0% -> 0% of each run, Pallas kernels for 53% -> 55%
where the time goes in v10:
time: 46.7 us; the launch traced here: 46.5 us
  Pallas kernels  29.8 us (64%)
  starting transfers between devices  14.1 us (30%)
  waiting for transfers between devices  2.32 us (5%)
    pallas_call x3, Pallas kernels, fetch(): pl.pallas_call(functools.partial(fetch_kernel, [first for source, first i...  14.8 us
    ppermute x12, starting transfers between devices, swap(): return lax.ppermute(value, 'tensor', pairs)  14.1 us
    pallas_call x3, Pallas kernels, multiply(): pl.pallas_call(functools.partial(multiply_kernel, start, len(pieces), len...  10.9 us
    pallas_call x1, Pallas kernels, finish(): pl.pallas_call(functools.partial(finish_kernel, start, len(pieces), len(l...  2.76 us
    ppermute x12, waiting for transfers between devices, swap(): return lax.ppermute(value, 'tensor', pairs)  2.32 us
    pallas_call x1, Pallas kernels, collect(): pl.pallas_call(functools.partial(collect_kernel, depth, width, sizes), ou...  1.27 us
  transfers between devices with their start and end apart: 12, of which 2 were waited for; matrix products, arithmetic and copies ran while one was open for 0% of the time, Pallas kernels for 55%

profile of v10, /device:TPU:0, one launch (start us, length us, event | category | flops | bytes accessed | tf_op | source)
XLA Modules:
  0.0 46.5 jit_solution(10823279594271164843)
XLA Ops:
  0.0 0.5 collective-permute-start
  0.5 3.6 %collective-permute-start.2 = (bf16[1,8,8192]{2,1,0:T(8,128)(2,1)}, bf16[1,8,8192]{2,1,0:T(8,128)(2,1)S(1)}, u32[]{:S(2)}, u32[]{:S(2)}) collective-permute-start(bf16[1,8,8192]{2,1,0:T(8,128)(2,1)} %bitcast.10), channel_id=1, source_target_pairs={{0,8},{1,9},{2,10},{3,11},{4,12},{5,13},{6,14},{7,15},{8,0},{9,1},... | collective-permute-start | bytes 393224 | tf_op jit(solution)/shard_map/ppermute | solution.py:45
  4.0 1.5 %collective-permute-start.3 = (bf16[1,8,8192]{2,1,0:T(8,128)(2,1)}, bf16[1,8,8192]{2,1,0:T(8,128)(2,1)S(1)}, u32[]{:S(2)}, u32[]{:S(2)}) collective-permute-start(bf16[1,8,8192]{2,1,0:T(8,128)(2,1)} %bitcast.11), channel_id=1, source_target_pairs={{0,2},{1,3},{2,0},{3,1},{4,6},{5,7},{6,4},{7,5},{8,10},{9,11},{10,... | collective-permute-start | bytes 393224 | tf_op jit(solution)/shard_map/ppermute | solution.py:45
  5.6 1.6 %collective-permute-start.1 = (bf16[1,8,8192]{2,1,0:T(8,128)(2,1)}, bf16[1,8,8192]{2,1,0:T(8,128)(2,1)S(1)}, u32[]{:S(2)}, u32[]{:S(2)}) collective-permute-start(bf16[1,8,8192]{2,1,0:T(8,128)(2,1)} %bitcast.12), channel_id=1, source_target_pairs={{0,4},{1,5},{2,6},{3,7},{4,0},{5,1},{6,2},{7,3},{8,12},{9,13},{10,... | collective-permute-start | bytes 393224 | tf_op jit(solution)/shard_map/ppermute | solution.py:45
  7.1 6.3 %fetch_0.1 = (bf16[1024,1792]{1,0:T(8,128)(2,1)S(1)}, bf16[1024,1792]{1,0:T(8,128)(2,1)S(1)}, bf16[1024,1792]{1,0:T(8,128)(2,1)S(1)}, bf16[1024,1792]{1,0:T(8,128)(2,1)S(1)}, bf16[1024,1792]{1,0:T(8,128)(2,1)S(1)}) custom-call(bf16[8192,1792]{1,0:T(8,128)(2,1)} %refs_0_.5, bf16[8192,1792]{1,0:T(8,128)(2,1)} %refs_0_.5, bf16[8192,1792]{1,0:T(8,128)(2,1)} %refs_0_.5, ...), custom_call_target="tpu_custom_call" | custom-call | bytes 18350080 | tf_op jit(solution)/shard_map/fetch_0/pallas_call | solution.py:79
  13.5 0.5 %collective-permute-start.4 = (bf16[1,8,8192]{2,1,0:T(8,128)(2,1)S(1)}, bf16[1,8,8192]{2,1,0:T(8,128)(2,1)S(1)}, u32[]{:S(2)}, u32[]{:S(2)}) collective-permute-start(bf16[1,8,8192]{2,1,0:T(8,128)(2,1)S(1)} %tie.2.refs_1_), channel_id=1, source_target_pairs={{0,4},{1,5},{2,6},{3,7},{4,0},{5,1},{6,2},{7,3},{8,12},{9,13},{10,... | collective-permute-start | bytes 393224 | tf_op jit(solution)/shard_map/ppermute | solution.py:45
  14.1 0.6 %collective-permute-start.5 = (bf16[2,8,8192]{2,1,0:T(8,128)(2,1)S(1)}, bf16[2,8,8192]{2,1,0:T(8,128)(2,1)S(1)}, u32[]{:S(2)}, u32[]{:S(2)}) collective-permute-start(bf16[2,8,8192]{2,1,0:T(8,128)(2,1)S(1)} %pack.3.refs_4_.refs_1_), channel_id=1, source_target_pairs={{0,2},{1,3},{2,0},{3,1},{4,6},{5,7},{6,4},{7,5},{8,10},{9,11},{10,... | collective-permute-start | bytes 786440 | tf_op jit(solution)/shard_map/ppermute | solution.py:45
  14.6 0.1 copy-done.1
  14.7 3.2 %fetch_1.1 = (bf16[1024,1792]{1,0:T(8,128)(2,1)S(1)}, bf16[1024,1792]{1,0:T(8,128)(2,1)S(1)}, bf16[128,8192]{1,0:T(8,128)(2,1)S(1)}) custom-call(bf16[8192,1792]{1,0:T(8,128)(2,1)} %refs_0_.5, bf16[8192,1792]{1,0:T(8,128)(2,1)} %refs_0_.5, bf16[64,8192]{1,0:T(8,128)(2,1)S(1)} %bitcast.9, bf16[64,8192]{1,0:T(8,128)(2,1)S(1)} %collective-permute-done.refs_4_.refs_3_, ...), custom_call_target="tpu_custom_call" | custom-call | bytes 7340032 | tf_op jit(solution)/shard_map/fetch_1/pallas_call | solution.py:79
  17.9 0.7 %collective-permute-done.4.refs_0_ = bf16[1,8,8192]{2,1,0:T(8,128)(2,1)S(1)} collective-permute-done((bf16[1,8,8192]{2,1,0:T(8,128)(2,1)S(1)}, bf16[1,8,8192]{2,1,0:T(8,128)(2,1)S(1)}, u32[]{:S(2)}, u32[]{:S(2)}) %collective-permute-start.4) | collective-permute-done | bytes 131104 | tf_op jit(solution)/shard_map/ppermute | solution.py:45
  18.6 0.8 %collective-permute-start.6 = (bf16[1,8,8192]{2,1,0:T(8,128)(2,1)S(1)}, bf16[1,8,8192]{2,1,0:T(8,128)(2,1)S(1)}, u32[]{:S(2)}, u32[]{:S(2)}) collective-permute-start(bf16[1,8,8192]{2,1,0:T(8,128)(2,1)S(1)} %tie.3.refs_2_), channel_id=1, source_target_pairs={{0,2},{1,3},{2,0},{3,1},{4,6},{5,7},{6,4},{7,5},{8,10},{9,11},{10,... | collective-permute-start | bytes 393224 | tf_op jit(solution)/shard_map/ppermute | solution.py:45
  19.5 0.1 collective-permute-start.7
  19.6 5.3 %fetch_2.1 = (bf16[1024,1792]{1,0:T(8,128)(2,1)S(1)}, bf16[1024,1792]{1,0:T(8,128)(2,1)S(1)}, bf16[1024,1792]{1,0:T(8,128)(2,1)S(1)}, bf16[1024,1792]{1,0:T(8,128)(2,1)S(1)}) custom-call(bf16[8192,1792]{1,0:T(8,128)(2,1)} %refs_0_.5, bf16[8192,1792]{1,0:T(8,128)(2,1)} %refs_7_.5, bf16[8192,1792]{1,0:T(8,128)(2,1)} %refs_7_.5, bf16[8192,1792]{1,0:T(8,128)(2,1)} %refs_7_.5, ...), custom_call_target="tpu_custom_call" | custom-call | bytes 14680064 | tf_op jit(solution)/shard_map/fetch_2/pallas_call | solution.py:79
  24.9 0.6 %collective-permute-start.8 = (bf16[4,8,8192]{2,1,0:T(8,128)(2,1)S(1)}, bf16[4,8,8192]{2,1,0:T(8,128)(2,1)S(1)}, u32[]{:S(2)}, u32[]{:S(2)}) collective-permute-start(bf16[4,8,8192]{2,1,0:T(8,128)(2,1)S(1)} %pack.5.refs_1_), channel_id=1, source_target_pairs={{0,1},{1,0},{2,3},{3,2},{4,5},{5,4},{6,7},{7,6},{8,9},{9,8},{10,11... | collective-permute-start | bytes 1572872 | tf_op jit(solution)/shard_map/ppermute | solution.py:45
  25.5 1.5 %collective-permute-done.8.refs_3_ = bf16[4,8,8192]{2,1,0:T(8,128)(2,1)S(1)} collective-permute-done((bf16[4,8,8192]{2,1,0:T(8,128)(2,1)S(1)}, bf16[4,8,8192]{2,1,0:T(8,128)(2,1)S(1)}, u32[]{:S(2)}, u32[]{:S(2)}) %collective-permute-start.8) | collective-permute-done | bytes 524320 | tf_op jit(solution)/shard_map/ppermute | solution.py:45
  27.0 1.3 %collect.1 = (bf16[128,8192]{1,0:T(8,128)(2,1)S(1)}, bf16[128,64]{1,0:T(8,128)(2,1)S(1)}) custom-call(s32[1,16]{1,0:T(1,128)S(1)} %bitcast.16, s32[1,128]{1,0:T(1,128)S(1)} %bitcast.14, bf16[128,8192]{1,0:T(8,128)(2,1)S(1)} %get-tuple-element.28.downs, bf16[4,8,8192]{2,1,0:T(8,128)(2,1)S(1)} %pack.4.refs_4_.refs_0_, bf16[4,8,8192]{2,1,0:T(8,128)(2,1)S(1)} %pack.5.refs_1_, ...), custom_call_target="tpu_custom_call" | custom-call | flops 268435456 | bytes 1048576 | tf_op jit(solution)/shard_map/collect/pallas_call | solution.py:196
  28.3 1.7 %collective-permute-start.9 = (bf16[128,64]{1,0:T(8,128)(2,1)S(1)}, bf16[128,64]{1,0:T(8,128)(2,1)S(1)}, u32[]{:S(2)}, u32[]{:S(2)}) collective-permute-start(bf16[128,64]{1,0:T(8,128)(2,1)S(1)} %get-tuple-element.32.refs_0_), channel_id=1, source_target_pairs={{0,8},{1,9},{2,10},{3,11},{4,12},{5,13},{6,14},{7,15},{8,0},{9,1},... | collective-permute-start | bytes 49160 | tf_op jit(solution)/shard_map/ppermute | solution.py:45
  30.0 3.2 %gate_a.1 = (f32[128,1792]{1,0:T(8,128)S(1)}, bf16[1024,1792]{1,0:T(8,128)(2,1)S(1)}, bf16[1024,1792]{1,0:T(8,128)(2,1)S(1)}) custom-call(bf16[128,64]{1,0:T(8,128)(2,1)S(1)} %get-tuple-element.32.refs_0_, bf16[128,8192]{1,0:T(8,128)(2,1)S(1)} %get-tuple-element.31.refs_1_.tokens, bf16[1024,1792]{1,0:T(8,128)(2,1)S(1)} %get-tuple-element.27.refs_1_.refs_2_, ...), custom_call_target="tpu_custom_call" | custom-call | flops 1879048192 | bytes 16777216 | tf_op jit(solution)/shard_map/gate_a/pallas_call | solution.py:262
  33.2 0.0 collective-permute-done.9.refs_1_
  33.2 1.6 %collective-permute-start.10 = (bf16[128,64]{1,0:T(8,128)(2,1)S(1)}, bf16[128,64]{1,0:T(8,128)(2,1)S(1)}, u32[]{:S(2)}, u32[]{:S(2)}) collective-permute-start(bf16[128,64]{1,0:T(8,128)(2,1)S(1)} %add.2.refs_0_), channel_id=1, source_target_pairs={{0,4},{1,5},{2,6},{3,7},{4,0},{5,1},{6,2},{7,3},{8,12},{9,13},{10,... | collective-permute-start | bytes 49160 | tf_op jit(solution)/shard_map/ppermute | solution.py:45
  34.9 3.2 %gate_b.1 = (f32[128,1792]{1,0:T(8,128)S(1)}, bf16[1024,1792]{1,0:T(8,128)(2,1)S(1)}, bf16[1024,1792]{1,0:T(8,128)(2,1)S(1)}) custom-call(bf16[128,64]{1,0:T(8,128)(2,1)S(1)} %add.2.refs_0_, bf16[128,8192]{1,0:T(8,128)(2,1)S(1)} %get-tuple-element.31.refs_1_.tokens, bf16[1024,1792]{1,0:T(8,128)(2,1)S(1)} %get-tuple-element.33.refs_2_, ...), custom_call_target="tpu_custom_call" | custom-call | flops 1879048192 | bytes 16777216 | tf_op jit(solution)/shard_map/gate_b/pallas_call | solution.py:262
  38.1 1.1 %collective-permute-start.11 = (bf16[128,64]{1,0:T(8,128)(2,1)S(1)}, bf16[128,64]{1,0:T(8,128)(2,1)S(1)}, u32[]{:S(2)}, u32[]{:S(2)}) collective-permute-start(bf16[128,64]{1,0:T(8,128)(2,1)S(1)} %add.3.refs_0_.refs_3_), channel_id=1, source_target_pairs={{0,2},{1,3},{2,0},{3,1},{4,6},{5,7},{6,4},{7,5},{8,10},{9,11},{10,... | collective-permute-start | bytes 49160 | tf_op jit(solution)/shard_map/ppermute | solution.py:45
  39.2 4.5 %up_a.1 = (f32[128,1792]{1,0:T(8,128)S(1)}, bf16[1024,1792]{1,0:T(8,128)(2,1)S(1)}) custom-call(bf16[128,64]{1,0:T(8,128)(2,1)S(1)} %add.3.refs_0_.refs_3_, bf16[128,8192]{1,0:T(8,128)(2,1)S(1)} %get-tuple-element.31.refs_1_.tokens, bf16[1024,1792]{1,0:T(8,128)(2,1)S(1)} %get-tuple-element.30.refs_3_.refs_2_, ...), custom_call_target="tpu_custom_call" | custom-call | flops 2348810240 | bytes 16777216 | tf_op jit(solution)/shard_map/up_a/pallas_call | solution.py:262
  43.7 2.8 %finish.1 = bf16[128,1792]{1,0:T(8,128)(2,1)} custom-call(s32[1,128]{1,0:T(1,128)S(1)} %bitcast.15, bf16[128,8192]{1,0:T(8,128)(2,1)S(1)} %get-tuple-element.31.refs_1_.tokens, bf16[1024,1792]{1,0:T(8,128)(2,1)S(1)} %bitcast.7, f32[128,1792]{1,0:T(8,128)S(1)} %get-tuple-element.40.gate, f32[128,1792]{1,0:T(8,128)S(1)} %get-tuple-element.45.up_pre, ...), custom_call_target="tpu_custom_call" | custom-call | flops 1879048192 | bytes 4194304 | tf_op jit(solution)/shard_map/finish/pallas_call | solution.py:322
  (25 shorter events, 0.2 us)
Async XLA Ops:
  0.0 14.0 %collective-permute-start = (bf16[64,8192]{1,0:T(8,128)(2,1)}, bf16[64,8192]{1,0:T(8,128)(2,1)S(1)}, u32[]{:S(2)}, u32[]{:S(2)}) collective-permute-start(bf16[64,8192]{1,0:T(8,128)(2,1)} %bitcast.8), channel_id=1, source_target_pairs={{0,1},{1,0},{2,3},{3,2},{4,5},{5,4},{6,7},{7,6},{8,9},{9,8},{10,11... | collective-permute-start | bytes 3145736 | tf_op jit(solution)/shard_map/ppermute | solution.py:45
  0.5 13.0 %collective-permute-start.2 = (bf16[1,8,8192]{2,1,0:T(8,128)(2,1)}, bf16[1,8,8192]{2,1,0:T(8,128)(2,1)S(1)}, u32[]{:S(2)}, u32[]{:S(2)}) collective-permute-start(bf16[1,8,8192]{2,1,0:T(8,128)(2,1)} %bitcast.10), channel_id=1, source_target_pairs={{0,8},{1,9},{2,10},{3,11},{4,12},{5,13},{6,14},{7,15},{8,0},{9,1},... | collective-permute-start | bytes 393224 | tf_op jit(solution)/shard_map/ppermute | solution.py:45
  4.0 10.0 %collective-permute-start.3 = (bf16[1,8,8192]{2,1,0:T(8,128)(2,1)}, bf16[1,8,8192]{2,1,0:T(8,128)(2,1)S(1)}, u32[]{:S(2)}, u32[]{:S(2)}) collective-permute-start(bf16[1,8,8192]{2,1,0:T(8,128)(2,1)} %bitcast.11), channel_id=1, source_target_pairs={{0,2},{1,3},{2,0},{3,1},{4,6},{5,7},{6,4},{7,5},{8,10},{9,11},{10,... | collective-permute-start | bytes 393224 | tf_op jit(solution)/shard_map/ppermute | solution.py:45
  5.6 8.5 %collective-permute-start.1 = (bf16[1,8,8192]{2,1,0:T(8,128)(2,1)}, bf16[1,8,8192]{2,1,0:T(8,128)(2,1)S(1)}, u32[]{:S(2)}, u32[]{:S(2)}) collective-permute-start(bf16[1,8,8192]{2,1,0:T(8,128)(2,1)} %bitcast.12), channel_id=1, source_target_pairs={{0,4},{1,5},{2,6},{3,7},{4,0},{5,1},{6,2},{7,3},{8,12},{9,13},{10,... | collective-permute-start | bytes 393224 | tf_op jit(solution)/shard_map/ppermute | solution.py:45
  13.5 1.2 %copy-start.1 = (bf16[1,8192,64]{1,2,0:T(8,128)(2,1)S(1)}, bf16[1,8192,64]{1,2,0:T(8,128)(2,1)}, u32[]{:S(2)}) copy-start(bf16[1,8192,64]{1,2,0:T(8,128)(2,1)} %param.11) | copy-start | bytes 3145732
  13.5 5.1 %collective-permute-start.4 = (bf16[1,8,8192]{2,1,0:T(8,128)(2,1)S(1)}, bf16[1,8,8192]{2,1,0:T(8,128)(2,1)S(1)}, u32[]{:S(2)}, u32[]{:S(2)}) collective-permute-start(bf16[1,8,8192]{2,1,0:T(8,128)(2,1)S(1)} %tie.2.refs_1_), channel_id=1, source_target_pairs={{0,4},{1,5},{2,6},{3,7},{4,0},{5,1},{6,2},{7,3},{8,12},{9,13},{10,... | collective-permute-start | bytes 393224 | tf_op jit(solution)/shard_map/ppermute | solution.py:45
  14.1 10.8 %collective-permute-start.5 = (bf16[2,8,8192]{2,1,0:T(8,128)(2,1)S(1)}, bf16[2,8,8192]{2,1,0:T(8,128)(2,1)S(1)}, u32[]{:S(2)}, u32[]{:S(2)}) collective-permute-start(bf16[2,8,8192]{2,1,0:T(8,128)(2,1)S(1)} %pack.3.refs_4_.refs_1_), channel_id=1, source_target_pairs={{0,2},{1,3},{2,0},{3,1},{4,6},{5,7},{6,4},{7,5},{8,10},{9,11},{10,... | collective-permute-start | bytes 786440 | tf_op jit(solution)/shard_map/ppermute | solution.py:45
  17.9 1.5 %copy-start.2 = (bf16[8,8192]{1,0:T(8,128)(2,1)S(1)}, bf16[8,8192]{1,0:T(8,128)(2,1)}, u32[]{:S(2)}) copy-start(bf16[8,8192]{1,0:T(8,128)(2,1)} %param.8) | copy-start | bytes 393220
  18.6 6.2 %collective-permute-start.6 = (bf16[1,8,8192]{2,1,0:T(8,128)(2,1)S(1)}, bf16[1,8,8192]{2,1,0:T(8,128)(2,1)S(1)}, u32[]{:S(2)}, u32[]{:S(2)}) collective-permute-start(bf16[1,8,8192]{2,1,0:T(8,128)(2,1)S(1)} %tie.3.refs_2_), channel_id=1, source_target_pairs={{0,2},{1,3},{2,0},{3,1},{4,6},{5,7},{6,4},{7,5},{8,10},{9,11},{10,... | collective-permute-start | bytes 393224 | tf_op jit(solution)/shard_map/ppermute | solution.py:45
  19.5 6.0 %collective-permute-start.7 = (bf16[4,8,8192]{2,1,0:T(8,128)(2,1)S(1)}, bf16[4,8,8192]{2,1,0:T(8,128)(2,1)S(1)}, u32[]{:S(2)}, u32[]{:S(2)}) collective-permute-start(bf16[4,8,8192]{2,1,0:T(8,128)(2,1)S(1)} %pack.4.refs_4_.refs_0_), channel_id=1, source_target_pairs={{0,1},{1,0},{2,3},{3,2},{4,5},{5,4},{6,7},{7,6},{8,9},{9,8},{10,11... | collective-permute-start | bytes 1572872 | tf_op jit(solution)/shard_map/ppermute | solution.py:45
  24.9 2.2 %copy-start.3 = (s32[128]{0:T(128)S(1)}, s32[128]{0:T(128)}, u32[]{:S(2)}) copy-start(s32[128]{0:T(128)} %param.13) | copy-start | bytes 1540
  24.9 2.2 %copy-start.4 = (s32[16]{0:T(128)S(1)}, s32[16]{0:T(128)}, u32[]{:S(2)}) copy-start(s32[16]{0:T(128)} %param.14) | copy-start | bytes 196
  24.9 2.1 %collective-permute-start.8 = (bf16[4,8,8192]{2,1,0:T(8,128)(2,1)S(1)}, bf16[4,8,8192]{2,1,0:T(8,128)(2,1)S(1)}, u32[]{:S(2)}, u32[]{:S(2)}) collective-permute-start(bf16[4,8,8192]{2,1,0:T(8,128)(2,1)S(1)} %pack.5.refs_1_), channel_id=1, source_target_pairs={{0,1},{1,0},{2,3},{3,2},{4,5},{5,4},{6,7},{7,6},{8,9},{9,8},{10,11... | collective-permute-start | bytes 1572872 | tf_op jit(solution)/shard_map/ppermute | solution.py:45
  28.3 4.9 %collective-permute-start.9 = (bf16[128,64]{1,0:T(8,128)(2,1)S(1)}, bf16[128,64]{1,0:T(8,128)(2,1)S(1)}, u32[]{:S(2)}, u32[]{:S(2)}) collective-permute-start(bf16[128,64]{1,0:T(8,128)(2,1)S(1)} %get-tuple-element.32.refs_0_), channel_id=1, source_target_pairs={{0,8},{1,9},{2,10},{3,11},{4,12},{5,13},{6,14},{7,15},{8,0},{9,1},... | collective-permute-start | bytes 49160 | tf_op jit(solution)/shard_map/ppermute | solution.py:45
  33.2 4.8 %collective-permute-start.10 = (bf16[128,64]{1,0:T(8,128)(2,1)S(1)}, bf16[128,64]{1,0:T(8,128)(2,1)S(1)}, u32[]{:S(2)}, u32[]{:S(2)}) collective-permute-start(bf16[128,64]{1,0:T(8,128)(2,1)S(1)} %add.2.refs_0_), channel_id=1, source_target_pairs={{0,4},{1,5},{2,6},{3,7},{4,0},{5,1},{6,2},{7,3},{8,12},{9,13},{10,... | collective-permute-start | bytes 49160 | tf_op jit(solution)/shard_map/ppermute | solution.py:45
  38.1 5.6 %collective-permute-start.11 = (bf16[128,64]{1,0:T(8,128)(2,1)S(1)}, bf16[128,64]{1,0:T(8,128)(2,1)S(1)}, u32[]{:S(2)}, u32[]{:S(2)}) collective-permute-start(bf16[128,64]{1,0:T(8,128)(2,1)S(1)} %add.3.refs_0_.refs_3_), channel_id=1, source_target_pairs={{0,2},{1,3},{2,0},{3,1},{4,6},{5,7},{6,4},{7,5},{8,10},{9,11},{10,... | collective-permute-start | bytes 49160 | tf_op jit(solution)/shard_map/ppermute | solution.py:45
  39.2 4.5 %copy-start = (bf16[16,64,1792]{2,1,0:T(8,128)(2,1)S(1)}, bf16[16,64,1792]{2,1,0:T(8,128)(2,1)}, u32[]{:S(2)}) copy-start(bf16[16,64,1792]{2,1,0:T(8,128)(2,1)} %param.12) | copy-start | bytes 11010052
